TPU v7x, 32 devices: a whole 2x2x4 slice. The times are simulated.
32 devices in a mesh: replica: 8 (over y, x, core), fsdp: 4 (over z).
Axes of the slice: x: 2, y: 2, z: 4, core: 2. Of those that a mesh axis runs over, the one named last changes fastest.
Arguments:
- activations: bfloat16 [8192, 4096], P(('replica', 'fsdp')), may hold values from -6 to 6
- output_grads: bfloat16 [8192, 512], P(('replica', 'fsdp')), may hold values from -0.1875 to 0.1875
- momentum: bfloat16 [8, 4096, 512], P('replica', 'fsdp'), may hold values from -6 to 6
- chosen_blocks: int32 [8, 64, 8], P('replica', 'fsdp'), may hold values from 0 to 255, as said below
Outputs:
- momentum_next: bfloat16 [8, 4096, 512], P('replica', 'fsdp')
- update: float32 [4096, 512], P('fsdp')
Inputs may be any that keep to these rules, and one draw needn't show every extreme that they name: `chosen_blocks`: the 8 numbers of each span row of each replica are different block numbers.
All inputs are finite; a program needn't handle non-finite values.
Results may differ from a plain program's by a relative error of at most 0.013.
Values may be sent and summed in bfloat16 or wider, within the bound.
No kernel may reach another device: no remote copies, remote signals or barrier semaphores. Data moves between devices by JAX's collectives and lax.ppermute only.
A program may use at most 64 MiB of HBM per device.

v0:
```python
import jax
import jax.numpy as jnp
from jax import lax
from jax.sharding import PartitionSpec as P


def cosine_table(size):
    order = lax.broadcasted_iota(jnp.float32, (size, size), 0)
    place = lax.broadcasted_iota(jnp.float32, (size, size), 1)
    factor = jnp.where(
        order == 0.0, jnp.sqrt(jnp.float32(1.0 / size)), jnp.sqrt(jnp.float32(2.0 / size))
    )
    return factor * jnp.cos(jnp.float32(jnp.pi) * (2.0 * place + 1.0) * order / (2.0 * size))


def forward_blocks(field, table, size, block_len):
    rows = field.shape[0] // size
    cols = field.shape[1] // size
    shaped = field.reshape(rows, size, cols, size)
    coeffs = jnp.einsum("pu,cujv,qv->cjpq", table, shaped, table, precision=lax.Precision.HIGHEST)
    return coeffs.reshape(rows, cols * (size * size // block_len), block_len)


def inverse_blocks(coeffs, table, size, block_len):
    rows = coeffs.shape[0]
    cols = coeffs.shape[1] * block_len // (size * size)
    shaped = coeffs.reshape(rows, cols, size, size)
    field = jnp.einsum("pu,cjpq,qv->cujv", table, shaped, table, precision=lax.Precision.HIGHEST)
    return field.reshape(rows * size, cols * size)


def body(activations, output_grads, momentum, chosen_blocks):
    size = 64
    block_len = 128
    width_out = momentum.shape[2]
    nblocks = width_out // size * (size * size // block_len)
    table = cosine_table(size)
    grad = lax.psum_scatter(
        lax.dot_general(
            activations, output_grads, (((0,), (0,)), ((), ())), preferred_element_type=jnp.float32
        ).astype(jnp.bfloat16),
        "fsdp",
        scatter_dimension=0,
        tiled=True,
    ).astype(jnp.float32)
    moment = 0.9 * momentum[0].astype(jnp.float32) + grad
    coeffs = forward_blocks(moment, table, size, block_len)
    picks = chosen_blocks[0]
    numbers = lax.broadcasted_iota(jnp.int32, (1, 1, nblocks), 2)
    selector = (picks[:, :, None] == numbers).astype(jnp.float32)
    mask = jnp.sum(selector, axis=1)
    kept = coeffs * (1.0 - mask[:, :, None])
    moment_next = inverse_blocks(kept, table, size, block_len).astype(jnp.bfloat16)
    values = jnp.einsum("ckb,cbv->ckv", selector, coeffs, precision=lax.Precision.HIGHEST).astype(
        jnp.bfloat16
    )
    piece_values = lax.all_gather(values[None], "replica", axis=0, tiled=True)
    piece_numbers = lax.all_gather(picks[None], "replica", axis=0, tiled=True)
    onehot = (piece_numbers[:, :, :, None] == numbers[None]).astype(jnp.bfloat16)
    total = jnp.einsum("rckb,rckv->cbv", onehot, piece_values, preferred_element_type=jnp.float32)
    update = inverse_blocks(total, table, size, block_len)
    return (moment_next[None], update)


def solution(mesh):
    return jax.shard_map(
        body,
        mesh=mesh,
        in_specs=(
            P(("replica", "fsdp"), None),
            P(("replica", "fsdp"), None),
            P("replica", "fsdp", None),
            P("replica", "fsdp", None),
        ),
        out_specs=(P("replica", "fsdp", None), P("fsdp", None)),
        check_vma=False,
    )
```

profile of v0, /device:TPU:0, one launch (start us, length us, event | category | flops | bytes accessed | tf_op | source)
XLA Modules:
  0.0 179.1 jit_solution(11788288346937459868)
XLA Ops:
  7.2 1.5 copy-done
  8.8 4.2 %convolution_convert_fusion = bf16[4096,512]{1,0:T(8,128)(2,1)} fusion(bf16[256,4096]{1,0:T(8,128)(2,1)S(1)} %copy-done, bf16[256,512]{1,0:T(8,128)(2,1)} %param.5), kind=kOutput, calls=%fused_computation | convolution fusion | flops 1075838976 | bytes 6553600 | tf_op jit(solution)/shard_map/dot_general | solution.py:39
  13.0 0.7 copy-done.3
  13.7 10.5 %all_gather.6 = s32[8,16,8]{1,2,0:T(8,128)S(1)} all-gather(s32[1,16,8]{1,2,0:T(8,128)S(1)} %copy-done.3), channel_id=1, replica_groups=mesh['replica'=8,'fsdp'=4] {'replica'}, dimensions={0}, use_global_device_ids=true | all-gather | bytes 4608 | tf_op jit(solution)/shard_map/all_gather | solution.py:58
  24.2 0.7 copy.35
  25.2 0.1 copy.31
  25.4 67.2 %reduce-scatter.2.cloned.1.call-done = bf16[1024,512]{1,0:T(8,128)(2,1)} async-done(((bf16[4096,512]{1,0:T(8,128)(2,1)}), bf16[1024,512]{1,0:T(8,128)(2,1)}) %reduce-scatter.2.cloned.1.call-update) | async-done | bytes 1048592 | tf_op jit(solution)/shard_map/reduce_scatter | solution.py:38
  92.6 2.8 %bitcast_add_fusion = f32[1024,512]{1,0:T(8,128)} fusion(bf16[1024,512]{1,0:T(8,128)(2,1)} %reduce-scatter.2.cloned.1.call-done, bf16[1,1024,512]{2,1,0:T(8,128)(2,1)S(1)} %copy-done.1), kind=kLoop, calls=%fused_computation.6 | loop fusion | flops 2097152 | bytes 4194304 | tf_op jit(solution)/shard_map/add | solution.py:46
  95.4 4.4 %reshape.39 = f32[16,64,8,64]{3,2,1,0:T(8,128)} reshape(f32[1024,512]{1,0:T(8,128)} %bitcast_add_fusion) | data formatting | bytes 4194304 | tf_op jit(solution)/shard_map/reshape | solution.py:19
  99.8 6.9 %fusion = f32[16,8,64,64]{2,3,1,0:T(8,128)S(1)} fusion(f32[16,64,8,64]{3,2,1,0:T(8,128)} %reshape.39, f32[64]{0:T(128)S(1)} %get-tuple-element.3, f32[64]{0:T(128)S(1)} %multiply_add_fusion, f32[64]{0:T(128)S(1)} %get-tuple-element.2), kind=kOutput, calls=%fused_computation.1 | convolution fusion | flops 402665472 | bytes 4195072 | tf_op jit(solution)/shard_map/pu,cujv,qv->cjpq/dot_general | solution.py:20
  106.7 5.3 %fusion.13 = f32[16,8,64,64]{3,2,1,0:T(8,128)} fusion(f32[16,8,64,64]{2,3,1,0:T(8,128)S(1)} %fusion, f32[64]{0:T(128)S(1)} %get-tuple-element.3, f32[64]{0:T(128)S(1)} %multiply_add_fusion, f32[64]{0:T(128)S(1)} %get-tuple-element.2), kind=kOutput, calls=%fused_computation.22 | convolution fusion | flops 402665472 | bytes 4195072 | tf_op jit(solution)/shard_map/pu,cujv,qv->cjpq/dot_general | solution.py:20
  112.0 4.6 %reshape.40 = f32[16,256,128]{2,1,0:T(8,128)} reshape(f32[16,8,64,64]{3,2,1,0:T(8,128)} %fusion.13) | data formatting | bytes 4194304 | tf_op jit(solution)/shard_map/reshape | solution.py:21
  116.6 2.4 %convolution_convert_fusion.1 = bf16[16,8,128]{2,1,0:T(8,128)(2,1)S(1)} fusion(f32[16,256,128]{2,1,0:T(8,128)} %reshape.40, s32[16,8]{1,0:T(8,128)S(1)} %copy.29), kind=kOutput, calls=%fused_computation.10 | convolution fusion | flops 50380800 | bytes 2130432 | tf_op jit(solution)/shard_map/ckb,cbv->ckv/dot_general | solution.py:54
  119.0 6.5 %fusion.2 = f32[16,8,64,64]{2,3,1,0:T(8,128)S(1)} fusion(f32[16,8,64,64]{3,2,1,0:T(8,128)} %fusion.13, f32[16,8,64]{2,1,0:T(8,128)S(1)} %copy.31, f32[64]{0:T(128)S(1)} %get-tuple-element.3, f32[64]{0:T(128)S(1)} %multiply_add_fusion, f32[64]{0:T(128)S(1)} %get-tuple-element.2), kind=kOutput, calls=%fused_computation.3 | convolution fusion | flops 403189760 | bytes 4227840 | tf_op jit(solution)/shard_map/pu,cjpq,qv->cujv/dot_general | solution.py:28
  125.5 4.2 %convert_bitcast_fusion = bf16[16,64,8,64]{3,1,2,0:T(8,128)(2,1)S(1)} fusion(f32[16,8,64,64]{2,3,1,0:T(8,128)S(1)} %fusion.2, f32[64]{0:T(128)S(1)} %get-tuple-element.3, f32[64]{0:T(128)S(1)} %multiply_add_fusion, f32[64]{0:T(128)S(1)} %get-tuple-element.2), kind=kOutput, calls=%fused_computation.7 | convolution fusion | flops 403189760 | bytes 3146496 | tf_op jit(solution)/shard_map/pu,cjpq,qv->cujv/dot_general | solution.py:28
  129.7 3.1 %copy.34 = bf16[16,64,8,64]{3,2,1,0:T(8,128)(2,1)} copy(bf16[16,64,8,64]{3,1,2,0:T(8,128)(2,1)S(1)} %convert_bitcast_fusion) | data formatting | bytes 2097152 | tf_op jit(solution)/shard_map/convert_element_type | solution.py:53
  132.8 4.0 %convert_element_type.39 = bf16[1,1024,512]{2,1,0:T(8,128)(2,1)} reshape(bf16[16,64,8,64]{3,2,1,0:T(8,128)(2,1)} %copy.34) | data formatting | bytes 2097152 | tf_op jit(solution)/shard_map/convert_element_type | solution.py:53
  136.9 9.3 %all-gather = bf16[128,8,128]{2,1,0:T(8,128)(2,1)S(1)} all-gather(bf16[16,8,128]{2,1,0:T(8,128)(2,1)S(1)} %convolution_convert_fusion.1), channel_id=2, replica_groups=mesh['replica'=8,'fsdp'=4] {'replica'}, dimensions={0}, use_global_device_ids=true | all-gather | bytes 294912 | tf_op jit(solution)/shard_map/all_gather | solution.py:57
  146.1 2.2 %convolution_bitcast_fusion.1 = f32[16,256,128]{2,1,0:T(8,128)} fusion(s32[8,16,8]{0,2,1:T(8,128)S(1)} %copy-done.2, bf16[8,16,8,128]{3,2,1,0:T(8,128)(2,1)S(1)} %bitcast.41), kind=kOutput, calls=%fused_computation.9 | convolution fusion | flops 67371008 | bytes 2363392 | tf_op jit(solution)/shard_map/rckb,rckv->cbv/dot_general | solution.py:60
  148.4 4.3 %reshape.41 = f32[16,8,64,64]{3,2,1,0:T(8,128)} reshape(f32[16,256,128]{2,1,0:T(8,128)} %convolution_bitcast_fusion.1) | data formatting | bytes 4194304 | tf_op jit(solution)/shard_map/reshape | solution.py:27
  152.7 5.9 %fusion.9 = f32[16,8,64,64]{2,3,1,0:T(8,128)S(1)} fusion(f32[16,8,64,64]{3,2,1,0:T(8,128)} %reshape.41, f32[64]{0:T(128)S(1)} %get-tuple-element.3, f32[64]{0:T(128)S(1)} %multiply_add_fusion, f32[64]{0:T(128)S(1)} %get-tuple-element.2), kind=kOutput, calls=%fused_computation.18 | convolution fusion | flops 402665472 | bytes 4195072 | tf_op jit(solution)/shard_map/pu,cjpq,qv->cujv/dot_general | solution.py:28
  158.6 3.6 %convolution_bitcast_fusion = f32[16,64,8,64]{3,1,2,0:T(8,128)S(1)} fusion(f32[16,8,64,64]{2,3,1,0:T(8,128)S(1)} %fusion.9, f32[64]{0:T(128)S(1)} %get-tuple-element.3, f32[64]{0:T(128)S(1)} %multiply_add_fusion, f32[64]{0:T(128)S(1)} %get-tuple-element.2), kind=kOutput, calls=%fused_computation.5 | convolution fusion | flops 402665472 | bytes 4195072 | tf_op jit(solution)/shard_map/pu,cjpq,qv->cujv/dot_general | solution.py:28
  162.2 5.2 %copy.39 = f32[16,64,8,64]{3,2,1,0:T(8,128)} copy(f32[16,64,8,64]{3,1,2,0:T(8,128)S(1)} %convolution_bitcast_fusion) | data formatting | bytes 4194304 | tf_op jit(solution)/shard_map/pu,cjpq,qv->cujv/transpose | solution.py:28
  167.4 4.8 %reshape.42 = f32[1024,512]{1,0:T(8,128)} reshape(f32[16,64,8,64]{3,2,1,0:T(8,128)} %copy.39) | data formatting | bytes 4194304 | tf_op jit(solution)/shard_map/reshape | solution.py:29
  (15 shorter events, 0.5 us)
Async XLA Ops:
  7.2 1.6 copy-start
  7.2 85.4 %reduce-scatter.2.cloned.1.call-start = ((), (), s32[]{:S(2)}) async-start(), calls=%async_computation.1 | async-start | bytes 5242880 | tf_op jit(solution)/shard_map/reduce_scatter | solution.py:38
  12.9 0.7 copy-start.3
  12.9 79.6 %copy-start.1 = (bf16[1,1024,512]{2,1,0:T(8,128)(2,1)S(1)}, bf16[1,1024,512]{2,1,0:T(8,128)(2,1)}, u32[]{:S(2)}) copy-start(bf16[1,1024,512]{2,1,0:T(8,128)(2,1)} %param.6) | copy-start | bytes 3145732
  129.7 16.4 %copy-start.2 = (s32[8,16,8]{0,2,1:T(8,128)S(1)}, s32[8,16,8]{0,2,1:T(8,128)}, u32[]{:S(2)}) copy-start(s32[8,16,8]{0,2,1:T(8,128)} %copy.35) | copy-start | bytes 12292
Sparse Core Ops, SparseCore 0:
  13.1 79.4 reduce-scatter.1
where the time goes:
time: 180 us; the launch traced here: 179 us
  waiting for transfers between devices  67.2 us (37%)
  matrix products  41.1 us (23%)
  local copies, waits for them, and re-layouts  33.8 us (19%)
  blocking collectives  19.8 us (11%)
  between operations  14.1 us (8%)
  other arithmetic  2.98 us (2%)
    reduce_scatter x1, waiting for transfers between devices, body(): lax.psum_scatter(lax.dot_general(activations, output_grads, (((0,), (0,))...  67.2 us
    dot_general x4, matrix products, inverse_blocks(): jnp.einsum('pu,cjpq,qv->cujv', table, shaped, table, precision=lax.Precis...  20.1 us
    dot_general x2, matrix products, forward_blocks(): jnp.einsum('pu,cujv,qv->cjpq', table, shaped, table, precision=lax.Precis...  12.2 us
    all_gather x1, blocking collectives, body(): piece_numbers = lax.all_gather(picks[None], 'replica', axis=0, tiled=True)  10.5 us
    all_gather x1, blocking collectives, body(): piece_values = lax.all_gather(values[None], 'replica', axis=0, tiled=True)  9.27 us
    convert_element_type x2, local copies, waits for them, and re-layouts, body(): inverse_blocks(kept, table, size, block_len).astype(jnp.bfloat16)  7.16 us
    transpose x1, local copies, waits for them, and re-layouts, inverse_blocks(): jnp.einsum('pu,cjpq,qv->cujv', table, shaped, table, precision=lax.Precis...  5.21 us
    reshape x1, local copies, waits for them, and re-layouts, inverse_blocks(): return field.reshape(rows * size, cols * size)  4.77 us
  transfers between devices with their start and end apart: 1, of which 1 were waited for; matrix products, arithmetic and copies ran while one was open for 1% of the time, Pallas kernels for 0%

commit v1 on v0

v1 whole, which is shorter than its diff:
```python
import functools

import jax
import jax.numpy as jnp
import numpy as np
from jax import lax
from jax.experimental import pallas as pl
from jax.experimental.pallas import tpu as pltpu
from jax.sharding import PartitionSpec as P

F32 = jnp.float32
BF16 = jnp.bfloat16
SIZE = 64
LANES = 128
GROUP = 4


def table_parts():
    order = np.arange(SIZE, dtype=np.float64)[:, None]
    place = np.arange(SIZE, dtype=np.float64)[None, :]
    factor = np.where(order == 0, np.sqrt(1.0 / SIZE), np.sqrt(2.0 / SIZE))
    table = factor * np.cos(np.pi * (2 * place + 1) * order / (2 * SIZE))
    high = table.astype(jnp.bfloat16)
    low = (table - high.astype(np.float64)).astype(jnp.bfloat16)
    return high, low


def dot(a, b):
    return lax.dot_general(a, b, (((1,), (0,)), ((), ())), preferred_element_type=F32)


def dot_nt(a, b):
    return lax.dot_general(a, b, (((1,), (1,)), ((), ())), preferred_element_type=F32)


def dot_tn(a, b):
    return lax.dot_general(a, b, (((0,), (0,)), ((), ())), preferred_element_type=F32)


def split(x):
    high = x.astype(BF16)
    return high, (x - high.astype(F32)).astype(BF16)


def iota(shape, dim):
    return lax.broadcasted_iota(jnp.int32, shape, dim)


def choice(picks, top):
    crows = picks.shape[0]
    rows = crows * top * 2
    r1 = iota((rows, crows), 0)
    owner = GROUP * (r1 // (2 * GROUP * top)) + (r1 // top) % GROUP
    spread = (iota((rows, crows), 1) == owner).astype(F32).astype(BF16)
    r2 = iota((rows, LANES), 0)
    numbers = jnp.where(iota((rows, LANES), 1) == r2 % top, dot(spread, picks), 0.0)
    number = jnp.sum(numbers, axis=1, keepdims=True).astype(jnp.int32)
    half = (iota((rows, 1), 0) // (GROUP * top)) % 2
    return number // (SIZE // 2), 2 * (number % (SIZE // 2)) + half


def onehot(order):
    rows = order.shape[0]
    return (iota((rows, SIZE), 1) == order).astype(F32).astype(BF16)


def chosen_rows(order, top, c4h, c4l):
    rows = order.shape[0]
    hot = onehot(order)
    own = (iota((rows, GROUP * SIZE), 1) // SIZE) == ((iota((rows, GROUP * SIZE), 0) // top) % GROUP)
    high = jnp.where(own, dot(hot, c4h), 0.0).astype(BF16)
    low = jnp.where(own, dot(hot, c4l), 0.0).astype(BF16)
    return high, low


def span_mask(span, width):
    rows = span.shape[0]
    return (iota((rows, width), 1) // SIZE) == span


def forward_cols(masked, csth, cstl):
    high, low = split(masked)
    return dot_nt(high, csth) + dot_nt(low, csth) + dot_nt(high, cstl)


def pack_halves(v, top):
    step = GROUP * top
    parts = []
    for g in range(v.shape[0] // (2 * step)):
        a = v[2 * g * step : (2 * g + 1) * step]
        b = v[(2 * g + 1) * step : (2 * g + 2) * step]
        parts.append(jnp.concatenate([a, b], axis=1))
    return jnp.concatenate(parts, axis=0)


def chosen_kernel(top, me_ref, picks_ref, acts_ref, g_ref, m_ref, c4h_ref, c4l_ref, csth_ref, cstl_ref,
                  own_ref, o1_ref, o2_ref, o3_ref):
    me = me_ref[0]
    shard = m_ref.shape[0]
    width = m_ref.shape[1]
    crows = shard // SIZE
    groups = crows // GROUP
    c4h, c4l = c4h_ref[...], c4l_ref[...]
    csth, cstl = csth_ref[...], cstl_ref[...]
    gmat = g_ref[...]
    outs = (own_ref, o1_ref, o2_ref, o3_ref)
    for s in range(4):
        target = me ^ s
        span, order = choice(picks_ref[s * crows : (s + 1) * crows, :], top)
        high, low = chosen_rows(order, top, c4h, c4l)
        step = 2 * GROUP * top
        parts = []
        for g in range(groups):
            start = pl.multiple_of(target * shard + g * GROUP * SIZE, GROUP * SIZE)
            block = acts_ref[:, pl.ds(start, GROUP * SIZE)]
            both = jnp.concatenate([high[g * step : (g + 1) * step], low[g * step : (g + 1) * step]], axis=0)
            t = dot_nt(both, block)
            parts.append(t[:step] + t[step:])
        th, tl = split(jnp.concatenate(parts, axis=0))
        a = dot(th, gmat) + dot(tl, gmat)
        if s == 0:
            parts = []
            for g in range(groups):
                block = m_ref[g * GROUP * SIZE : (g + 1) * GROUP * SIZE, :]
                parts.append(
                    dot(high[g * step : (g + 1) * step], block) + dot(low[g * step : (g + 1) * step], block)
                )
            a = a + 0.9 * jnp.concatenate(parts, axis=0)
        v = forward_cols(jnp.where(span_mask(span, width), a, 0.0), csth, cstl)
        outs[s][...] = pack_halves(v, top).astype(outs[s].dtype)


def base_kernel(top, picks_ref, v_ref, m_ref, a0_ref, ao_ref, g_ref, gp_ref, c4th_ref, c4tl_ref, csth_ref, cstl_ref,
                out_ref):
    shard, width = m_ref.shape
    crows = shard // SIZE
    groups = crows // GROUP
    step = GROUP * top
    span, order = choice(picks_ref[...], top)
    hot = onehot(order)
    v = v_ref[...]
    parts = []
    for g in range(groups):
        block = v[g * step : (g + 1) * step]
        parts += [block[:, :SIZE], block[:, SIZE:]]
    vh, vl = split(jnp.concatenate(parts, axis=0))
    csth, cstl = csth_ref[...], cstl_ref[...]
    x = dot(vh, csth) + dot(vl, csth) + dot(vh, cstl)
    xh, xl = split(jnp.where(span_mask(span, width), x, 0.0))
    gmat, gpmat = g_ref[...], gp_ref[...]
    rows = GROUP * SIZE
    own = (iota((rows, 2 * step), 0) // SIZE) == ((iota((rows, 2 * step), 1) // top) % GROUP)
    for g in range(groups):
        here = slice(g * 2 * step, (g + 1) * 2 * step)
        th = jnp.where(own, dot_nt(c4th_ref[...], hot[here]), 0.0).astype(BF16)
        tl = jnp.where(own, dot_nt(c4tl_ref[...], hot[here]), 0.0).astype(BF16)
        inv = dot(th, xh[here]) + dot(tl, xh[here]) + dot(th, xl[here])
        at = slice(g * rows, (g + 1) * rows)
        pair = dot_tn(a0_ref[:, at], gmat) + dot_tn(ao_ref[:, at], gpmat)
        out_ref[at, :] = 0.9 * m_ref[at, :].astype(F32) + pair - inv


def update_kernel(top, crows, pack_ref, c2th_ref, c2tl_ref, csth_ref, cstl_ref, out_ref, xh_ref, xl_ref):
    reps = pack_ref.shape[0]
    width = out_ref.shape[1]
    per = crows * top

    @pl.when(pl.program_id(0) == 0)
    def _():
        out_ref[...] = jnp.zeros_like(out_ref)

    r1 = iota((per, crows), 0)
    spread = (iota((per, crows), 1) == r1 // top).astype(F32).astype(BF16)
    pickmask = iota((per, LANES), 1) == iota((per, LANES), 0) % top
    csth, cstl = csth_ref[...], cstl_ref[...]
    zero = jnp.zeros_like(csth)
    numbers = []
    for r in range(reps):
        v = pack_ref[r, :per, :]
        picks = pack_ref[r, per : per + crows, :]
        number = jnp.sum(jnp.where(pickmask, dot(spread, picks), 0.0), axis=1, keepdims=True).astype(jnp.int32)
        numbers.append(number)
        mask = span_mask(number // (SIZE // 2), width)
        for p in range(2):
            wh = jnp.concatenate([csth, zero] if p == 0 else [zero, csth], axis=0)
            wl = jnp.concatenate([cstl, zero] if p == 0 else [zero, cstl], axis=0)
            xh, xl = split(jnp.where(mask, dot(v, wh) + dot(v, wl), 0.0))
            xh_ref[p, r] = xh
            xl_ref[p, r] = xl
    pair = 2 * top
    cols = 2 * reps * pair
    rows = 2 * SIZE
    own = (iota((rows, cols), 0) // SIZE) == ((iota((rows, cols), 1) // top) % 2)
    for g in range(crows // 2):
        at = slice(g * pair, (g + 1) * pair)
        bh = jnp.concatenate([xh_ref[p, r, at, :] for p in range(2) for r in range(reps)], axis=0)
        bl = jnp.concatenate([xl_ref[p, r, at, :] for p in range(2) for r in range(reps)], axis=0)
        order = jnp.concatenate(
            [2 * (numbers[r][at] % (SIZE // 2)) + p for p in range(2) for r in range(reps)], axis=0
        )
        hot = onehot(order)
        th = jnp.where(own, dot_nt(c2th_ref[...], hot), 0.0).astype(BF16)
        tl = jnp.where(own, dot_nt(c2tl_ref[...], hot), 0.0).astype(BF16)
        out_ref[g * rows : (g + 1) * rows, :] += dot(th, bh) + dot(tl, bh) + dot(th, bl)


VMEM = functools.partial(pl.BlockSpec, memory_space=pltpu.VMEM)
PARAMS = pltpu.CompilerParams(vmem_limit_bytes=32 * 1024 * 1024)


def swap(x, bit, axis, size):
    return lax.ppermute(x, axis, [(i, i ^ bit) for i in range(size)])


def gather_replicas(x, replicas):
    if replicas & (replicas - 1):
        return lax.all_gather(x, "replica", axis=0, tiled=False)
    stack, bit = x[None], 1
    while bit < replicas:
        stack = jnp.concatenate([stack, swap(stack, bit, "replica", replicas)], axis=0)
        bit *= 2
    return stack


def body(replicas, fsdp, activations, output_grads, momentum, chosen_blocks):
    old = momentum[0]
    shard, width = old.shape
    tokens = activations.shape[0]
    crows = shard // SIZE
    top = chosen_blocks.shape[2]
    chunks = 4
    rows = shard // chunks
    spans = width // SIZE
    high, low = table_parts()
    c4h, c4l = (np.tile(t, (1, GROUP)) for t in (high, low))
    c4th, c4tl = (np.tile(t.T, (GROUP, 1)) for t in (high, low))
    c2th, c2tl = (np.tile(t.T, (2, 1)) for t in (high, low))
    csth, cstl = (np.tile(t, (1, spans)) for t in (high, low))
    me = lax.axis_index("fsdp")

    partner_grads = swap(output_grads, 1, "fsdp", fsdp)
    picks = jnp.pad(chosen_blocks[0].astype(BF16), ((0, 0), (0, LANES - top)))

    def columns(s, start, size):
        return lax.dynamic_slice(activations, (0, (me ^ s) * shard + start), (tokens, size))

    partner_cols = [swap(columns(3, i * rows, rows), 1, "fsdp", fsdp) for i in range(chunks)]
    picks2 = jnp.concatenate([picks, swap(picks, 1, "fsdp", fsdp)], axis=0)
    picks4 = jnp.concatenate([picks2, swap(picks2, 2, "fsdp", fsdp)], axis=0)
    partner_own = swap(columns(1, 0, shard), 1, "fsdp", fsdp)

    vals = jax.ShapeDtypeStruct((crows * top, 2 * SIZE), BF16)
    v0, v1, v2, v3 = pl.pallas_call(
        functools.partial(chosen_kernel, top),
        out_shape=[jax.ShapeDtypeStruct((crows * top, 2 * SIZE), F32), vals, vals, vals],
        in_specs=[pl.BlockSpec(memory_space=pltpu.SMEM)] + [VMEM()] * 8,
        out_specs=[VMEM()] * 4,
        compiler_params=PARAMS,
        name="chosen",
    )(jnp.reshape(me, (1,)), picks4, activations, output_grads, old, c4h, c4l, csth, cstl)
    from_partner = swap(jnp.concatenate([v1, v3], axis=0), 1, "fsdp", fsdp)
    own_pair = v0 + from_partner[: crows * top].astype(F32)
    far_pair = (v2.astype(F32) + from_partner[crows * top :].astype(F32)).astype(BF16)
    values = own_pair + swap(far_pair, 2, "fsdp", fsdp).astype(F32)
    pack = jnp.concatenate([values.astype(BF16), picks], axis=0)

    sums = []
    for i in range(chunks):
        s = dot_tn(columns(2, i * rows, rows), output_grads) + dot_tn(partner_cols[i], partner_grads)
        sums.append(swap(s.astype(BF16), 2, "fsdp", fsdp))

    base = pl.pallas_call(
        functools.partial(base_kernel, top),
        out_shape=jax.ShapeDtypeStruct((shard, width), F32),
        in_specs=[VMEM()] * 11,
        out_specs=VMEM(),
        compiler_params=PARAMS,
        name="base",
    )(picks, values, old, columns(0, 0, shard), partner_own, output_grads, partner_grads, c4th, c4tl, csth, cstl)

    everyone = gather_replicas(pack, replicas)
    step = 8 if replicas % 8 == 0 else 1
    update = pl.pallas_call(
        functools.partial(update_kernel, top, crows),
        grid=(replicas // step,),
        out_shape=jax.ShapeDtypeStruct((shard, width), F32),
        in_specs=[pl.BlockSpec((step, pack.shape[0], LANES), lambda i: (i, 0, 0))] + [VMEM()] * 4,
        out_specs=pl.BlockSpec((shard, width), lambda i: (0, 0)),
        scratch_shapes=[pltpu.VMEM((2, step, crows * top, width), BF16)] * 2,
        compiler_params=PARAMS,
        name="update",
    )(everyone, c2th, c2tl, csth, cstl)
    moment_next = (base + jnp.concatenate(sums, axis=0).astype(F32)).astype(BF16)
    return moment_next[None], update


def solution(mesh):
    return jax.shard_map(
        functools.partial(body, mesh.shape["replica"], mesh.shape["fsdp"]),
        mesh=mesh,
        in_specs=(
            P(("replica", "fsdp"), None),
            P(("replica", "fsdp"), None),
            P("replica", "fsdp", None),
            P("replica", "fsdp", None),
        ),
        out_specs=(P("replica", "fsdp", None), P("fsdp", None)),
        check_vma=False,
    )
```

time: 180 us -> 103 us (0.57)
  matrix products: 41.1 us -> 6.43 us
  local copies, waits for them, and re-layouts: 33.8 us -> 5.35 us
  starting transfers between devices: 0.04 us -> 26.2 us
  blocking collectives: 19.8 us -> 0 us
  waiting for transfers between devices: 67.2 us -> 48.7 us
  between operations: 14.1 us -> 0.93 us
  Pallas kernels: 0 us -> 13.1 us
    reduce_scatter x1 -> x0, waiting for transfers between devices: 67.2 us -> none  [body(): lax.psum_scatter(lax.dot_general(activations, output_grads, (((0,), (0,))...]
    ppermute x0 -> x17, waiting for transfers between devices: none -> 48.7 us  [swap(): return lax.ppermute(x, axis, [(i, i ^ bit) for i in range(size)])]
    dot_general x9 -> x8, matrix products: 41.1 us -> 6.43 us  [dot_tn(): lax.dot_general(a, b, (((0,), (0,)), ((), ())), preferred_element_type=F32)]
    ppermute x0 -> x17, starting transfers between devices: none -> 26.2 us  [swap(): return lax.ppermute(x, axis, [(i, i ^ bit) for i in range(size)])]
    all_gather x2 -> x0, blocking collectives: 19.8 us -> none  [the longest x1 10.5 us: body(): piece_numbers = lax.all_gather(picks[None], 'replica', axis=0, tiled=True)]
    reshape x4 -> x0, local copies, waits for them, and re-layouts: 18.1 us -> none  [the longest x1 4.77 us: inverse_blocks(): return field.reshape(rows * size, cols * size)]
    pallas_call x0 -> x3, Pallas kernels: none -> 13.1 us  [the longest x1 5.16 us: body(): pl.pallas_call(functools.partial(update_kernel, top, crows), grid=(replic...]
    convert_element_type x2 -> x1, local copies, waits for them, and re-layouts: 7.16 us -> 0.09 us  [body(): picks = jnp.pad(chosen_blocks[0].astype(BF16), ((0, 0), (0, LANES - top)))]
  transfers between devices with their start and end apart: 1 -> 17, of which waited for: 1 -> 9; matrix products, arithmetic and copies ran while one was open for 1% -> 10% of each run, Pallas kernels for 0% -> 13%
where the time goes in v1:
time: 103 us
  waiting for transfers between devices  48.7 us (47%)
  starting transfers between devices  26.2 us (25%)
  Pallas kernels  13.1 us (13%)
  matrix products  6.43 us (6%)
  local copies, waits for them, and re-layouts  5.35 us (5%)
  other arithmetic  2.29 us (2%)
    ppermute x17, waiting for transfers between devices, swap(): return lax.ppermute(x, axis, [(i, i ^ bit) for i in range(size)])  48.7 us
    ppermute x17, starting transfers between devices, swap(): return lax.ppermute(x, axis, [(i, i ^ bit) for i in range(size)])  26.2 us
    dot_general x8, matrix products, dot_tn(): lax.dot_general(a, b, (((0,), (0,)), ((), ())), preferred_element_type=F32)  6.43 us
    pallas_call x1, Pallas kernels, body(): pl.pallas_call(functools.partial(update_kernel, top, crows), grid=(replic...  5.16 us
    pallas_call x1, Pallas kernels, body(): pl.pallas_call(functools.partial(chosen_kernel, top), out_shape=[jax.Shap...  4.47 us
    dynamic_slice x2, local copies, waits for them, and re-layouts, columns(): lax.dynamic_slice(activations, (0, (me ^ s) * shard + start), (tokens, si...  3.96 us
    pallas_call x1, Pallas kernels, body(): pl.pallas_call(functools.partial(base_kernel, top), out_shape=jax.ShapeDt...  3.48 us
  transfers between devices with their start and end apart: 17, of which 9 were waited for; matrix products, arithmetic and copies ran while one was open for 10% of the time, Pallas kernels for 13%

profile of v1, /device:TPU:0, one launch (start us, length us, event | category | flops | bytes accessed | tf_op | source)
XLA Modules:
  0.0 103.1 jit_solution(9853025666193422691)
XLA Ops:
  1.6 3.0 %collective-permute-start = (bf16[16,128]{1,0:T(8,128)(2,1)S(1)}, bf16[16,128]{1,0:T(8,128)(2,1)S(1)}, u32[]{:S(2)}, u32[]{:S(2)}) collective-permute-start(bf16[16,128]{1,0:T(8,128)(2,1)S(1)} %pad.4.picks_ref), channel_id=1, source_target_pairs={{0,1},{1,0},{2,3},{3,2},{4,5},{5,4},{6,7},{7,6},{8,9},{9,8},{10,11... | collective-permute-start | bytes 12296 | tf_op jit(solution)/shard_map/ppermute | solution.py:212
  4.7 2.1 %constant_dynamic-slice_fusion.4 = (bf16[256,1024]{1,0:T(8,128)(2,1)}, bf16[256,1024]{1,0:T(8,128)(2,1)S(1)}) fusion(bf16[256,4096]{1,0:T(8,128)(2,1)} %acts_ref.1, s32[]{:T(128)S(6)} %select_n.31, s32[]{:T(128)S(6)} %select_n.30), kind=kLoop, calls=%fused_computation.35 | loop fusion | bytes 2097160 | tf_op jit(solution)/shard_map/dynamic_slice | solution.py:245
  6.8 2.0 %collective-permute-start.5 = (bf16[256,512]{1,0:T(8,128)(2,1)S(1)}, bf16[256,512]{1,0:T(8,128)(2,1)S(1)}, u32[]{:S(2)}, u32[]{:S(2)}) collective-permute-start(bf16[256,512]{1,0:T(8,128)(2,1)S(1)} %copy-done), channel_id=1, source_target_pairs={{0,1},{1,0},{2,3},{3,2},{4,5},{5,4},{6,7},{7,6},{8,9},{9,8},{10,11... | collective-permute-start | bytes 786440 | tf_op jit(solution)/shard_map/ppermute | solution.py:212
  8.8 2.6 %collective-permute-start.1 = (bf16[32,128]{1,0:T(8,128)(2,1)S(1)}, bf16[32,128]{1,0:T(8,128)(2,1)S(1)}, u32[]{:S(2)}, u32[]{:S(2)}) collective-permute-start(bf16[32,128]{1,0:T(8,128)(2,1)S(1)} %pad_maximum_fusion.5), channel_id=1, source_target_pairs={{0,2},{1,3},{2,0},{3,1},{4,6},{5,7},{6,4},{7,5},{8,10},{9,11},{10,... | collective-permute-start | bytes 24584 | tf_op jit(solution)/shard_map/ppermute | solution.py:212
  11.4 1.9 %constant_dynamic-slice_fusion.3 = (bf16[256,256]{1,0:T(8,128)(2,1)}, bf16[256,256]{1,0:T(8,128)(2,1)}, bf16[256,256]{1,0:T(8,128)(2,1)}, bf16[256,256]{1,0:T(8,128)(2,1)}) fusion(bf16[256,4096]{1,0:T(8,128)(2,1)} %acts_ref.1, s32[]{:T(128)S(6)} %select_n.33, s32[]{:T(128)S(6)} %select_n.37, s32[]{:T(128)S(6)} %select_n.35, s32[]{:T(128)S(6)} %select_n.39), kind=kLoop, calls=%fused_computation.33 | loop fusion | bytes 1048592 | tf_op jit(solution)/shard_map/dynamic_slice | solution.py:245
  13.7 1.6 %collective-permute-start.12 = (bf16[256,256]{1,0:T(8,128)(2,1)}, bf16[256,256]{1,0:T(8,128)(2,1)}, u32[]{:S(2)}, u32[]{:S(2)}) collective-permute-start(bf16[256,256]{1,0:T(8,128)(2,1)} %get-tuple-element.15), channel_id=1, source_target_pairs={{0,1},{1,0},{2,3},{3,2},{4,5},{5,4},{6,7},{7,6},{8,9},{9,8},{10,11... | collective-permute-start | bytes 393224 | tf_op jit(solution)/shard_map/ppermute | solution.py:212
  15.3 9.8 %collective-permute-done.1 = bf16[32,128]{1,0:T(8,128)(2,1)S(1)} collective-permute-done((bf16[32,128]{1,0:T(8,128)(2,1)S(1)}, bf16[32,128]{1,0:T(8,128)(2,1)S(1)}, u32[]{:S(2)}, u32[]{:S(2)}) %collective-permute-start.1) | collective-permute-done | bytes 8224 | tf_op jit(solution)/shard_map/ppermute | solution.py:212
  26.4 4.5 %chosen.1 = (f32[128,128]{1,0:T(8,128)S(1)}, bf16[128,128]{1,0:T(8,128)(2,1)S(1)}, bf16[128,128]{1,0:T(8,128)(2,1)S(1)}, bf16[128,128]{1,0:T(8,128)(2,1)S(1)}) custom-call(s32[1]{0:T(128)} %bitcast.1.me_ref, bf16[64,128]{1,0:T(8,128)(2,1)S(1)} %pad_maximum_fusion.4.picks_ref, bf16[256,4096]{1,0:T(8,128)(2,1)S(1)} %copy-done.1, bf16[256,512]{1,0:T(8,128)(2,1)S(1)} %copy-done, ...), custom_call_target="tpu_custom_call" | custom-call | tf_op jit(solution)/shard_map/chosen/pallas_call | solution.py:253
  30.8 5.1 %collective-permute-start.2 = (bf16[256,128]{1,0:T(8,128)(2,1)S(1)}, bf16[256,128]{1,0:T(8,128)(2,1)S(1)}, u32[]{:S(2)}, u32[]{:S(2)}) collective-permute-start(bf16[256,128]{1,0:T(8,128)(2,1)S(1)} %pad_maximum_fusion.3), channel_id=1, source_target_pairs={{0,1},{1,0},{2,3},{3,2},{4,5},{5,4},{6,7},{7,6},{8,9},{9,8},{10,11... | collective-permute-start | bytes 196616 | tf_op jit(solution)/shard_map/ppermute | solution.py:212
  37.1 1.5 %collective-permute-done.2 = bf16[256,128]{1,0:T(8,128)(2,1)S(1)} collective-permute-done((bf16[256,128]{1,0:T(8,128)(2,1)S(1)}, bf16[256,128]{1,0:T(8,128)(2,1)S(1)}, u32[]{:S(2)}, u32[]{:S(2)}) %collective-permute-start.2) | collective-permute-done | bytes 65568 | tf_op jit(solution)/shard_map/ppermute | solution.py:212
  39.7 3.7 %collective-permute-done.3 = bf16[128,128]{1,0:T(8,128)(2,1)S(1)} collective-permute-done((bf16[128,128]{1,0:T(8,128)(2,1)S(1)}, bf16[128,128]{1,0:T(8,128)(2,1)S(1)}, u32[]{:S(2)}, u32[]{:S(2)}) %collective-permute-start.3) | collective-permute-done | bytes 32800 | tf_op jit(solution)/shard_map/ppermute | solution.py:212
  44.8 1.6 %collective-permute-start.15 = (bf16[2,144,128]{2,1,0:T(8,128)(2,1)S(1)}, bf16[2,144,128]{2,1,0:T(8,128)(2,1)S(1)}, u32[]{:S(2)}, u32[]{:S(2)}) collective-permute-start(bf16[2,144,128]{2,1,0:T(8,128)(2,1)S(1)} %pad_maximum_fusion.2), channel_id=1, source_target_pairs={{0,8},{4,12},{8,0},{12,4},{16,24},{20,28},{24,16},{28,20},{1,9},{5... | collective-permute-start | bytes 221192 | tf_op jit(solution)/shard_map/ppermute | solution.py:212
  46.6 2.8 %collective-permute-done.15 = bf16[2,144,128]{2,1,0:T(8,128)(2,1)S(1)} collective-permute-done((bf16[2,144,128]{2,1,0:T(8,128)(2,1)S(1)}, bf16[2,144,128]{2,1,0:T(8,128)(2,1)S(1)}, u32[]{:S(2)}, u32[]{:S(2)}) %collective-permute-start.15) | collective-permute-done | bytes 73760 | tf_op jit(solution)/shard_map/ppermute | solution.py:212
  49.4 1.7 %collective-permute-start.8 = (bf16[256,256]{1,0:T(8,128)(2,1)}, bf16[256,256]{1,0:T(8,128)(2,1)S(1)}, u32[]{:S(2)}, u32[]{:S(2)}) collective-permute-start(bf16[256,256]{1,0:T(8,128)(2,1)} %get-tuple-element.14), channel_id=1, source_target_pairs={{0,1},{1,0},{2,3},{3,2},{4,5},{5,4},{6,7},{7,6},{8,9},{9,8},{10,11... | collective-permute-start | bytes 393224 | tf_op jit(solution)/shard_map/ppermute | solution.py:212
  51.5 1.5 %collective-permute-start.16 = (bf16[4,144,128]{2,1,0:T(8,128)(2,1)S(1)}, bf16[4,144,128]{2,1,0:T(8,128)(2,1)S(1)}, u32[]{:S(2)}, u32[]{:S(2)}) collective-permute-start(bf16[4,144,128]{2,1,0:T(8,128)(2,1)S(1)} %pad_maximum_fusion.1), channel_id=1, source_target_pairs={{0,16},{4,20},{8,24},{12,28},{16,0},{20,4},{24,8},{28,12},{1,17},{... | collective-permute-start | bytes 442376 | tf_op jit(solution)/shard_map/ppermute | solution.py:212
  53.1 1.4 %fusion.2 = bf16[256,512]{1,0:T(8,128)(2,1)S(1)} fusion(f32[256,512]{1,0:T(8,128)} %fusion.7, bf16[256,256]{1,0:T(8,128)(2,1)} %collective-permute-done.10, bf16[256,512]{1,0:T(8,128)(2,1)S(1)} %collective-permute-done.5.gp_ref), kind=kOutput, calls=%fused_computation.7 | convolution fusion | flops 67371008 | bytes 1179648 | tf_op jit(solution)/shard_map/dot_general | solution.py:37
  56.2 2.5 %collective-permute-start.13 = (bf16[256,512]{1,0:T(8,128)(2,1)S(1)}, bf16[256,512]{1,0:T(8,128)(2,1)S(1)}, u32[]{:S(2)}, u32[]{:S(2)}) collective-permute-start(bf16[256,512]{1,0:T(8,128)(2,1)S(1)} %fusion.3), channel_id=1, source_target_pairs={{0,2},{1,3},{2,0},{3,1},{4,6},{5,7},{6,4},{7,5},{8,10},{9,11},{10,... | collective-permute-start | bytes 786440 | tf_op jit(solution)/shard_map/ppermute | solution.py:212
  59.8 2.5 %collective-permute-start.7 = (bf16[256,512]{1,0:T(8,128)(2,1)S(1)}, bf16[256,512]{1,0:T(8,128)(2,1)S(1)}, u32[]{:S(2)}, u32[]{:S(2)}) collective-permute-start(bf16[256,512]{1,0:T(8,128)(2,1)S(1)} %fusion), channel_id=1, source_target_pairs={{0,2},{1,3},{2,0},{3,1},{4,6},{5,7},{6,4},{7,5},{8,10},{9,11},{10,... | collective-permute-start | bytes 786440 | tf_op jit(solution)/shard_map/ppermute | solution.py:212
  62.4 5.2 %update.1 = f32[1024,512]{1,0:T(8,128)} custom-call(bf16[8,144,128]{2,1,0:T(8,128)(2,1)S(1)} %pad_maximum_fusion.pack_ref, bf16[128,64]{1,0:T(8,128)(2,1)S(1)} %copy-done.8, bf16[128,64]{1,0:T(8,128)(2,1)S(1)} %copy-done.9, bf16[64,512]{1,0:T(8,128)(2,1)S(1)} %copy-done.4, bf16[64,512]{1,0:T(8,128)(2,1)S(1)} %copy-done.5), custom_call_target="tpu_custom_call" | custom-call | tf_op jit(solution)/shard_map/update/pallas_call | solution.py:283
  67.5 3.5 %base.1 = f32[1024,512]{1,0:T(8,128)S(1)} custom-call(bf16[16,128]{1,0:T(8,128)(2,1)S(1)} %pad.4.picks_ref, f32[128,128]{1,0:T(8,128)S(1)} %get-tuple-element.11.v_ref, bf16[1024,512]{1,0:T(8,128)(2,1)S(1)} %bitcast.21, bf16[256,1024]{1,0:T(8,128)(2,1)S(1)} %get-tuple-element.17.a0_ref, bf16[256,1024]{1,0:T(8,128)(2,1)} %collective-permute-done.4.ao_ref, ...), custom_call_target="tpu_custom_call" | custom-call | tf_op jit(solution)/shard_map/base/pallas_call | solution.py:272
  71.0 15.0 %collective-permute-done.11 = bf16[256,512]{1,0:T(8,128)(2,1)S(1)} collective-permute-done((bf16[256,512]{1,0:T(8,128)(2,1)S(1)}, bf16[256,512]{1,0:T(8,128)(2,1)S(1)}, u32[]{:S(2)}, u32[]{:S(2)}) %collective-permute-start.11) | collective-permute-done | bytes 262176 | tf_op jit(solution)/shard_map/ppermute | solution.py:212
  86.1 5.6 %collective-permute-done.13 = bf16[256,512]{1,0:T(8,128)(2,1)S(1)} collective-permute-done((bf16[256,512]{1,0:T(8,128)(2,1)S(1)}, bf16[256,512]{1,0:T(8,128)(2,1)S(1)}, u32[]{:S(2)}, u32[]{:S(2)}) %collective-permute-start.13) | collective-permute-done | bytes 262176 | tf_op jit(solution)/shard_map/ppermute | solution.py:212
  91.7 5.6 %collective-permute-done.9 = bf16[256,512]{1,0:T(8,128)(2,1)S(1)} collective-permute-done((bf16[256,512]{1,0:T(8,128)(2,1)S(1)}, bf16[256,512]{1,0:T(8,128)(2,1)S(1)}, u32[]{:S(2)}, u32[]{:S(2)}) %collective-permute-start.9) | collective-permute-done | bytes 262176 | tf_op jit(solution)/shard_map/ppermute | solution.py:212
  97.3 4.4 %collective-permute-done.7 = bf16[256,512]{1,0:T(8,128)(2,1)S(1)} collective-permute-done((bf16[256,512]{1,0:T(8,128)(2,1)S(1)}, bf16[256,512]{1,0:T(8,128)(2,1)S(1)}, u32[]{:S(2)}, u32[]{:S(2)}) %collective-permute-start.7) | collective-permute-done | bytes 262176 | tf_op jit(solution)/shard_map/ppermute | solution.py:212
  (64 shorter events, 11.1 us)
Async XLA Ops:
  0.6 24.5 %copy-start.10 = (bf16[64,256]{1,0:T(8,128)(2,1)S(1)}, bf16[64,256]{1,0:T(8,128)(2,1)}, u32[]{:S(2)}) copy-start(bf16[64,256]{1,0:T(8,128)(2,1)} %constant.49.clone.c4h_ref) | copy-start | bytes 98308
  0.6 24.5 %copy-start.11 = (bf16[64,256]{1,0:T(8,128)(2,1)S(1)}, bf16[64,256]{1,0:T(8,128)(2,1)}, u32[]{:S(2)}) copy-start(bf16[64,256]{1,0:T(8,128)(2,1)} %constant.50.clone.c4l_ref) | copy-start | bytes 98308
  0.7 24.5 %copy-start.4 = (bf16[64,512]{1,0:T(8,128)(2,1)S(1)}, bf16[64,512]{1,0:T(8,128)(2,1)}, u32[]{:S(2)}) copy-start(bf16[64,512]{1,0:T(8,128)(2,1)} %constant.51.clone.csth_ref) | copy-start | bytes 196612
  0.7 24.4 %copy-start.5 = (bf16[64,512]{1,0:T(8,128)(2,1)S(1)}, bf16[64,512]{1,0:T(8,128)(2,1)}, u32[]{:S(2)}) copy-start(bf16[64,512]{1,0:T(8,128)(2,1)} %constant.52.clone.cstl_ref) | copy-start | bytes 196612
  0.7 24.4 %copy-start.1 = (bf16[256,4096]{1,0:T(8,128)(2,1)S(1)}, bf16[256,4096]{1,0:T(8,128)(2,1)}, u32[]{:S(2)}) copy-start(bf16[256,4096]{1,0:T(8,128)(2,1)} %acts_ref.1) | copy-start | bytes 6291460
  1.6 7.1 %collective-permute-start = (bf16[16,128]{1,0:T(8,128)(2,1)S(1)}, bf16[16,128]{1,0:T(8,128)(2,1)S(1)}, u32[]{:S(2)}, u32[]{:S(2)}) collective-permute-start(bf16[16,128]{1,0:T(8,128)(2,1)S(1)} %pad.4.picks_ref), channel_id=1, source_target_pairs={{0,1},{1,0},{2,3},{3,2},{4,5},{5,4},{6,7},{7,6},{8,9},{9,8},{10,11... | collective-permute-start | bytes 12296 | tf_op jit(solution)/shard_map/ppermute | solution.py:212
  6.7 60.8 %collective-permute-start.4 = (bf16[256,1024]{1,0:T(8,128)(2,1)}, bf16[256,1024]{1,0:T(8,128)(2,1)}, u32[]{:S(2)}, u32[]{:S(2)}) collective-permute-start(bf16[256,1024]{1,0:T(8,128)(2,1)} %get-tuple-element.16), channel_id=1, source_target_pairs={{0,1},{1,0},{2,3},{3,2},{4,5},{5,4},{6,7},{7,6},{8,9},{9,8},{10,11... | collective-permute-start | bytes 1572872 | tf_op jit(solution)/shard_map/ppermute | solution.py:212
  6.8 44.8 %collective-permute-start.5 = (bf16[256,512]{1,0:T(8,128)(2,1)S(1)}, bf16[256,512]{1,0:T(8,128)(2,1)S(1)}, u32[]{:S(2)}, u32[]{:S(2)}) collective-permute-start(bf16[256,512]{1,0:T(8,128)(2,1)S(1)} %copy-done), channel_id=1, source_target_pairs={{0,1},{1,0},{2,3},{3,2},{4,5},{5,4},{6,7},{7,6},{8,9},{9,8},{10,11... | collective-permute-start | bytes 786440 | tf_op jit(solution)/shard_map/ppermute | solution.py:212
  8.8 16.3 %collective-permute-start.1 = (bf16[32,128]{1,0:T(8,128)(2,1)S(1)}, bf16[32,128]{1,0:T(8,128)(2,1)S(1)}, u32[]{:S(2)}, u32[]{:S(2)}) collective-permute-start(bf16[32,128]{1,0:T(8,128)(2,1)S(1)} %pad_maximum_fusion.5), channel_id=1, source_target_pairs={{0,2},{1,3},{2,0},{3,1},{4,6},{5,7},{6,4},{7,5},{8,10},{9,11},{10,... | collective-permute-start | bytes 24584 | tf_op jit(solution)/shard_map/ppermute | solution.py:212
  13.3 37.8 %collective-permute-start.10 = (bf16[256,256]{1,0:T(8,128)(2,1)}, bf16[256,256]{1,0:T(8,128)(2,1)}, u32[]{:S(2)}, u32[]{:S(2)}) collective-permute-start(bf16[256,256]{1,0:T(8,128)(2,1)} %get-tuple-element.13), channel_id=1, source_target_pairs={{0,1},{1,0},{2,3},{3,2},{4,5},{5,4},{6,7},{7,6},{8,9},{9,8},{10,11... | collective-permute-start | bytes 393224 | tf_op jit(solution)/shard_map/ppermute | solution.py:212
  13.7 40.7 %collective-permute-start.12 = (bf16[256,256]{1,0:T(8,128)(2,1)}, bf16[256,256]{1,0:T(8,128)(2,1)}, u32[]{:S(2)}, u32[]{:S(2)}) collective-permute-start(bf16[256,256]{1,0:T(8,128)(2,1)} %get-tuple-element.15), channel_id=1, source_target_pairs={{0,1},{1,0},{2,3},{3,2},{4,5},{5,4},{6,7},{7,6},{8,9},{9,8},{10,11... | collective-permute-start | bytes 393224 | tf_op jit(solution)/shard_map/ppermute | solution.py:212
  30.8 7.7 %collective-permute-start.2 = (bf16[256,128]{1,0:T(8,128)(2,1)S(1)}, bf16[256,128]{1,0:T(8,128)(2,1)S(1)}, u32[]{:S(2)}, u32[]{:S(2)}) collective-permute-start(bf16[256,128]{1,0:T(8,128)(2,1)S(1)} %pad_maximum_fusion.3), channel_id=1, source_target_pairs={{0,1},{1,0},{2,3},{3,2},{4,5},{5,4},{6,7},{7,6},{8,9},{9,8},{10,11... | collective-permute-start | bytes 196616 | tf_op jit(solution)/shard_map/ppermute | solution.py:212
  38.6 4.9 %collective-permute-start.3 = (bf16[128,128]{1,0:T(8,128)(2,1)S(1)}, bf16[128,128]{1,0:T(8,128)(2,1)S(1)}, u32[]{:S(2)}, u32[]{:S(2)}) collective-permute-start(bf16[128,128]{1,0:T(8,128)(2,1)S(1)} %add_convert_fusion.1), channel_id=1, source_target_pairs={{0,2},{1,3},{2,0},{3,1},{4,6},{5,7},{6,4},{7,5},{8,10},{9,11},{10,... | collective-permute-start | bytes 98312 | tf_op jit(solution)/shard_map/ppermute | solution.py:212
  43.5 1.3 %collective-permute-start.14 = (bf16[1,144,128]{2,1,0:T(8,128)(2,1)S(1)}, bf16[1,144,128]{2,1,0:T(8,128)(2,1)S(1)}, u32[]{:S(2)}, u32[]{:S(2)}) collective-permute-start(bf16[1,144,128]{2,1,0:T(8,128)(2,1)S(1)} %maximum_bitcast_fusion), channel_id=1, source_target_pairs={{0,4},{4,0},{8,12},{12,8},{16,20},{20,16},{24,28},{28,24},{1,5},{5... | collective-permute-start | bytes 110600 | tf_op jit(solution)/shard_map/ppermute | solution.py:212
  44.7 10.4 %copy-start.12 = (f32[256,512]{1,0:T(8,128)S(1)}, f32[256,512]{1,0:T(8,128)}, u32[]{:S(2)}) copy-start(f32[256,512]{1,0:T(8,128)} %fusion.5) | copy-start | bytes 1572868
  44.7 14.0 %copy-start.13 = (f32[256,512]{1,0:T(8,128)S(1)}, f32[256,512]{1,0:T(8,128)}, u32[]{:S(2)}) copy-start(f32[256,512]{1,0:T(8,128)} %fusion.9) | copy-start | bytes 1572868
  44.8 4.6 %collective-permute-start.15 = (bf16[2,144,128]{2,1,0:T(8,128)(2,1)S(1)}, bf16[2,144,128]{2,1,0:T(8,128)(2,1)S(1)}, u32[]{:S(2)}, u32[]{:S(2)}) collective-permute-start(bf16[2,144,128]{2,1,0:T(8,128)(2,1)S(1)} %pad_maximum_fusion.2), channel_id=1, source_target_pairs={{0,8},{4,12},{8,0},{12,4},{16,24},{20,28},{24,16},{28,20},{1,9},{5... | collective-permute-start | bytes 221192 | tf_op jit(solution)/shard_map/ppermute | solution.py:212
  49.4 6.8 %collective-permute-start.8 = (bf16[256,256]{1,0:T(8,128)(2,1)}, bf16[256,256]{1,0:T(8,128)(2,1)S(1)}, u32[]{:S(2)}, u32[]{:S(2)}) collective-permute-start(bf16[256,256]{1,0:T(8,128)(2,1)} %get-tuple-element.14), channel_id=1, source_target_pairs={{0,1},{1,0},{2,3},{3,2},{4,5},{5,4},{6,7},{7,6},{8,9},{9,8},{10,11... | collective-permute-start | bytes 393224 | tf_op jit(solution)/shard_map/ppermute | solution.py:212
  51.1 7.9 %collective-permute-start.6 = (bf16[256,256]{1,0:T(8,128)(2,1)}, bf16[256,256]{1,0:T(8,128)(2,1)S(1)}, u32[]{:S(2)}, u32[]{:S(2)}) collective-permute-start(bf16[256,256]{1,0:T(8,128)(2,1)} %get-tuple-element.12), channel_id=1, source_target_pairs={{0,1},{1,0},{2,3},{3,2},{4,5},{5,4},{6,7},{7,6},{8,9},{9,8},{10,11... | collective-permute-start | bytes 393224 | tf_op jit(solution)/shard_map/ppermute | solution.py:212
  51.5 8.3 %collective-permute-start.16 = (bf16[4,144,128]{2,1,0:T(8,128)(2,1)S(1)}, bf16[4,144,128]{2,1,0:T(8,128)(2,1)S(1)}, u32[]{:S(2)}, u32[]{:S(2)}) collective-permute-start(bf16[4,144,128]{2,1,0:T(8,128)(2,1)S(1)} %pad_maximum_fusion.1), channel_id=1, source_target_pairs={{0,16},{4,20},{8,24},{12,28},{16,0},{20,4},{24,8},{28,12},{1,17},{... | collective-permute-start | bytes 442376 | tf_op jit(solution)/shard_map/ppermute | solution.py:212
  54.5 31.6 %collective-permute-start.11 = (bf16[256,512]{1,0:T(8,128)(2,1)S(1)}, bf16[256,512]{1,0:T(8,128)(2,1)S(1)}, u32[]{:S(2)}, u32[]{:S(2)}) collective-permute-start(bf16[256,512]{1,0:T(8,128)(2,1)S(1)} %fusion.2), channel_id=1, source_target_pairs={{0,2},{1,3},{2,0},{3,1},{4,6},{5,7},{6,4},{7,5},{8,10},{9,11},{10,... | collective-permute-start | bytes 786440 | tf_op jit(solution)/shard_map/ppermute | solution.py:212
  56.2 35.5 %collective-permute-start.13 = (bf16[256,512]{1,0:T(8,128)(2,1)S(1)}, bf16[256,512]{1,0:T(8,128)(2,1)S(1)}, u32[]{:S(2)}, u32[]{:S(2)}) collective-permute-start(bf16[256,512]{1,0:T(8,128)(2,1)S(1)} %fusion.3), channel_id=1, source_target_pairs={{0,2},{1,3},{2,0},{3,1},{4,6},{5,7},{6,4},{7,5},{8,10},{9,11},{10,... | collective-permute-start | bytes 786440 | tf_op jit(solution)/shard_map/ppermute | solution.py:212
  59.0 38.3 %collective-permute-start.9 = (bf16[256,512]{1,0:T(8,128)(2,1)S(1)}, bf16[256,512]{1,0:T(8,128)(2,1)S(1)}, u32[]{:S(2)}, u32[]{:S(2)}) collective-permute-start(bf16[256,512]{1,0:T(8,128)(2,1)S(1)} %fusion.1), channel_id=1, source_target_pairs={{0,2},{1,3},{2,0},{3,1},{4,6},{5,7},{6,4},{7,5},{8,10},{9,11},{10,... | collective-permute-start | bytes 786440 | tf_op jit(solution)/shard_map/ppermute | solution.py:212
  59.8 41.9 %collective-permute-start.7 = (bf16[256,512]{1,0:T(8,128)(2,1)S(1)}, bf16[256,512]{1,0:T(8,128)(2,1)S(1)}, u32[]{:S(2)}, u32[]{:S(2)}) collective-permute-start(bf16[256,512]{1,0:T(8,128)(2,1)S(1)} %fusion), channel_id=1, source_target_pairs={{0,2},{1,3},{2,0},{3,1},{4,6},{5,7},{6,4},{7,5},{8,10},{9,11},{10,... | collective-permute-start | bytes 786440 | tf_op jit(solution)/shard_map/ppermute | solution.py:212
  (7 other events, 48.9 us)

commit v2 on v1

--- a/solution.py
+++ b/solution.py
@@ -12,6 +12,7 @@
 BF16 = jnp.bfloat16
 SIZE = 64
 LANES = 128
+GATHER = True
 GROUP = 4
 
 
@@ -94,7 +95,8 @@
 
 
 def chosen_kernel(top, me_ref, picks_ref, acts_ref, g_ref, m_ref, c4h_ref, c4l_ref, csth_ref, cstl_ref,
-                  own_ref, o1_ref, o2_ref, o3_ref):
+                  after_ref, *outs):
+    del after_ref
     me = me_ref[0]
     shard = m_ref.shape[0]
     width = m_ref.shape[1]
@@ -103,7 +105,6 @@
     c4h, c4l = c4h_ref[...], c4l_ref[...]
     csth, cstl = csth_ref[...], cstl_ref[...]
     gmat = g_ref[...]
-    outs = (own_ref, o1_ref, o2_ref, o3_ref)
     for s in range(4):
         target = me ^ s
         span, order = choice(picks_ref[s * crows : (s + 1) * crows, :], top)
@@ -130,8 +131,10 @@
         outs[s][...] = pack_halves(v, top).astype(outs[s].dtype)
 
 
-def base_kernel(top, picks_ref, v_ref, m_ref, a0_ref, ao_ref, g_ref, gp_ref, c4th_ref, c4tl_ref, csth_ref, cstl_ref,
-                out_ref):
+def base_kernel(top, me_ref, picks_ref, v_ref, m_ref, acts_ref, ao_ref, g_ref, gp_ref, c4th_ref, c4tl_ref, csth_ref,
+                cstl_ref, out_ref, a0_ref, sem):
+    copy = fetch(me_ref, acts_ref, 0, 0, a0_ref, sem)
+    copy.start()
     shard, width = m_ref.shape
     crows = shard // SIZE
     groups = crows // GROUP
@@ -148,6 +151,7 @@
     x = dot(vh, csth) + dot(vl, csth) + dot(vh, cstl)
     xh, xl = split(jnp.where(span_mask(span, width), x, 0.0))
     gmat, gpmat = g_ref[...], gp_ref[...]
+    copy.wait()
     rows = GROUP * SIZE
     own = (iota((rows, 2 * step), 0) // SIZE) == ((iota((rows, 2 * step), 1) // top) % GROUP)
     for g in range(groups):
@@ -160,7 +164,8 @@
         out_ref[at, :] = 0.9 * m_ref[at, :].astype(F32) + pair - inv
 
 
-def update_kernel(top, crows, pack_ref, c2th_ref, c2tl_ref, csth_ref, cstl_ref, out_ref, xh_ref, xl_ref):
+def update_kernel(top, crows, pack_ref, c2th_ref, c2tl_ref, csth_ref, cstl_ref, after_ref, out_ref, xh_ref, xl_ref):
+    del after_ref
     reps = pack_ref.shape[0]
     width = out_ref.shape[1]
     per = crows * top
@@ -204,7 +209,54 @@
         out_ref[g * rows : (g + 1) * rows, :] += dot(th, bh) + dot(tl, bh) + dot(th, bl)
 
 
+def fetch(me_ref, acts_ref, s, start, cols, sem):
+    shard = acts_ref.shape[1] // 4
+    at = pl.multiple_of((me_ref[0] ^ s) * shard + start, LANES)
+    return pltpu.make_async_copy(acts_ref.at[:, pl.ds(at, cols.shape[1])], cols, sem)
+
+
+def cut_kernel(cuts, me_ref, acts_ref, after_ref, out_ref, sems):
+    del after_ref
+    shard = acts_ref.shape[1] // 4
+    copies, to = [], 0
+    for n, (s, start, size) in enumerate(cuts):
+        at = pl.multiple_of((me_ref[0] ^ s) * shard + start, LANES)
+        copies.append(
+            pltpu.make_async_copy(acts_ref.at[:, pl.ds(at, size)], out_ref.at[:, to : to + size], sems.at[n])
+        )
+        to += size
+    for copy in copies:
+        copy.start()
+    for copy in copies:
+        copy.wait()
+
+
+def sum_kernel(start, me_ref, acts_ref, g_ref, gp_ref, theirs_ref, after_ref, out_ref, cols, sem):
+    del after_ref
+    copy = fetch(me_ref, acts_ref, 2, start, cols, sem)
+    copy.start()
+    part = dot_tn(theirs_ref[...], gp_ref[...])
+    copy.wait()
+    out_ref[...] = (part + dot_tn(cols[...], g_ref[...])).astype(BF16)
+
+
+def hold_kernel(x_ref, after_ref, out_ref):
+    del x_ref, after_ref, out_ref
+
+
+def pack_kernel(own_ref, got1_ref, got2_ref, got3_ref, picks_ref, values_ref, pack_ref):
+    count = own_ref.shape[0]
+    values = own_ref[...] + got1_ref[...].astype(F32) + got2_ref[...].astype(F32) + got3_ref[...].astype(F32)
+    values_ref[...] = values
+    pack_ref[:count, :] = values.astype(BF16)
+    pack_ref[count:, :] = picks_ref[...]
+
+
 VMEM = functools.partial(pl.BlockSpec, memory_space=pltpu.VMEM)
+SMEM = pl.BlockSpec(memory_space=pltpu.SMEM)
+ANY = pl.BlockSpec(memory_space=pl.ANY)
+HBM = pl.BlockSpec(memory_space=pltpu.HBM)
+COST = pl.CostEstimate(flops=1, bytes_accessed=1, transcendentals=0)
 PARAMS = pltpu.CompilerParams(vmem_limit_bytes=32 * 1024 * 1024)
 
 
@@ -213,7 +265,7 @@
 
 
 def gather_replicas(x, replicas):
-    if replicas & (replicas - 1):
+    if GATHER or replicas & (replicas - 1):
         return lax.all_gather(x, "replica", axis=0, tiled=False)
     stack, bit = x[None], 1
     while bit < replicas:
@@ -228,8 +280,7 @@
     tokens = activations.shape[0]
     crows = shard // SIZE
     top = chosen_blocks.shape[2]
-    chunks = 4
-    rows = shard // chunks
+    lead = shard // 4
     spans = width // SIZE
     high, low = table_parts()
     c4h, c4l = (np.tile(t, (1, GROUP)) for t in (high, low))
@@ -238,45 +289,90 @@
     csth, cstl = (np.tile(t, (1, spans)) for t in (high, low))
     me = lax.axis_index("fsdp")
 
-    partner_grads = swap(output_grads, 1, "fsdp", fsdp)
+    mine = jnp.reshape(me, (1,))
     picks = jnp.pad(chosen_blocks[0].astype(BF16), ((0, 0), (0, LANES - top)))
-
-    def columns(s, start, size):
-        return lax.dynamic_slice(activations, (0, (me ^ s) * shard + start), (tokens, size))
-
-    partner_cols = [swap(columns(3, i * rows, rows), 1, "fsdp", fsdp) for i in range(chunks)]
-    picks2 = jnp.concatenate([picks, swap(picks, 1, "fsdp", fsdp)], axis=0)
-    picks4 = jnp.concatenate([picks2, swap(picks2, 2, "fsdp", fsdp)], axis=0)
-    partner_own = swap(columns(1, 0, shard), 1, "fsdp", fsdp)
-
-    vals = jax.ShapeDtypeStruct((crows * top, 2 * SIZE), BF16)
-    v0, v1, v2, v3 = pl.pallas_call(
+    count = crows * top
+
+    def swap_near(x, bit):
+        return swap(x, bit, "fsdp", fsdp)
+
+    def call(kernel, name, outs, args, specs, cols=0):
+        scratch = [pltpu.VMEM((tokens, cols), BF16), pltpu.SemaphoreType.DMA] if cols else []
+        return pl.pallas_call(
+            kernel,
+            out_shape=outs,
+            in_specs=[{"s": SMEM, "a": ANY, "h": HBM, "v": VMEM()}[c] for c in specs],
+            out_specs=jax.tree.map(lambda _: VMEM(), outs),
+            scratch_shapes=scratch,
+            compiler_params=PARAMS,
+            cost_estimate=COST,
+            name=name,
+        )(*args)
+
+    def cut(cuts, after):
+        return pl.pallas_call(
+            functools.partial(cut_kernel, cuts),
+            out_shape=bf(tokens, sum(size for _, _, size in cuts)),
+            in_specs=[SMEM, HBM, ANY],
+            out_specs=ANY,
+            scratch_shapes=[pltpu.SemaphoreType.DMA((len(cuts),))],
+            compiler_params=PARAMS,
+            cost_estimate=COST,
+            name="cut",
+        )(mine, activations, after)
+
+    def bf(*shape):
+        return jax.ShapeDtypeStruct(shape, BF16)
+
+    def f32(*shape):
+        return jax.ShapeDtypeStruct(shape, F32)
+
+    acts, grads = activations, output_grads
+    picks4 = jnp.concatenate([picks] + [swap_near(picks, s) for s in (1, 2, 3)], axis=0)
+    got_grads = swap_near(grads, 1)
+    cols_1 = swap_near(cut([(3, 0, lead)], picks), 1)
+
+    def sums(start, cols, after, name):
+        size = cols.shape[1]
+        kernel = functools.partial(sum_kernel, start)
+        return call(kernel, name, bf(size, width), (mine, acts, grads, got_grads, cols, after), "shvvva", size)
+
+    cut_2 = cut([(3, lead, shard - lead)], picks4)
+    cols_2 = swap_near(cut_2, 1)
+    sum_1 = sums(0, cols_1, cut_2, "sum_1")
+    got_1 = swap_near(sum_1, 2)
+    own, *parts = call(
         functools.partial(chosen_kernel, top),
-        out_shape=[jax.ShapeDtypeStruct((crows * top, 2 * SIZE), F32), vals, vals, vals],
-        in_specs=[pl.BlockSpec(memory_space=pltpu.SMEM)] + [VMEM()] * 8,
-        out_specs=[VMEM()] * 4,
+        "chosen",
+        [f32(count, 2 * SIZE)] + [bf(count, 2 * SIZE)] * 3,
+        (mine, picks4, acts, grads, old, c4h, c4l, csth, cstl, sum_1),
+        "s" + "v" * 8 + "a",
+    )
+    got = [swap_near(x, s + 1) for s, x in enumerate(parts)]
+    values, pack = call(
+        pack_kernel, "pack", [f32(count, 2 * SIZE), bf(count + crows, 2 * SIZE)], (own, *got, picks), "vvvvv"
+    )
+    sum_2 = sums(lead, cols_2, values, "sum_2")
+    sum_2 = pl.pallas_call(
+        hold_kernel,
+        out_shape=bf(*sum_2.shape),
+        in_specs=[ANY] * 2,
+        out_specs=ANY,
+        input_output_aliases={0: 0},
         compiler_params=PARAMS,
-        name="chosen",
-    )(jnp.reshape(me, (1,)), picks4, activations, output_grads, old, c4h, c4l, csth, cstl)
-    from_partner = swap(jnp.concatenate([v1, v3], axis=0), 1, "fsdp", fsdp)
-    own_pair = v0 + from_partner[: crows * top].astype(F32)
-    far_pair = (v2.astype(F32) + from_partner[crows * top :].astype(F32)).astype(BF16)
-    values = own_pair + swap(far_pair, 2, "fsdp", fsdp).astype(F32)
-    pack = jnp.concatenate([values.astype(BF16), picks], axis=0)
-
-    sums = []
-    for i in range(chunks):
-        s = dot_tn(columns(2, i * rows, rows), output_grads) + dot_tn(partner_cols[i], partner_grads)
-        sums.append(swap(s.astype(BF16), 2, "fsdp", fsdp))
-
-    base = pl.pallas_call(
+        cost_estimate=COST,
+        name="hold",
+    )(sum_2, got_1)
+    got_2 = swap_near(sum_2, 2)
+    cols_own = swap_near(cut([(1, 0, shard)], sum_2), 1)
+    base = call(
         functools.partial(base_kernel, top),
-        out_shape=jax.ShapeDtypeStruct((shard, width), F32),
-        in_specs=[VMEM()] * 11,
-        out_specs=VMEM(),
-        compiler_params=PARAMS,
-        name="base",
-    )(picks, values, old, columns(0, 0, shard), partner_own, output_grads, partner_grads, c4th, c4tl, csth, cstl)
+        "base",
+        f32(shard, width),
+        (mine, picks, values, old, acts, cols_own, grads, got_grads, c4th, c4tl, csth, cstl),
+        "svvvhvvvvvvv",
+        shard,
+    )
 
     everyone = gather_replicas(pack, replicas)
     step = 8 if replicas % 8 == 0 else 1
@@ -284,13 +380,14 @@
         functools.partial(update_kernel, top, crows),
         grid=(replicas // step,),
         out_shape=jax.ShapeDtypeStruct((shard, width), F32),
-        in_specs=[pl.BlockSpec((step, pack.shape[0], LANES), lambda i: (i, 0, 0))] + [VMEM()] * 4,
+        in_specs=[pl.BlockSpec((step, pack.shape[0], LANES), lambda i: (i, 0, 0))] + [VMEM()] * 4 + [ANY],
         out_specs=pl.BlockSpec((shard, width), lambda i: (0, 0)),
         scratch_shapes=[pltpu.VMEM((2, step, crows * top, width), BF16)] * 2,
         compiler_params=PARAMS,
+        cost_estimate=COST,
         name="update",
-    )(everyone, c2th, c2tl, csth, cstl)
-    moment_next = (base + jnp.concatenate(sums, axis=0).astype(F32)).astype(BF16)
+    )(everyone, c2th, c2tl, csth, cstl, values)
+    moment_next = (base + jnp.concatenate([got_1, got_2], axis=0).astype(F32)).astype(BF16)
     return moment_next[None], update
 
 

time: 103 us -> 71.2 us (0.69)
  waiting for transfers between devices: 48.7 us -> 20.4 us
  blocking collectives: 0 us -> 9.43 us
  matrix products: 6.43 us -> 0 us
  local copies, waits for them, and re-layouts: 5.35 us -> 1.76 us
  starting transfers between devices: 26.2 us -> 23 us
    ppermute x17 -> x12, waiting for transfers between devices: 48.7 us -> 20.4 us  [swap(): return lax.ppermute(x, axis, [(i, i ^ bit) for i in range(size)])]
    all_gather x0 -> x1, blocking collectives: none -> 9.43 us  [gather_replicas(): return lax.all_gather(x, 'replica', axis=0, tiled=False)]
    dot_general x8 -> x0, matrix products: 6.43 us -> none  [dot_tn(): lax.dot_general(a, b, (((0,), (0,)), ((), ())), preferred_element_type=F32)]
    dynamic_slice x2 -> x0, local copies, waits for them, and re-layouts: 3.96 us -> none  [columns(): lax.dynamic_slice(activations, (0, (me ^ s) * shard + start), (tokens, si...]
    ppermute x17 -> x12, starting transfers between devices: 26.2 us -> 23 us  [swap(): return lax.ppermute(x, axis, [(i, i ^ bit) for i in range(size)])]
    pallas_call x2 -> x9, Pallas kernels: 7.95 us -> 8.32 us  [the longest x5 8.18 us: call(): pl.pallas_call(kernel, out_shape=outs, in_specs=[{'s': SMEM, 'a': ANY, 'h...]
  transfers between devices with their start and end apart: 17 -> 12, of which waited for: 9 -> 6; matrix products, arithmetic and copies ran while one was open for 10% -> 1% of each run, Pallas kernels for 13% -> 19%
where the time goes in v2:
time: 71.2 us; the launch traced here: 71 us
  starting transfers between devices  23 us (32%)
  waiting for transfers between devices  20.4 us (29%)
  Pallas kernels  13.5 us (19%)
  blocking collectives  9.43 us (13%)
  other arithmetic  2.07 us (3%)
  local copies, waits for them, and re-layouts  1.76 us (2%)
  between operations  0.88 us (1%)
    ppermute x12, starting transfers between devices, swap(): return lax.ppermute(x, axis, [(i, i ^ bit) for i in range(size)])  23 us
    ppermute x12, waiting for transfers between devices, swap(): return lax.ppermute(x, axis, [(i, i ^ bit) for i in range(size)])  20.4 us
    all_gather x1, blocking collectives, gather_replicas(): return lax.all_gather(x, 'replica', axis=0, tiled=False)  9.43 us
    pallas_call x5, Pallas kernels, call(): pl.pallas_call(kernel, out_shape=outs, in_specs=[{'s': SMEM, 'a': ANY, 'h...  8.18 us
    pallas_call x1, Pallas kernels, body(): pl.pallas_call(functools.partial(update_kernel, top, crows), grid=(replic...  5.17 us
    unnamed x24, local copies, waits for them, and re-layouts  1.66 us
  transfers between devices with their start and end apart: 12, of which 6 were waited for; matrix products, arithmetic and copies ran while one was open for 1% of the time, Pallas kernels for 19%

profile of v2, /device:TPU:0, one launch (start us, length us, event | category | flops | bytes accessed | tf_op | source)
XLA Modules:
  0.0 71.0 jit_solution(14974532476374941130)
XLA Ops:
  0.6 3.1 %collective-permute-start.3 = (bf16[256,512]{1,0:T(8,128)(2,1)}, bf16[256,512]{1,0:T(8,128)(2,1)S(1)}, u32[]{:S(2)}, u32[]{:S(2)}) collective-permute-start(bf16[256,512]{1,0:T(8,128)(2,1)} %g_ref.7), channel_id=1, source_target_pairs={{0,1},{1,0},{2,3},{3,2},{4,5},{5,4},{6,7},{7,6},{8,9},{9,8},{10,11... | collective-permute-start | bytes 786440 | tf_op jit(solution)/shard_map/ppermute | solution.py:264
  3.7 0.7 convert_bitcast_fusion
  4.5 3.0 %collective-permute-start.1 = (bf16[16,128]{1,0:T(8,128)(2,1)S(1)}, bf16[16,128]{1,0:T(8,128)(2,1)S(1)}, u32[]{:S(2)}, u32[]{:S(2)}) collective-permute-start(bf16[16,128]{1,0:T(8,128)(2,1)S(1)} %pad.4.after_ref.picks_ref), channel_id=1, source_target_pairs={{0,2},{1,3},{2,0},{3,1},{4,6},{5,7},{6,4},{7,5},{8,10},{9,11},{10,... | collective-permute-start | bytes 12296 | tf_op jit(solution)/shard_map/ppermute | solution.py:264
  7.5 1.3 %collective-permute-start.2 = (bf16[16,128]{1,0:T(8,128)(2,1)S(1)}, bf16[16,128]{1,0:T(8,128)(2,1)S(1)}, u32[]{:S(2)}, u32[]{:S(2)}) collective-permute-start(bf16[16,128]{1,0:T(8,128)(2,1)S(1)} %pad.4.after_ref.picks_ref), channel_id=1, source_target_pairs={{0,3},{1,2},{2,1},{3,0},{4,7},{5,6},{6,5},{7,4},{8,11},{9,10},{10,... | collective-permute-start | bytes 12296 | tf_op jit(solution)/shard_map/ppermute | solution.py:264
  8.9 1.6 %copy-done = bf16[256,4096]{1,0:T(8,128)(2,1)S(1)} copy-done((bf16[256,4096]{1,0:T(8,128)(2,1)S(1)}, bf16[256,4096]{1,0:T(8,128)(2,1)}, u32[]{:S(2)}) %copy-start) | copy-done | bytes 2097176
  10.5 2.4 %collective-permute-done.2 = bf16[16,128]{1,0:T(8,128)(2,1)S(1)} collective-permute-done((bf16[16,128]{1,0:T(8,128)(2,1)S(1)}, bf16[16,128]{1,0:T(8,128)(2,1)S(1)}, u32[]{:S(2)}, u32[]{:S(2)}) %collective-permute-start.2) | collective-permute-done | bytes 4128 | tf_op jit(solution)/shard_map/ppermute | solution.py:264
  13.0 0.3 collective-permute-start.4
  13.3 1.8 %collective-permute-start.8 = (bf16[256,768]{1,0:T(8,128)(2,1)S(1)}, bf16[256,768]{1,0:T(8,128)(2,1)S(1)}, u32[]{:S(2)}, u32[]{:S(2)}) collective-permute-start(bf16[256,768]{1,0:T(8,128)(2,1)S(1)} %cut.4.after_ref), channel_id=1, source_target_pairs={{0,1},{1,0},{2,3},{3,2},{4,5},{5,4},{6,7},{7,6},{8,9},{9,8},{10,11... | collective-permute-start | bytes 1179656 | tf_op jit(solution)/shard_map/ppermute | solution.py:264
  15.2 7.0 %collective-permute-done.4.theirs_ref = bf16[256,256]{1,0:T(8,128)(2,1)S(1)} collective-permute-done((bf16[256,256]{1,0:T(8,128)(2,1)S(1)}, bf16[256,256]{1,0:T(8,128)(2,1)S(1)}, u32[]{:S(2)}, u32[]{:S(2)}) %collective-permute-start.4) | collective-permute-done | bytes 131104 | tf_op jit(solution)/shard_map/ppermute | solution.py:264
  22.2 0.4 sum_1.1.after_ref
  22.7 4.5 %chosen.1 = (f32[128,128]{1,0:T(8,128)S(1)}, bf16[128,128]{1,0:T(8,128)(2,1)S(1)}, bf16[128,128]{1,0:T(8,128)(2,1)S(1)}, bf16[128,128]{1,0:T(8,128)(2,1)S(1)}) custom-call(s32[1]{0:T(128)} %bitcast.me_ref, bf16[64,128]{1,0:T(8,128)(2,1)S(1)} %pad_maximum_fusion.after_ref.picks_ref, bf16[256,4096]{1,0:T(8,128)(2,1)S(1)} %copy-done, ...), custom_call_target="tpu_custom_call" | custom-call | flops 1 | bytes 1 | tf_op jit(solution)/shard_map/chosen/pallas_call | solution.py:301
  27.3 3.0 %collective-permute-start.6 = (bf16[128,128]{1,0:T(8,128)(2,1)S(1)}, bf16[128,128]{1,0:T(8,128)(2,1)S(1)}, u32[]{:S(2)}, u32[]{:S(2)}) collective-permute-start(bf16[128,128]{1,0:T(8,128)(2,1)S(1)} %get-tuple-element.10), channel_id=1, source_target_pairs={{0,2},{1,3},{2,0},{3,1},{4,6},{5,7},{6,4},{7,5},{8,10},{9,11},{10,... | collective-permute-start | bytes 98312 | tf_op jit(solution)/shard_map/ppermute | solution.py:264
  30.3 1.4 %collective-permute-start.7 = (bf16[128,128]{1,0:T(8,128)(2,1)S(1)}, bf16[128,128]{1,0:T(8,128)(2,1)S(1)}, u32[]{:S(2)}, u32[]{:S(2)}) collective-permute-start(bf16[128,128]{1,0:T(8,128)(2,1)S(1)} %get-tuple-element.11), channel_id=1, source_target_pairs={{0,3},{1,2},{2,1},{3,0},{4,7},{5,6},{6,5},{7,4},{8,11},{9,10},{10,... | collective-permute-start | bytes 98312 | tf_op jit(solution)/shard_map/ppermute | solution.py:264
  31.7 3.6 %collective-permute-done.6.got2_ref = bf16[128,128]{1,0:T(8,128)(2,1)S(1)} collective-permute-done((bf16[128,128]{1,0:T(8,128)(2,1)S(1)}, bf16[128,128]{1,0:T(8,128)(2,1)S(1)}, u32[]{:S(2)}, u32[]{:S(2)}) %collective-permute-start.6) | collective-permute-done | bytes 32800 | tf_op jit(solution)/shard_map/ppermute | solution.py:264
  35.3 1.1 %collective-permute-done.7.got3_ref = bf16[128,128]{1,0:T(8,128)(2,1)S(1)} collective-permute-done((bf16[128,128]{1,0:T(8,128)(2,1)S(1)}, bf16[128,128]{1,0:T(8,128)(2,1)S(1)}, u32[]{:S(2)}, u32[]{:S(2)}) %collective-permute-start.7) | collective-permute-done | bytes 32800 | tf_op jit(solution)/shard_map/ppermute | solution.py:264
  36.4 0.7 sum_2.1.x_ref
  37.1 7.7 %collective-permute-start.11 = (bf16[768,512]{1,0:T(8,128)(2,1)S(1)}, bf16[768,512]{1,0:T(8,128)(2,1)S(1)}, u32[]{:S(2)}, u32[]{:S(2)}) collective-permute-start(bf16[768,512]{1,0:T(8,128)(2,1)S(1)} %hold.1.after_ref), channel_id=1, source_target_pairs={{0,2},{1,3},{2,0},{3,1},{4,6},{5,7},{6,4},{7,5},{8,10},{9,11},{10,... | collective-permute-start | bytes 2359304 | tf_op jit(solution)/shard_map/ppermute | solution.py:264
  44.9 1.2 %collective-permute-start.10 = (bf16[256,1024]{1,0:T(8,128)(2,1)S(1)}, bf16[256,1024]{1,0:T(8,128)(2,1)S(1)}, u32[]{:S(2)}, u32[]{:S(2)}) collective-permute-start(bf16[256,1024]{1,0:T(8,128)(2,1)S(1)} %cut.5), channel_id=1, source_target_pairs={{0,1},{1,0},{2,3},{3,2},{4,5},{5,4},{6,7},{7,6},{8,9},{9,8},{10,11... | collective-permute-start | bytes 1572872 | tf_op jit(solution)/shard_map/ppermute | solution.py:264
  46.2 9.4 %all-gather = bf16[1152,128]{1,0:T(8,128)(2,1)S(1)} all-gather(bf16[144,128]{1,0:T(8,128)(2,1)S(1)} %get-tuple-element.13), channel_id=2, replica_groups=mesh['replica'=8,'fsdp'=4] {'replica'}, dimensions={0}, use_global_device_ids=true | all-gather | bytes 331776 | tf_op jit(solution)/shard_map/all_gather | solution.py:269
  55.6 5.2 %update.1 = f32[1024,512]{1,0:T(8,128)} custom-call(bf16[8,144,128]{2,1,0:T(8,128)(2,1)S(1)} %bitcast.9, bf16[128,64]{1,0:T(8,128)(2,1)S(1)} %copy-done.10, bf16[128,64]{1,0:T(8,128)(2,1)S(1)} %copy-done.11, bf16[64,512]{1,0:T(8,128)(2,1)S(1)} %copy-done.4, bf16[64,512]{1,0:T(8,128)(2,1)S(1)} %copy-done.5, f32[128,128]{1,0:T(8,128)S(1)} %get-tuple-element.12.after_ref.v_ref), custom_call_target="tpu_custom_call" | custom-call | flops 1 | bytes 1 | tf_op jit(solution)/shard_map/update/pallas_call | solution.py:379
  60.8 0.3 collective-permute-done.10.ao_ref
  61.1 2.6 %base.1 = f32[1024,512]{1,0:T(8,128)S(1)} custom-call(s32[1]{0:T(128)} %bitcast.me_ref, bf16[16,128]{1,0:T(8,128)(2,1)S(1)} %pad.4.after_ref.picks_ref, f32[128,128]{1,0:T(8,128)S(1)} %get-tuple-element.12.after_ref.v_ref, bf16[1024,512]{1,0:T(8,128)(2,1)S(1)} %bitcast.8, bf16[256,4096]{1,0:T(8,128)(2,1)S(1)} %copy-done.1, ...), custom_call_target="tpu_custom_call" | custom-call | flops 1 | bytes 1 | tf_op jit(solution)/shard_map/base/pallas_call | solution.py:301
  63.7 6.0 %collective-permute-done.11 = bf16[768,512]{1,0:T(8,128)(2,1)S(1)} collective-permute-done((bf16[768,512]{1,0:T(8,128)(2,1)S(1)}, bf16[768,512]{1,0:T(8,128)(2,1)S(1)}, u32[]{:S(2)}, u32[]{:S(2)}) %collective-permute-start.11) | collective-permute-done | bytes 786464 | tf_op jit(solution)/shard_map/ppermute | solution.py:264
  69.7 1.4 %fusion = bf16[1,1024,512]{2,1,0:T(8,128)(2,1)} fusion(f32[1024,512]{1,0:T(8,128)S(1)} %base.1, bf16[768,512]{1,0:T(8,128)(2,1)S(1)} %collective-permute-done.11, bf16[256,512]{1,0:T(8,128)(2,1)S(1)} %collective-permute-done.9.after_ref), kind=kLoop, calls=%fused_computation.1 | loop fusion | flops 3145728 | bytes 4194304 | tf_op jit(solution)/shard_map/broadcast_in_dim | solution.py:391
  (40 shorter events, 0.5 us)
Async XLA Ops:
  0.6 21.6 %collective-permute-start.3 = (bf16[256,512]{1,0:T(8,128)(2,1)}, bf16[256,512]{1,0:T(8,128)(2,1)S(1)}, u32[]{:S(2)}, u32[]{:S(2)}) collective-permute-start(bf16[256,512]{1,0:T(8,128)(2,1)} %g_ref.7), channel_id=1, source_target_pairs={{0,1},{1,0},{2,3},{3,2},{4,5},{5,4},{6,7},{7,6},{8,9},{9,8},{10,11... | collective-permute-start | bytes 786440 | tf_op jit(solution)/shard_map/ppermute | solution.py:264
  4.5 6.0 %collective-permute-start = (bf16[16,128]{1,0:T(8,128)(2,1)S(1)}, bf16[16,128]{1,0:T(8,128)(2,1)S(1)}, u32[]{:S(2)}, u32[]{:S(2)}) collective-permute-start(bf16[16,128]{1,0:T(8,128)(2,1)S(1)} %pad.4.after_ref.picks_ref), channel_id=1, source_target_pairs={{0,1},{1,0},{2,3},{3,2},{4,5},{5,4},{6,7},{7,6},{8,9},{9,8},{10,11... | collective-permute-start | bytes 12296 | tf_op jit(solution)/shard_map/ppermute | solution.py:264
  4.5 6.0 %collective-permute-start.1 = (bf16[16,128]{1,0:T(8,128)(2,1)S(1)}, bf16[16,128]{1,0:T(8,128)(2,1)S(1)}, u32[]{:S(2)}, u32[]{:S(2)}) collective-permute-start(bf16[16,128]{1,0:T(8,128)(2,1)S(1)} %pad.4.after_ref.picks_ref), channel_id=1, source_target_pairs={{0,2},{1,3},{2,0},{3,1},{4,6},{5,7},{6,4},{7,5},{8,10},{9,11},{10,... | collective-permute-start | bytes 12296 | tf_op jit(solution)/shard_map/ppermute | solution.py:264
  7.5 5.4 %collective-permute-start.2 = (bf16[16,128]{1,0:T(8,128)(2,1)S(1)}, bf16[16,128]{1,0:T(8,128)(2,1)S(1)}, u32[]{:S(2)}, u32[]{:S(2)}) collective-permute-start(bf16[16,128]{1,0:T(8,128)(2,1)S(1)} %pad.4.after_ref.picks_ref), channel_id=1, source_target_pairs={{0,3},{1,2},{2,1},{3,0},{4,7},{5,6},{6,5},{7,4},{8,11},{9,10},{10,... | collective-permute-start | bytes 12296 | tf_op jit(solution)/shard_map/ppermute | solution.py:264
  8.9 1.6 %copy-start = (bf16[256,4096]{1,0:T(8,128)(2,1)S(1)}, bf16[256,4096]{1,0:T(8,128)(2,1)}, u32[]{:S(2)}) copy-start(bf16[256,4096]{1,0:T(8,128)(2,1)} %acts_ref.13) | copy-start | bytes 6291460
  10.5 11.7 %copy-start.2 = (bf16[256,512]{1,0:T(8,128)(2,1)S(1)}, bf16[256,512]{1,0:T(8,128)(2,1)}, u32[]{:S(2)}) copy-start(bf16[256,512]{1,0:T(8,128)(2,1)} %g_ref.7) | copy-start | bytes 786436
  13.0 9.2 %collective-permute-start.4 = (bf16[256,256]{1,0:T(8,128)(2,1)S(1)}, bf16[256,256]{1,0:T(8,128)(2,1)S(1)}, u32[]{:S(2)}, u32[]{:S(2)}) collective-permute-start(bf16[256,256]{1,0:T(8,128)(2,1)S(1)} %cut.3), channel_id=1, source_target_pairs={{0,1},{1,0},{2,3},{3,2},{4,5},{5,4},{6,7},{7,6},{8,9},{9,8},{10,11... | collective-permute-start | bytes 393224 | tf_op jit(solution)/shard_map/ppermute | solution.py:264
  13.3 9.4 %copy-start.3 = (bf16[1,1024,512]{2,1,0:T(8,128)(2,1)S(1)}, bf16[1,1024,512]{2,1,0:T(8,128)(2,1)}, u32[]{:S(2)}) copy-start(bf16[1,1024,512]{2,1,0:T(8,128)(2,1)} %param.14) | copy-start | bytes 3145732
  13.3 9.4 %copy-start.4 = (bf16[64,512]{1,0:T(8,128)(2,1)S(1)}, bf16[64,512]{1,0:T(8,128)(2,1)}, u32[]{:S(2)}) copy-start(bf16[64,512]{1,0:T(8,128)(2,1)} %constant.25.clone.csth_ref) | copy-start | bytes 196612
  13.3 9.4 %copy-start.5 = (bf16[64,512]{1,0:T(8,128)(2,1)S(1)}, bf16[64,512]{1,0:T(8,128)(2,1)}, u32[]{:S(2)}) copy-start(bf16[64,512]{1,0:T(8,128)(2,1)} %constant.26.clone.cstl_ref) | copy-start | bytes 196612
  13.3 9.4 %copy-start.8 = (bf16[64,256]{1,0:T(8,128)(2,1)S(1)}, bf16[64,256]{1,0:T(8,128)(2,1)}, u32[]{:S(2)}) copy-start(bf16[64,256]{1,0:T(8,128)(2,1)} %constant.23.clone.c4h_ref) | copy-start | bytes 98308
  13.3 9.4 %copy-start.9 = (bf16[64,256]{1,0:T(8,128)(2,1)S(1)}, bf16[64,256]{1,0:T(8,128)(2,1)}, u32[]{:S(2)}) copy-start(bf16[64,256]{1,0:T(8,128)(2,1)} %constant.24.clone.c4l_ref) | copy-start | bytes 98308
  13.3 23.0 %collective-permute-start.8 = (bf16[256,768]{1,0:T(8,128)(2,1)S(1)}, bf16[256,768]{1,0:T(8,128)(2,1)S(1)}, u32[]{:S(2)}, u32[]{:S(2)}) collective-permute-start(bf16[256,768]{1,0:T(8,128)(2,1)S(1)} %cut.4.after_ref), channel_id=1, source_target_pairs={{0,1},{1,0},{2,3},{3,2},{4,5},{5,4},{6,7},{7,6},{8,9},{9,8},{10,11... | collective-permute-start | bytes 1179656 | tf_op jit(solution)/shard_map/ppermute | solution.py:264
  22.6 13.8 %copy-start.1 = (bf16[256,4096]{1,0:T(8,128)(2,1)S(1)}, bf16[256,4096]{1,0:T(8,128)(2,1)}, u32[]{:S(2)}) copy-start(bf16[256,4096]{1,0:T(8,128)(2,1)} %acts_ref.13) | copy-start | bytes 6291460
  22.6 14.5 %collective-permute-start.9 = (bf16[256,512]{1,0:T(8,128)(2,1)S(1)}, bf16[256,512]{1,0:T(8,128)(2,1)S(1)}, u32[]{:S(2)}, u32[]{:S(2)}) collective-permute-start(bf16[256,512]{1,0:T(8,128)(2,1)S(1)} %sum_1.1.after_ref), channel_id=1, source_target_pairs={{0,2},{1,3},{2,0},{3,1},{4,6},{5,7},{6,4},{7,5},{8,10},{9,11},{10,... | collective-permute-start | bytes 786440 | tf_op jit(solution)/shard_map/ppermute | solution.py:264
  27.2 4.5 %collective-permute-start.5 = (bf16[128,128]{1,0:T(8,128)(2,1)S(1)}, bf16[128,128]{1,0:T(8,128)(2,1)S(1)}, u32[]{:S(2)}, u32[]{:S(2)}) collective-permute-start(bf16[128,128]{1,0:T(8,128)(2,1)S(1)} %get-tuple-element.9), channel_id=1, source_target_pairs={{0,1},{1,0},{2,3},{3,2},{4,5},{5,4},{6,7},{7,6},{8,9},{9,8},{10,11... | collective-permute-start | bytes 98312 | tf_op jit(solution)/shard_map/ppermute | solution.py:264
  27.3 8.0 %collective-permute-start.6 = (bf16[128,128]{1,0:T(8,128)(2,1)S(1)}, bf16[128,128]{1,0:T(8,128)(2,1)S(1)}, u32[]{:S(2)}, u32[]{:S(2)}) collective-permute-start(bf16[128,128]{1,0:T(8,128)(2,1)S(1)} %get-tuple-element.10), channel_id=1, source_target_pairs={{0,2},{1,3},{2,0},{3,1},{4,6},{5,7},{6,4},{7,5},{8,10},{9,11},{10,... | collective-permute-start | bytes 98312 | tf_op jit(solution)/shard_map/ppermute | solution.py:264
  30.3 6.1 %collective-permute-start.7 = (bf16[128,128]{1,0:T(8,128)(2,1)S(1)}, bf16[128,128]{1,0:T(8,128)(2,1)S(1)}, u32[]{:S(2)}, u32[]{:S(2)}) collective-permute-start(bf16[128,128]{1,0:T(8,128)(2,1)S(1)} %get-tuple-element.11), channel_id=1, source_target_pairs={{0,3},{1,2},{2,1},{3,0},{4,7},{5,6},{6,5},{7,4},{8,11},{9,10},{10,... | collective-permute-start | bytes 98312 | tf_op jit(solution)/shard_map/ppermute | solution.py:264
  37.1 18.5 %copy-start.10 = (bf16[128,64]{1,0:T(8,128)(2,1)S(1)}, bf16[128,64]{1,0:T(8,128)(2,1)}, u32[]{:S(2)}) copy-start(bf16[128,64]{1,0:T(8,128)(2,1)} %constant.29.clone.c2th_ref) | copy-start | bytes 49156
  37.1 18.5 %copy-start.11 = (bf16[128,64]{1,0:T(8,128)(2,1)S(1)}, bf16[128,64]{1,0:T(8,128)(2,1)}, u32[]{:S(2)}) copy-start(bf16[128,64]{1,0:T(8,128)(2,1)} %constant.30.clone.c2tl_ref) | copy-start | bytes 49156
  37.1 32.5 %collective-permute-start.11 = (bf16[768,512]{1,0:T(8,128)(2,1)S(1)}, bf16[768,512]{1,0:T(8,128)(2,1)S(1)}, u32[]{:S(2)}, u32[]{:S(2)}) collective-permute-start(bf16[768,512]{1,0:T(8,128)(2,1)S(1)} %hold.1.after_ref), channel_id=1, source_target_pairs={{0,2},{1,3},{2,0},{3,1},{4,6},{5,7},{6,4},{7,5},{8,10},{9,11},{10,... | collective-permute-start | bytes 2359304 | tf_op jit(solution)/shard_map/ppermute | solution.py:264
  44.9 16.2 %copy-start.6 = (bf16[256,64]{1,0:T(8,128)(2,1)S(1)}, bf16[256,64]{1,0:T(8,128)(2,1)}, u32[]{:S(2)}) copy-start(bf16[256,64]{1,0:T(8,128)(2,1)} %constant.27.clone.c4th_ref) | copy-start | bytes 98308
  44.9 16.1 %copy-start.7 = (bf16[256,64]{1,0:T(8,128)(2,1)S(1)}, bf16[256,64]{1,0:T(8,128)(2,1)}, u32[]{:S(2)}) copy-start(bf16[256,64]{1,0:T(8,128)(2,1)} %constant.28.clone.c4tl_ref) | copy-start | bytes 98308
  44.9 16.1 %collective-permute-start.10 = (bf16[256,1024]{1,0:T(8,128)(2,1)S(1)}, bf16[256,1024]{1,0:T(8,128)(2,1)S(1)}, u32[]{:S(2)}, u32[]{:S(2)}) collective-permute-start(bf16[256,1024]{1,0:T(8,128)(2,1)S(1)} %cut.5), channel_id=1, source_target_pairs={{0,1},{1,0},{2,3},{3,2},{4,5},{5,4},{6,7},{7,6},{8,9},{9,8},{10,11... | collective-permute-start | bytes 1572872 | tf_op jit(solution)/shard_map/ppermute | solution.py:264

commit v3 on v2

--- a/solution.py
+++ b/solution.py
@@ -215,8 +215,8 @@
     return pltpu.make_async_copy(acts_ref.at[:, pl.ds(at, cols.shape[1])], cols, sem)
 
 
-def cut_kernel(cuts, me_ref, acts_ref, after_ref, out_ref, sems):
-    del after_ref
+def cut_kernel(cuts, me_ref, acts_ref, after_ref, after2_ref, after3_ref, out_ref, sems):
+    del after_ref, after2_ref, after3_ref
     shard = acts_ref.shape[1] // 4
     copies, to = [], 0
     for n, (s, start, size) in enumerate(cuts):
@@ -240,11 +240,24 @@
     out_ref[...] = (part + dot_tn(cols[...], g_ref[...])).astype(BF16)
 
 
-def hold_kernel(x_ref, after_ref, out_ref):
-    del x_ref, after_ref, out_ref
-
-
-def pack_kernel(own_ref, got1_ref, got2_ref, got3_ref, picks_ref, values_ref, pack_ref):
+def hold_kernel(x_ref, after_ref, after2_ref, out_ref):
+    del x_ref, after_ref, after2_ref, out_ref
+
+
+def final_kernel(base_ref, got1_ref, got2_ref, out_ref, rows, sems):
+    size = rows.shape[1]
+    copies = []
+    for n in range(rows.shape[0]):
+        got = got1_ref[...] if n == 0 else got2_ref[(n - 1) * size : n * size, :]
+        rows[n] = (base_ref[n * size : (n + 1) * size, :] + got.astype(F32)).astype(BF16)
+        copies.append(pltpu.make_async_copy(rows.at[n], out_ref.at[n * size : (n + 1) * size], sems.at[n]))
+        copies[-1].start()
+    for copy in copies:
+        copy.wait()
+
+
+def pack_kernel(own_ref, got1_ref, got2_ref, got3_ref, picks_ref, after_ref, values_ref, pack_ref):
+    del after_ref
     count = own_ref.shape[0]
     values = own_ref[...] + got1_ref[...].astype(F32) + got2_ref[...].astype(F32) + got3_ref[...].astype(F32)
     values_ref[...] = values
@@ -309,17 +322,17 @@
             name=name,
         )(*args)
 
-    def cut(cuts, after):
+    def cut(cuts, after, after2, after3):
         return pl.pallas_call(
             functools.partial(cut_kernel, cuts),
             out_shape=bf(tokens, sum(size for _, _, size in cuts)),
-            in_specs=[SMEM, HBM, ANY],
+            in_specs=[SMEM, HBM, ANY, ANY, ANY],
             out_specs=ANY,
             scratch_shapes=[pltpu.SemaphoreType.DMA((len(cuts),))],
             compiler_params=PARAMS,
             cost_estimate=COST,
             name="cut",
-        )(mine, activations, after)
+        )(mine, activations, after, after2, after3)
 
     def bf(*shape):
         return jax.ShapeDtypeStruct(shape, BF16)
@@ -330,16 +343,16 @@
     acts, grads = activations, output_grads
     picks4 = jnp.concatenate([picks] + [swap_near(picks, s) for s in (1, 2, 3)], axis=0)
     got_grads = swap_near(grads, 1)
-    cols_1 = swap_near(cut([(3, 0, lead)], picks), 1)
+    cols_1 = swap_near(cut([(3, 0, lead)], picks, picks, picks), 1)
 
     def sums(start, cols, after, name):
         size = cols.shape[1]
         kernel = functools.partial(sum_kernel, start)
         return call(kernel, name, bf(size, width), (mine, acts, grads, got_grads, cols, after), "shvvva", size)
 
-    cut_2 = cut([(3, lead, shard - lead)], picks4)
+    cut_2 = cut([(3, lead, shard - lead)], picks4, cols_1, got_grads)
     cols_2 = swap_near(cut_2, 1)
-    sum_1 = sums(0, cols_1, cut_2, "sum_1")
+    sum_1 = sums(0, cols_1, cols_1, "sum_1")
     got_1 = swap_near(sum_1, 2)
     own, *parts = call(
         functools.partial(chosen_kernel, top),
@@ -349,22 +362,22 @@
         "s" + "v" * 8 + "a",
     )
     got = [swap_near(x, s + 1) for s, x in enumerate(parts)]
+    sum_2 = sums(lead, cols_2, parts[0], "sum_2")
     values, pack = call(
-        pack_kernel, "pack", [f32(count, 2 * SIZE), bf(count + crows, 2 * SIZE)], (own, *got, picks), "vvvvv"
+        pack_kernel, "pack", [f32(count, 2 * SIZE), bf(count + crows, 2 * SIZE)], (own, *got, picks, sum_2), "vvvvva"
     )
-    sum_2 = sums(lead, cols_2, values, "sum_2")
     sum_2 = pl.pallas_call(
         hold_kernel,
         out_shape=bf(*sum_2.shape),
-        in_specs=[ANY] * 2,
+        in_specs=[ANY] * 3,
         out_specs=ANY,
         input_output_aliases={0: 0},
         compiler_params=PARAMS,
         cost_estimate=COST,
         name="hold",
-    )(sum_2, got_1)
+    )(sum_2, got_1, values)
     got_2 = swap_near(sum_2, 2)
-    cols_own = swap_near(cut([(1, 0, shard)], sum_2), 1)
+    cols_own = swap_near(cut([(1, 0, shard)], sum_2, sum_2, sum_2), 1)
     base = call(
         functools.partial(base_kernel, top),
         "base",
@@ -387,7 +400,16 @@
         cost_estimate=COST,
         name="update",
     )(everyone, c2th, c2tl, csth, cstl, values)
-    moment_next = (base + jnp.concatenate([got_1, got_2], axis=0).astype(F32)).astype(BF16)
+    moment_next = pl.pallas_call(
+        final_kernel,
+        out_shape=bf(shard, width),
+        in_specs=[VMEM()] * 3,
+        out_specs=HBM,
+        scratch_shapes=[pltpu.VMEM((shard // lead, lead, width), BF16), pltpu.SemaphoreType.DMA((shard // lead,))],
+        compiler_params=PARAMS,
+        cost_estimate=COST,
+        name="final",
+    )(base, got_1, got_2)
     return moment_next[None], update
 
 

time: 71.2 us -> 69.2 us (0.972)
  starting transfers between devices: 23 us -> 16.2 us
  waiting for transfers between devices: 20.4 us -> 25.1 us
  other arithmetic: 2.07 us -> 0.69 us
  Pallas kernels: 13.5 us -> 14.6 us
    ppermute x12, starting transfers between devices: 23 us -> 16.2 us  [swap(): return lax.ppermute(x, axis, [(i, i ^ bit) for i in range(size)])]
    ppermute x12, waiting for transfers between devices: 20.4 us -> 25.1 us  [swap(): return lax.ppermute(x, axis, [(i, i ^ bit) for i in range(size)])]
    broadcast_in_dim x1 -> x0, other arithmetic: 1.38 us -> none  [body(): return (moment_next[None], update)]
    pallas_call x0 -> x1, Pallas kernels: none -> 1.07 us  [body(): pl.pallas_call(final_kernel, out_shape=bf(shard, width), in_specs=[VMEM()...]
where the time goes in v3:
time: 69.2 us; the launch traced here: 68.9 us
  waiting for transfers between devices  25.1 us (36%)
  starting transfers between devices  16.2 us (23%)
  Pallas kernels  14.6 us (21%)
  blocking collectives  9.44 us (14%)
  local copies, waits for them, and re-layouts  2.17 us (3%)
  between operations  0.84 us (1%)
    ppermute x12, waiting for transfers between devices, swap(): return lax.ppermute(x, axis, [(i, i ^ bit) for i in range(size)])  25.1 us
    ppermute x12, starting transfers between devices, swap(): return lax.ppermute(x, axis, [(i, i ^ bit) for i in range(size)])  16.2 us
    all_gather x1, blocking collectives, gather_replicas(): return lax.all_gather(x, 'replica', axis=0, tiled=False)  9.44 us
    pallas_call x5, Pallas kernels, call(): pl.pallas_call(kernel, out_shape=outs, in_specs=[{'s': SMEM, 'a': ANY, 'h...  8.18 us
    pallas_call x1, Pallas kernels, body(): pl.pallas_call(functools.partial(update_kernel, top, crows), grid=(replic...  5.16 us
    unnamed x24, local copies, waits for them, and re-layouts  2.08 us
  transfers between devices with their start and end apart: 12, of which 6 were waited for; matrix products, arithmetic and copies ran while one was open for 1% of the time, Pallas kernels for 19%

profile of v3, /device:TPU:0, one launch (start us, length us, event | category | flops | bytes accessed | tf_op | source)
XLA Modules:
  0.0 68.9 jit_solution(7577619632570099652)
XLA Ops:
  0.6 3.1 %collective-permute-start.3 = (bf16[256,512]{1,0:T(8,128)(2,1)}, bf16[256,512]{1,0:T(8,128)(2,1)S(1)}, u32[]{:S(2)}, u32[]{:S(2)}) collective-permute-start(bf16[256,512]{1,0:T(8,128)(2,1)} %g_ref.7), channel_id=1, source_target_pairs={{0,1},{1,0},{2,3},{3,2},{4,5},{5,4},{6,7},{7,6},{8,9},{9,8},{10,11... | collective-permute-start | bytes 786440 | tf_op jit(solution)/shard_map/ppermute | solution.py:277
  3.7 0.7 %convert_bitcast_fusion = bf16[16,8]{0,1:T(8,128)(2,1)S(1)} fusion(s32[1,16,8]{1,2,0:T(8,128)} %param.15), kind=kLoop, calls=%fused_computation.1 | loop fusion | flops 128 | bytes 768 | tf_op jit(solution)/shard_map/convert_element_type | solution.py:306
  4.5 1.6 %copy-done = bf16[256,4096]{1,0:T(8,128)(2,1)S(1)} copy-done((bf16[256,4096]{1,0:T(8,128)(2,1)S(1)}, bf16[256,4096]{1,0:T(8,128)(2,1)}, u32[]{:S(2)}) %copy-start) | copy-done | bytes 2097176
  6.2 2.0 %collective-permute-start = (bf16[16,128]{1,0:T(8,128)(2,1)S(1)}, bf16[16,128]{1,0:T(8,128)(2,1)S(1)}, u32[]{:S(2)}, u32[]{:S(2)}) collective-permute-start(bf16[16,128]{1,0:T(8,128)(2,1)S(1)} %pad.4.after_ref.after2_ref.after3_ref.picks_ref), channel_id=1, source_target_pairs={{0,1},{1,0},{2,3},{3,2},{4,5},{5,4},{6,7},{7,6},{8,9},{9,8},{10,11... | collective-permute-start | bytes 12296 | tf_op jit(solution)/shard_map/ppermute | solution.py:277
  8.2 2.6 %collective-permute-start.1 = (bf16[16,128]{1,0:T(8,128)(2,1)S(1)}, bf16[16,128]{1,0:T(8,128)(2,1)S(1)}, u32[]{:S(2)}, u32[]{:S(2)}) collective-permute-start(bf16[16,128]{1,0:T(8,128)(2,1)S(1)} %pad.4.after_ref.after2_ref.after3_ref.picks_ref), channel_id=1, source_target_pairs={{0,2},{1,3},{2,0},{3,1},{4,6},{5,7},{6,4},{7,5},{8,10},{9,11},{10,... | collective-permute-start | bytes 12296 | tf_op jit(solution)/shard_map/ppermute | solution.py:277
  10.8 2.4 %collective-permute-done = bf16[16,128]{1,0:T(8,128)(2,1)S(1)} collective-permute-done((bf16[16,128]{1,0:T(8,128)(2,1)S(1)}, bf16[16,128]{1,0:T(8,128)(2,1)S(1)}, u32[]{:S(2)}, u32[]{:S(2)}) %collective-permute-start) | collective-permute-done | bytes 4128 | tf_op jit(solution)/shard_map/ppermute | solution.py:277
  13.2 3.0 %collective-permute-done.2 = bf16[16,128]{1,0:T(8,128)(2,1)S(1)} collective-permute-done((bf16[16,128]{1,0:T(8,128)(2,1)S(1)}, bf16[16,128]{1,0:T(8,128)(2,1)S(1)}, u32[]{:S(2)}, u32[]{:S(2)}) %collective-permute-start.2) | collective-permute-done | bytes 4128 | tf_op jit(solution)/shard_map/ppermute | solution.py:277
  16.5 0.4 sum_1.1.after_ref
  16.8 1.5 %collective-permute-start.9 = (bf16[256,512]{1,0:T(8,128)(2,1)S(1)}, bf16[256,512]{1,0:T(8,128)(2,1)S(1)}, u32[]{:S(2)}, u32[]{:S(2)}) collective-permute-start(bf16[256,512]{1,0:T(8,128)(2,1)S(1)} %sum_1.1.after_ref), channel_id=1, source_target_pairs={{0,2},{1,3},{2,0},{3,1},{4,6},{5,7},{6,4},{7,5},{8,10},{9,11},{10,... | collective-permute-start | bytes 786440 | tf_op jit(solution)/shard_map/ppermute | solution.py:277
  18.3 4.5 %chosen.1 = (f32[128,128]{1,0:T(8,128)S(1)}, bf16[128,128]{1,0:T(8,128)(2,1)S(1)}, bf16[128,128]{1,0:T(8,128)(2,1)S(1)}, bf16[128,128]{1,0:T(8,128)(2,1)S(1)}) custom-call(s32[1]{0:T(128)} %bitcast.me_ref, bf16[64,128]{1,0:T(8,128)(2,1)S(1)} %pad_maximum_fusion.picks_ref.after_ref, bf16[256,4096]{1,0:T(8,128)(2,1)S(1)} %copy-done, ...), custom_call_target="tpu_custom_call" | custom-call | flops 1 | bytes 1 | tf_op jit(solution)/shard_map/chosen/pallas_call | solution.py:314
  22.8 0.7 collective-permute-start.5
  23.5 2.9 %collective-permute-start.6 = (bf16[128,128]{1,0:T(8,128)(2,1)S(1)}, bf16[128,128]{1,0:T(8,128)(2,1)S(1)}, u32[]{:S(2)}, u32[]{:S(2)}) collective-permute-start(bf16[128,128]{1,0:T(8,128)(2,1)S(1)} %get-tuple-element.10), channel_id=1, source_target_pairs={{0,2},{1,3},{2,0},{3,1},{4,6},{5,7},{6,4},{7,5},{8,10},{9,11},{10,... | collective-permute-start | bytes 98312 | tf_op jit(solution)/shard_map/ppermute | solution.py:277
  26.4 0.9 %collective-permute-start.7 = (bf16[128,128]{1,0:T(8,128)(2,1)S(1)}, bf16[128,128]{1,0:T(8,128)(2,1)S(1)}, u32[]{:S(2)}, u32[]{:S(2)}) collective-permute-start(bf16[128,128]{1,0:T(8,128)(2,1)S(1)} %get-tuple-element.11), channel_id=1, source_target_pairs={{0,3},{1,2},{2,1},{3,0},{4,7},{5,6},{6,5},{7,4},{8,11},{9,10},{10,... | collective-permute-start | bytes 98312 | tf_op jit(solution)/shard_map/ppermute | solution.py:277
  27.3 5.1 %collective-permute-done.8.theirs_ref = bf16[256,768]{1,0:T(8,128)(2,1)S(1)} collective-permute-done((bf16[256,768]{1,0:T(8,128)(2,1)S(1)}, bf16[256,768]{1,0:T(8,128)(2,1)S(1)}, u32[]{:S(2)}, u32[]{:S(2)}) %collective-permute-start.8) | collective-permute-done | bytes 393248 | tf_op jit(solution)/shard_map/ppermute | solution.py:277
  32.4 0.7 sum_2.1.after_ref.x_ref
  33.3 1.0 %collective-permute-start.11 = (bf16[768,512]{1,0:T(8,128)(2,1)S(1)}, bf16[768,512]{1,0:T(8,128)(2,1)S(1)}, u32[]{:S(2)}, u32[]{:S(2)}) collective-permute-start(bf16[768,512]{1,0:T(8,128)(2,1)S(1)} %hold.1.after_ref.after2_ref.after3_ref), channel_id=1, source_target_pairs={{0,2},{1,3},{2,0},{3,1},{4,6},{5,7},{6,4},{7,5},{8,10},{9,11},{10,... | collective-permute-start | bytes 2359304 | tf_op jit(solution)/shard_map/ppermute | solution.py:277
  34.3 0.4 copy-done.1
  34.8 1.5 %collective-permute-start.10 = (bf16[256,1024]{1,0:T(8,128)(2,1)S(1)}, bf16[256,1024]{1,0:T(8,128)(2,1)S(1)}, u32[]{:S(2)}, u32[]{:S(2)}) collective-permute-start(bf16[256,1024]{1,0:T(8,128)(2,1)S(1)} %cut.5), channel_id=1, source_target_pairs={{0,1},{1,0},{2,3},{3,2},{4,5},{5,4},{6,7},{7,6},{8,9},{9,8},{10,11... | collective-permute-start | bytes 1572872 | tf_op jit(solution)/shard_map/ppermute | solution.py:277
  36.3 9.4 %all-gather = bf16[1152,128]{1,0:T(8,128)(2,1)S(1)} all-gather(bf16[144,128]{1,0:T(8,128)(2,1)S(1)} %get-tuple-element.13), channel_id=2, replica_groups=mesh['replica'=8,'fsdp'=4] {'replica'}, dimensions={0}, use_global_device_ids=true | all-gather | bytes 331776 | tf_op jit(solution)/shard_map/all_gather | solution.py:282
  45.7 5.2 %update.1 = f32[1024,512]{1,0:T(8,128)} custom-call(bf16[8,144,128]{2,1,0:T(8,128)(2,1)S(1)} %bitcast.8, bf16[128,64]{1,0:T(8,128)(2,1)S(1)} %copy-done.10, bf16[128,64]{1,0:T(8,128)(2,1)S(1)} %copy-done.11, bf16[64,512]{1,0:T(8,128)(2,1)S(1)} %copy-done.4, bf16[64,512]{1,0:T(8,128)(2,1)S(1)} %copy-done.5, ...), custom_call_target="tpu_custom_call" | custom-call | flops 1 | bytes 1 | tf_op jit(solution)/shard_map/update/pallas_call | solution.py:392
  50.9 8.9 %collective-permute-done.10.ao_ref = bf16[256,1024]{1,0:T(8,128)(2,1)S(1)} collective-permute-done((bf16[256,1024]{1,0:T(8,128)(2,1)S(1)}, bf16[256,1024]{1,0:T(8,128)(2,1)S(1)}, u32[]{:S(2)}, u32[]{:S(2)}) %collective-permute-start.10) | collective-permute-done | bytes 524320 | tf_op jit(solution)/shard_map/ppermute | solution.py:277
  59.7 2.6 %base.1.base_ref = f32[1024,512]{1,0:T(8,128)S(1)} custom-call(s32[1]{0:T(128)} %bitcast.me_ref, bf16[16,128]{1,0:T(8,128)(2,1)S(1)} %pad.4.after_ref.after2_ref.after3_ref.picks_ref, f32[128,128]{1,0:T(8,128)S(1)} %get-tuple-element.12.after2_ref.v_ref.after_ref, bf16[1024,512]{1,0:T(8,128)(2,1)S(1)} %bitcast.7, bf16[256,4096]{1,0:T(8,128)(2,1)S(1)} %copy-done.1, ...), custom_call_target="tpu_custom_call" | custom-call | flops 1 | bytes 1 | tf_op jit(solution)/shard_map/base/pallas_call | solution.py:314
  62.3 5.6 %collective-permute-done.11.got2_ref = bf16[768,512]{1,0:T(8,128)(2,1)S(1)} collective-permute-done((bf16[768,512]{1,0:T(8,128)(2,1)S(1)}, bf16[768,512]{1,0:T(8,128)(2,1)S(1)}, u32[]{:S(2)}, u32[]{:S(2)}) %collective-permute-start.11) | collective-permute-done | bytes 786464 | tf_op jit(solution)/shard_map/ppermute | solution.py:277
  67.9 1.1 %final.1 = bf16[1024,512]{1,0:T(8,128)(2,1)} custom-call(f32[1024,512]{1,0:T(8,128)S(1)} %base.1.base_ref, bf16[256,512]{1,0:T(8,128)(2,1)S(1)} %collective-permute-done.9.after_ref.got1_ref, bf16[768,512]{1,0:T(8,128)(2,1)S(1)} %collective-permute-done.11.got2_ref), custom_call_target="tpu_custom_call" | custom-call | flops 1 | bytes 1 | tf_op jit(solution)/shard_map/final/pallas_call | solution.py:403
  (40 shorter events, 0.6 us)
Async XLA Ops:
  0.6 15.6 %collective-permute-start.3 = (bf16[256,512]{1,0:T(8,128)(2,1)}, bf16[256,512]{1,0:T(8,128)(2,1)S(1)}, u32[]{:S(2)}, u32[]{:S(2)}) collective-permute-start(bf16[256,512]{1,0:T(8,128)(2,1)} %g_ref.7), channel_id=1, source_target_pairs={{0,1},{1,0},{2,3},{3,2},{4,5},{5,4},{6,7},{7,6},{8,9},{9,8},{10,11... | collective-permute-start | bytes 786440 | tf_op jit(solution)/shard_map/ppermute | solution.py:277
  4.5 1.6 %copy-start = (bf16[256,4096]{1,0:T(8,128)(2,1)S(1)}, bf16[256,4096]{1,0:T(8,128)(2,1)}, u32[]{:S(2)}) copy-start(bf16[256,4096]{1,0:T(8,128)(2,1)} %acts_ref.13) | copy-start | bytes 6291460
  6.1 10.3 %copy-start.2 = (bf16[256,512]{1,0:T(8,128)(2,1)S(1)}, bf16[256,512]{1,0:T(8,128)(2,1)}, u32[]{:S(2)}) copy-start(bf16[256,512]{1,0:T(8,128)(2,1)} %g_ref.7) | copy-start | bytes 786436
  6.1 10.1 %collective-permute-start.4 = (bf16[256,256]{1,0:T(8,128)(2,1)S(1)}, bf16[256,256]{1,0:T(8,128)(2,1)S(1)}, u32[]{:S(2)}, u32[]{:S(2)}) collective-permute-start(bf16[256,256]{1,0:T(8,128)(2,1)S(1)} %cut.3), channel_id=1, source_target_pairs={{0,1},{1,0},{2,3},{3,2},{4,5},{5,4},{6,7},{7,6},{8,9},{9,8},{10,11... | collective-permute-start | bytes 393224 | tf_op jit(solution)/shard_map/ppermute | solution.py:277
  6.2 7.0 %collective-permute-start = (bf16[16,128]{1,0:T(8,128)(2,1)S(1)}, bf16[16,128]{1,0:T(8,128)(2,1)S(1)}, u32[]{:S(2)}, u32[]{:S(2)}) collective-permute-start(bf16[16,128]{1,0:T(8,128)(2,1)S(1)} %pad.4.after_ref.after2_ref.after3_ref.picks_ref), channel_id=1, source_target_pairs={{0,1},{1,0},{2,3},{3,2},{4,5},{5,4},{6,7},{7,6},{8,9},{9,8},{10,11... | collective-permute-start | bytes 12296 | tf_op jit(solution)/shard_map/ppermute | solution.py:277
  8.2 5.0 %collective-permute-start.1 = (bf16[16,128]{1,0:T(8,128)(2,1)S(1)}, bf16[16,128]{1,0:T(8,128)(2,1)S(1)}, u32[]{:S(2)}, u32[]{:S(2)}) collective-permute-start(bf16[16,128]{1,0:T(8,128)(2,1)S(1)} %pad.4.after_ref.after2_ref.after3_ref.picks_ref), channel_id=1, source_target_pairs={{0,2},{1,3},{2,0},{3,1},{4,6},{5,7},{6,4},{7,5},{8,10},{9,11},{10,... | collective-permute-start | bytes 12296 | tf_op jit(solution)/shard_map/ppermute | solution.py:277
  10.8 5.4 %collective-permute-start.2 = (bf16[16,128]{1,0:T(8,128)(2,1)S(1)}, bf16[16,128]{1,0:T(8,128)(2,1)S(1)}, u32[]{:S(2)}, u32[]{:S(2)}) collective-permute-start(bf16[16,128]{1,0:T(8,128)(2,1)S(1)} %pad.4.after_ref.after2_ref.after3_ref.picks_ref), channel_id=1, source_target_pairs={{0,3},{1,2},{2,1},{3,0},{4,7},{5,6},{6,5},{7,4},{8,11},{9,10},{10,... | collective-permute-start | bytes 12296 | tf_op jit(solution)/shard_map/ppermute | solution.py:277
  16.3 2.0 %copy-start.3 = (bf16[1,1024,512]{2,1,0:T(8,128)(2,1)S(1)}, bf16[1,1024,512]{2,1,0:T(8,128)(2,1)}, u32[]{:S(2)}) copy-start(bf16[1,1024,512]{2,1,0:T(8,128)(2,1)} %param.14) | copy-start | bytes 3145732
  16.3 2.0 %copy-start.4 = (bf16[64,512]{1,0:T(8,128)(2,1)S(1)}, bf16[64,512]{1,0:T(8,128)(2,1)}, u32[]{:S(2)}) copy-start(bf16[64,512]{1,0:T(8,128)(2,1)} %constant.25.clone.csth_ref) | copy-start | bytes 196612
  16.3 2.0 %copy-start.5 = (bf16[64,512]{1,0:T(8,128)(2,1)S(1)}, bf16[64,512]{1,0:T(8,128)(2,1)}, u32[]{:S(2)}) copy-start(bf16[64,512]{1,0:T(8,128)(2,1)} %constant.26.clone.cstl_ref) | copy-start | bytes 196612
  16.3 2.0 %copy-start.8 = (bf16[64,256]{1,0:T(8,128)(2,1)S(1)}, bf16[64,256]{1,0:T(8,128)(2,1)}, u32[]{:S(2)}) copy-start(bf16[64,256]{1,0:T(8,128)(2,1)} %constant.23.clone.c4h_ref) | copy-start | bytes 98308
  16.4 2.0 %copy-start.9 = (bf16[64,256]{1,0:T(8,128)(2,1)S(1)}, bf16[64,256]{1,0:T(8,128)(2,1)}, u32[]{:S(2)}) copy-start(bf16[64,256]{1,0:T(8,128)(2,1)} %constant.24.clone.c4l_ref) | copy-start | bytes 98308
  16.4 16.0 %collective-permute-start.8 = (bf16[256,768]{1,0:T(8,128)(2,1)S(1)}, bf16[256,768]{1,0:T(8,128)(2,1)S(1)}, u32[]{:S(2)}, u32[]{:S(2)}) collective-permute-start(bf16[256,768]{1,0:T(8,128)(2,1)S(1)} %cut.4), channel_id=1, source_target_pairs={{0,1},{1,0},{2,3},{3,2},{4,5},{5,4},{6,7},{7,6},{8,9},{9,8},{10,11... | collective-permute-start | bytes 1179656 | tf_op jit(solution)/shard_map/ppermute | solution.py:277
  16.8 16.4 %collective-permute-start.9 = (bf16[256,512]{1,0:T(8,128)(2,1)S(1)}, bf16[256,512]{1,0:T(8,128)(2,1)S(1)}, u32[]{:S(2)}, u32[]{:S(2)}) collective-permute-start(bf16[256,512]{1,0:T(8,128)(2,1)S(1)} %sum_1.1.after_ref), channel_id=1, source_target_pairs={{0,2},{1,3},{2,0},{3,1},{4,6},{5,7},{6,4},{7,5},{8,10},{9,11},{10,... | collective-permute-start | bytes 786440 | tf_op jit(solution)/shard_map/ppermute | solution.py:277
  22.8 10.3 %collective-permute-start.5 = (bf16[128,128]{1,0:T(8,128)(2,1)S(1)}, bf16[128,128]{1,0:T(8,128)(2,1)S(1)}, u32[]{:S(2)}, u32[]{:S(2)}) collective-permute-start(bf16[128,128]{1,0:T(8,128)(2,1)S(1)} %get-tuple-element.9.after_ref), channel_id=1, source_target_pairs={{0,1},{1,0},{2,3},{3,2},{4,5},{5,4},{6,7},{7,6},{8,9},{9,8},{10,11... | collective-permute-start | bytes 98312 | tf_op jit(solution)/shard_map/ppermute | solution.py:277
  23.5 9.6 %collective-permute-start.6 = (bf16[128,128]{1,0:T(8,128)(2,1)S(1)}, bf16[128,128]{1,0:T(8,128)(2,1)S(1)}, u32[]{:S(2)}, u32[]{:S(2)}) collective-permute-start(bf16[128,128]{1,0:T(8,128)(2,1)S(1)} %get-tuple-element.10), channel_id=1, source_target_pairs={{0,2},{1,3},{2,0},{3,1},{4,6},{5,7},{6,4},{7,5},{8,10},{9,11},{10,... | collective-permute-start | bytes 98312 | tf_op jit(solution)/shard_map/ppermute | solution.py:277
  26.4 6.8 %collective-permute-start.7 = (bf16[128,128]{1,0:T(8,128)(2,1)S(1)}, bf16[128,128]{1,0:T(8,128)(2,1)S(1)}, u32[]{:S(2)}, u32[]{:S(2)}) collective-permute-start(bf16[128,128]{1,0:T(8,128)(2,1)S(1)} %get-tuple-element.11), channel_id=1, source_target_pairs={{0,3},{1,2},{2,1},{3,0},{4,7},{5,6},{6,5},{7,4},{8,11},{9,10},{10,... | collective-permute-start | bytes 98312 | tf_op jit(solution)/shard_map/ppermute | solution.py:277
  33.1 1.6 %copy-start.1 = (bf16[256,4096]{1,0:T(8,128)(2,1)S(1)}, bf16[256,4096]{1,0:T(8,128)(2,1)}, u32[]{:S(2)}) copy-start(bf16[256,4096]{1,0:T(8,128)(2,1)} %acts_ref.13) | copy-start | bytes 6291460
  33.3 12.4 %copy-start.10 = (bf16[128,64]{1,0:T(8,128)(2,1)S(1)}, bf16[128,64]{1,0:T(8,128)(2,1)}, u32[]{:S(2)}) copy-start(bf16[128,64]{1,0:T(8,128)(2,1)} %constant.29.clone.c2th_ref) | copy-start | bytes 49156
  33.3 12.4 %copy-start.11 = (bf16[128,64]{1,0:T(8,128)(2,1)S(1)}, bf16[128,64]{1,0:T(8,128)(2,1)}, u32[]{:S(2)}) copy-start(bf16[128,64]{1,0:T(8,128)(2,1)} %constant.30.clone.c2tl_ref) | copy-start | bytes 49156
  33.3 34.6 %collective-permute-start.11 = (bf16[768,512]{1,0:T(8,128)(2,1)S(1)}, bf16[768,512]{1,0:T(8,128)(2,1)S(1)}, u32[]{:S(2)}, u32[]{:S(2)}) collective-permute-start(bf16[768,512]{1,0:T(8,128)(2,1)S(1)} %hold.1.after_ref.after2_ref.after3_ref), channel_id=1, source_target_pairs={{0,2},{1,3},{2,0},{3,1},{4,6},{5,7},{6,4},{7,5},{8,10},{9,11},{10,... | collective-permute-start | bytes 2359304 | tf_op jit(solution)/shard_map/ppermute | solution.py:277
  34.8 24.9 %copy-start.6 = (bf16[256,64]{1,0:T(8,128)(2,1)S(1)}, bf16[256,64]{1,0:T(8,128)(2,1)}, u32[]{:S(2)}) copy-start(bf16[256,64]{1,0:T(8,128)(2,1)} %constant.27.clone.c4th_ref) | copy-start | bytes 98308
  34.8 24.9 %copy-start.7 = (bf16[256,64]{1,0:T(8,128)(2,1)S(1)}, bf16[256,64]{1,0:T(8,128)(2,1)}, u32[]{:S(2)}) copy-start(bf16[256,64]{1,0:T(8,128)(2,1)} %constant.28.clone.c4tl_ref) | copy-start | bytes 98308
  34.8 24.9 %collective-permute-start.10 = (bf16[256,1024]{1,0:T(8,128)(2,1)S(1)}, bf16[256,1024]{1,0:T(8,128)(2,1)S(1)}, u32[]{:S(2)}, u32[]{:S(2)}) collective-permute-start(bf16[256,1024]{1,0:T(8,128)(2,1)S(1)} %cut.5), channel_id=1, source_target_pairs={{0,1},{1,0},{2,3},{3,2},{4,5},{5,4},{6,7},{7,6},{8,9},{9,8},{10,11... | collective-permute-start | bytes 1572872 | tf_op jit(solution)/shard_map/ppermute | solution.py:277

commit v4 on v3

--- a/solution.py
+++ b/solution.py
@@ -13,6 +13,7 @@
 SIZE = 64
 LANES = 128
 GATHER = True
+SECOND = 384
 GROUP = 4
 
 
@@ -131,7 +132,7 @@
         outs[s][...] = pack_halves(v, top).astype(outs[s].dtype)
 
 
-def base_kernel(top, me_ref, picks_ref, v_ref, m_ref, acts_ref, ao_ref, g_ref, gp_ref, c4th_ref, c4tl_ref, csth_ref,
+def base_kernel(top, me_ref, picks_ref, v_ref, m_ref, acts_ref, ao1_ref, ao2_ref, g_ref, gp_ref, c4th_ref, c4tl_ref, csth_ref,
                 cstl_ref, out_ref, a0_ref, sem):
     copy = fetch(me_ref, acts_ref, 0, 0, a0_ref, sem)
     copy.start()
@@ -160,7 +161,9 @@
         tl = jnp.where(own, dot_nt(c4tl_ref[...], hot[here]), 0.0).astype(BF16)
         inv = dot(th, xh[here]) + dot(tl, xh[here]) + dot(th, xl[here])
         at = slice(g * rows, (g + 1) * rows)
-        pair = dot_tn(a0_ref[:, at], gmat) + dot_tn(ao_ref[:, at], gpmat)
+        ao_ref, first = (ao1_ref, 0) if 2 * g < groups else (ao2_ref, shard // 2)
+        theirs = ao_ref[:, g * rows - first : (g + 1) * rows - first]
+        pair = dot_tn(a0_ref[:, at], gmat) + dot_tn(theirs, gpmat)
         out_ref[at, :] = 0.9 * m_ref[at, :].astype(F32) + pair - inv
 
 
@@ -244,13 +247,28 @@
     del x_ref, after_ref, after2_ref, out_ref
 
 
-def final_kernel(base_ref, got1_ref, got2_ref, out_ref, rows, sems):
-    size = rows.shape[1]
+def early_kernel(base_ref, got1_ref, got2_ref, out_ref, rows, sems):
+    copies, at = [], 0
+    for n, got_ref in enumerate((got1_ref, got2_ref)):
+        here = slice(at, at + got_ref.shape[0])
+        rows[here, :] = (base_ref[here, :] + got_ref[...].astype(F32)).astype(BF16)
+        copies.append(pltpu.make_async_copy(rows.at[here], out_ref.at[here], sems.at[n]))
+        copies[-1].start()
+        at += got_ref.shape[0]
+    for copy in copies:
+        copy.wait()
+
+
+def last_kernel(base_ref, got_ref, early_ref, out_ref, rows, sems):
+    del early_ref
+    shard = base_ref.shape[0]
+    size = got_ref.shape[0] // 2
     copies = []
-    for n in range(rows.shape[0]):
-        got = got1_ref[...] if n == 0 else got2_ref[(n - 1) * size : n * size, :]
-        rows[n] = (base_ref[n * size : (n + 1) * size, :] + got.astype(F32)).astype(BF16)
-        copies.append(pltpu.make_async_copy(rows.at[n], out_ref.at[n * size : (n + 1) * size], sems.at[n]))
+    for n in range(2):
+        here = slice(n * size, (n + 1) * size)
+        there = slice(shard - (2 - n) * size, shard - (1 - n) * size)
+        rows[here, :] = (base_ref[there, :] + got_ref[here, :].astype(F32)).astype(BF16)
+        copies.append(pltpu.make_async_copy(rows.at[here], out_ref.at[there], sems.at[n]))
         copies[-1].start()
     for copy in copies:
         copy.wait()
@@ -294,6 +312,7 @@
     crows = shard // SIZE
     top = chosen_blocks.shape[2]
     lead = shard // 4
+    second = SECOND
     spans = width // SIZE
     high, low = table_parts()
     c4h, c4l = (np.tile(t, (1, GROUP)) for t in (high, low))
@@ -341,7 +360,7 @@
         return jax.ShapeDtypeStruct(shape, F32)
 
     acts, grads = activations, output_grads
-    picks4 = jnp.concatenate([picks] + [swap_near(picks, s) for s in (1, 2, 3)], axis=0)
+    got_picks = [swap_near(picks, s) for s in (1, 2, 3)]
     got_grads = swap_near(grads, 1)
     cols_1 = swap_near(cut([(3, 0, lead)], picks, picks, picks), 1)
 
@@ -350,10 +369,11 @@
         kernel = functools.partial(sum_kernel, start)
         return call(kernel, name, bf(size, width), (mine, acts, grads, got_grads, cols, after), "shvvva", size)
 
-    cut_2 = cut([(3, lead, shard - lead)], picks4, cols_1, got_grads)
-    cols_2 = swap_near(cut_2, 1)
     sum_1 = sums(0, cols_1, cols_1, "sum_1")
     got_1 = swap_near(sum_1, 2)
+    picks4 = jnp.concatenate([picks, *got_picks], axis=0)
+    cut_2 = cut([(3, lead, second)], picks4, cols_1, got_grads)
+    cols_2 = swap_near(cut_2, 1)
     own, *parts = call(
         functools.partial(chosen_kernel, top),
         "chosen",
@@ -362,7 +382,7 @@
         "s" + "v" * 8 + "a",
     )
     got = [swap_near(x, s + 1) for s, x in enumerate(parts)]
-    sum_2 = sums(lead, cols_2, parts[0], "sum_2")
+    sum_2 = sums(lead, cols_2, got_1, "sum_2")
     values, pack = call(
         pack_kernel, "pack", [f32(count, 2 * SIZE), bf(count + crows, 2 * SIZE)], (own, *got, picks, sum_2), "vvvvva"
     )
@@ -377,13 +397,18 @@
         name="hold",
     )(sum_2, got_1, values)
     got_2 = swap_near(sum_2, 2)
-    cols_own = swap_near(cut([(1, 0, shard)], sum_2, sum_2, sum_2), 1)
+    cols_3 = swap_near(cut([(3, lead + second, shard - lead - second)], values, values, values), 1)
+    sum_3 = sums(lead + second, cols_3, sum_2, "sum_3")
+    got_3 = swap_near(sum_3, 2)
+    cols_own = [
+        swap_near(cut([(1, n * (shard // 2), shard // 2)], sum_3, sum_3, sum_3), 1) for n in range(2)
+    ]
     base = call(
         functools.partial(base_kernel, top),
         "base",
         f32(shard, width),
-        (mine, picks, values, old, acts, cols_own, grads, got_grads, c4th, c4tl, csth, cstl),
-        "svvvhvvvvvvv",
+        (mine, picks, values, old, acts, *cols_own, grads, got_grads, c4th, c4tl, csth, cstl),
+        "svvvhvvvvvvvv",
         shard,
     )
 
@@ -400,16 +425,27 @@
         cost_estimate=COST,
         name="update",
     )(everyone, c2th, c2tl, csth, cstl, values)
-    moment_next = pl.pallas_call(
-        final_kernel,
+    early = pl.pallas_call(
+        early_kernel,
         out_shape=bf(shard, width),
         in_specs=[VMEM()] * 3,
         out_specs=HBM,
-        scratch_shapes=[pltpu.VMEM((shard // lead, lead, width), BF16), pltpu.SemaphoreType.DMA((shard // lead,))],
+        scratch_shapes=[pltpu.VMEM((lead + second, width), BF16), pltpu.SemaphoreType.DMA((2,))],
         compiler_params=PARAMS,
         cost_estimate=COST,
-        name="final",
+        name="early",
     )(base, got_1, got_2)
+    moment_next = pl.pallas_call(
+        last_kernel,
+        out_shape=bf(shard, width),
+        in_specs=[VMEM(), VMEM(), HBM],
+        out_specs=HBM,
+        scratch_shapes=[pltpu.VMEM((shard - lead - second, width), BF16), pltpu.SemaphoreType.DMA((2,))],
+        input_output_aliases={2: 0},
+        compiler_params=PARAMS,
+        cost_estimate=COST,
+        name="last",
+    )(base, got_3, early)
     return moment_next[None], update
 
 

time: 69.2 us -> 68.9 us (level)
  waiting for transfers between devices: 25.1 us -> 18.1 us
  starting transfers between devices: 16.2 us -> 22.5 us
  Pallas kernels: 14.6 us -> 15.5 us
    ppermute x12 -> x15, waiting for transfers between devices: 25.1 us -> 18.1 us  [swap(): return lax.ppermute(x, axis, [(i, i ^ bit) for i in range(size)])]
    ppermute x12 -> x15, starting transfers between devices: 16.2 us -> 22.5 us  [swap(): return lax.ppermute(x, axis, [(i, i ^ bit) for i in range(size)])]
    pallas_call x1 -> x2, Pallas kernels: 1.07 us -> 1.71 us  [the longest x1 0.91 us: body(): pl.pallas_call(early_kernel, out_shape=bf(shard, width), in_specs=[VMEM()...]
    pallas_call x5 -> x6, Pallas kernels: 8.18 us -> 8.43 us  [call(): pl.pallas_call(kernel, out_shape=outs, in_specs=[{'s': SMEM, 'a': ANY, 'h...]
  transfers between devices with their start and end apart: 12 -> 15, of which waited for: 6 -> 6; matrix products, arithmetic and copies ran while one was open for 1% -> 1% of each run, Pallas kernels for 19% -> 21%
where the time goes in v4:
time: 68.9 us; the launch traced here: 68.7 us
  starting transfers between devices  22.5 us (33%)
  waiting for transfers between devices  18.1 us (26%)
  Pallas kernels  15.5 us (22%)
  blocking collectives  9.33 us (14%)
  local copies, waits for them, and re-layouts  1.76 us (3%)
  between operations  0.88 us (1%)
  other arithmetic  0.69 us (1%)
    ppermute x15, starting transfers between devices, swap(): return lax.ppermute(x, axis, [(i, i ^ bit) for i in range(size)])  22.5 us
    ppermute x15, waiting for transfers between devices, swap(): return lax.ppermute(x, axis, [(i, i ^ bit) for i in range(size)])  18.1 us
    all_gather x1, blocking collectives, gather_replicas(): return lax.all_gather(x, 'replica', axis=0, tiled=False)  9.33 us
    pallas_call x6, Pallas kernels, call(): pl.pallas_call(kernel, out_shape=outs, in_specs=[{'s': SMEM, 'a': ANY, 'h...  8.43 us
    pallas_call x1, Pallas kernels, body(): pl.pallas_call(functools.partial(update_kernel, top, crows), grid=(replic...  5.16 us
    unnamed x24, local copies, waits for them, and re-layouts  1.66 us
  transfers between devices with their start and end apart: 15, of which 6 were waited for; matrix products, arithmetic and copies ran while one was open for 1% of the time, Pallas kernels for 21%

profile of v4, /device:TPU:0, one launch (start us, length us, event | category | flops | bytes accessed | tf_op | source)
XLA Modules:
  0.0 68.7 jit_solution(13759107335187571707)
XLA Ops:
  0.6 3.1 %collective-permute-start.3 = (bf16[256,512]{1,0:T(8,128)(2,1)}, bf16[256,512]{1,0:T(8,128)(2,1)S(1)}, u32[]{:S(2)}, u32[]{:S(2)}) collective-permute-start(bf16[256,512]{1,0:T(8,128)(2,1)} %g_ref.9), channel_id=1, source_target_pairs={{0,1},{1,0},{2,3},{3,2},{4,5},{5,4},{6,7},{7,6},{8,9},{9,8},{10,11... | collective-permute-start | bytes 786440 | tf_op jit(solution)/shard_map/ppermute | solution.py:295
  3.7 0.7 %convert_bitcast_fusion = bf16[16,8]{0,1:T(8,128)(2,1)S(1)} fusion(s32[1,16,8]{1,2,0:T(8,128)} %param.15), kind=kLoop, calls=%fused_computation.1 | loop fusion | flops 128 | bytes 768 | tf_op jit(solution)/shard_map/convert_element_type | solution.py:325
  4.5 1.6 %copy-done = bf16[256,4096]{1,0:T(8,128)(2,1)S(1)} copy-done((bf16[256,4096]{1,0:T(8,128)(2,1)S(1)}, bf16[256,4096]{1,0:T(8,128)(2,1)}, u32[]{:S(2)}) %copy-start) | copy-done | bytes 2097176
  6.2 2.0 %collective-permute-start = (bf16[16,128]{1,0:T(8,128)(2,1)S(1)}, bf16[16,128]{1,0:T(8,128)(2,1)S(1)}, u32[]{:S(2)}, u32[]{:S(2)}) collective-permute-start(bf16[16,128]{1,0:T(8,128)(2,1)S(1)} %pad.4.after_ref.after2_ref.after3_ref.picks_ref), channel_id=1, source_target_pairs={{0,1},{1,0},{2,3},{3,2},{4,5},{5,4},{6,7},{7,6},{8,9},{9,8},{10,11... | collective-permute-start | bytes 12296 | tf_op jit(solution)/shard_map/ppermute | solution.py:295
  8.2 2.6 %collective-permute-start.1 = (bf16[16,128]{1,0:T(8,128)(2,1)S(1)}, bf16[16,128]{1,0:T(8,128)(2,1)S(1)}, u32[]{:S(2)}, u32[]{:S(2)}) collective-permute-start(bf16[16,128]{1,0:T(8,128)(2,1)S(1)} %pad.4.after_ref.after2_ref.after3_ref.picks_ref), channel_id=1, source_target_pairs={{0,2},{1,3},{2,0},{3,1},{4,6},{5,7},{6,4},{7,5},{8,10},{9,11},{10,... | collective-permute-start | bytes 12296 | tf_op jit(solution)/shard_map/ppermute | solution.py:295
  10.8 2.4 %collective-permute-done.4.theirs_ref.after_ref.after2_ref = bf16[256,256]{1,0:T(8,128)(2,1)S(1)} collective-permute-done((bf16[256,256]{1,0:T(8,128)(2,1)S(1)}, bf16[256,256]{1,0:T(8,128)(2,1)S(1)}, u32[]{:S(2)}, u32[]{:S(2)}) %collective-permute-start.4) | collective-permute-done | bytes 131104 | tf_op jit(solution)/shard_map/ppermute | solution.py:295
  13.6 2.8 %collective-permute-start.9 = (bf16[256,512]{1,0:T(8,128)(2,1)S(1)}, bf16[256,512]{1,0:T(8,128)(2,1)S(1)}, u32[]{:S(2)}, u32[]{:S(2)}) collective-permute-start(bf16[256,512]{1,0:T(8,128)(2,1)S(1)} %sum_1.1.after_ref), channel_id=1, source_target_pairs={{0,2},{1,3},{2,0},{3,1},{4,6},{5,7},{6,4},{7,5},{8,10},{9,11},{10,... | collective-permute-start | bytes 786440 | tf_op jit(solution)/shard_map/ppermute | solution.py:295
  16.5 1.7 %collective-permute-start.8 = (bf16[256,384]{1,0:T(8,128)(2,1)S(1)}, bf16[256,384]{1,0:T(8,128)(2,1)S(1)}, u32[]{:S(2)}, u32[]{:S(2)}) collective-permute-start(bf16[256,384]{1,0:T(8,128)(2,1)S(1)} %cut.6), channel_id=1, source_target_pairs={{0,1},{1,0},{2,3},{3,2},{4,5},{5,4},{6,7},{7,6},{8,9},{9,8},{10,11... | collective-permute-start | bytes 589832 | tf_op jit(solution)/shard_map/ppermute | solution.py:295
  18.3 4.5 %chosen.1 = (f32[128,128]{1,0:T(8,128)S(1)}, bf16[128,128]{1,0:T(8,128)(2,1)S(1)}, bf16[128,128]{1,0:T(8,128)(2,1)S(1)}, bf16[128,128]{1,0:T(8,128)(2,1)S(1)}) custom-call(s32[1]{0:T(128)} %bitcast.me_ref, bf16[64,128]{1,0:T(8,128)(2,1)S(1)} %pad_maximum_fusion.picks_ref.after_ref, bf16[256,4096]{1,0:T(8,128)(2,1)S(1)} %copy-done, ...), custom_call_target="tpu_custom_call" | custom-call | flops 1 | bytes 1 | tf_op jit(solution)/shard_map/chosen/pallas_call | solution.py:333
  23.2 0.6 collective-permute-start.6
  23.8 3.5 %collective-permute-start.7 = (bf16[128,128]{1,0:T(8,128)(2,1)S(1)}, bf16[128,128]{1,0:T(8,128)(2,1)S(1)}, u32[]{:S(2)}, u32[]{:S(2)}) collective-permute-start(bf16[128,128]{1,0:T(8,128)(2,1)S(1)} %get-tuple-element.11), channel_id=1, source_target_pairs={{0,3},{1,2},{2,1},{3,0},{4,7},{5,6},{6,5},{7,4},{8,11},{9,10},{10,... | collective-permute-start | bytes 98312 | tf_op jit(solution)/shard_map/ppermute | solution.py:295
  27.2 2.5 %collective-permute-done.9.after_ref.got1_ref = bf16[256,512]{1,0:T(8,128)(2,1)S(1)} collective-permute-done((bf16[256,512]{1,0:T(8,128)(2,1)S(1)}, bf16[256,512]{1,0:T(8,128)(2,1)S(1)}, u32[]{:S(2)}, u32[]{:S(2)}) %collective-permute-start.9) | collective-permute-done | bytes 262176 | tf_op jit(solution)/shard_map/ppermute | solution.py:295
  30.4 0.8 %collective-permute-start.10 = (bf16[256,384]{1,0:T(8,128)(2,1)S(1)}, bf16[256,384]{1,0:T(8,128)(2,1)S(1)}, u32[]{:S(2)}, u32[]{:S(2)}) collective-permute-start(bf16[256,384]{1,0:T(8,128)(2,1)S(1)} %cut.7), channel_id=1, source_target_pairs={{0,1},{1,0},{2,3},{3,2},{4,5},{5,4},{6,7},{7,6},{8,9},{9,8},{10,11... | collective-permute-start | bytes 589832 | tf_op jit(solution)/shard_map/ppermute | solution.py:295
  31.2 2.6 %collective-permute-start.14 = (bf16[384,512]{1,0:T(8,128)(2,1)S(1)}, bf16[384,512]{1,0:T(8,128)(2,1)S(1)}, u32[]{:S(2)}, u32[]{:S(2)}) collective-permute-start(bf16[384,512]{1,0:T(8,128)(2,1)S(1)} %hold.1.after_ref), channel_id=1, source_target_pairs={{0,2},{1,3},{2,0},{3,1},{4,6},{5,7},{6,4},{7,5},{8,10},{9,11},{10,... | collective-permute-start | bytes 1179656 | tf_op jit(solution)/shard_map/ppermute | solution.py:295
  33.8 7.4 %collective-permute-done.10.theirs_ref = bf16[256,384]{1,0:T(8,128)(2,1)S(1)} collective-permute-done((bf16[256,384]{1,0:T(8,128)(2,1)S(1)}, bf16[256,384]{1,0:T(8,128)(2,1)S(1)}, u32[]{:S(2)}, u32[]{:S(2)}) %collective-permute-start.10) | collective-permute-done | bytes 196640 | tf_op jit(solution)/shard_map/ppermute | solution.py:295
  41.9 1.0 %collective-permute-start.12 = (bf16[256,512]{1,0:T(8,128)(2,1)S(1)}, bf16[256,512]{1,0:T(8,128)(2,1)S(1)}, u32[]{:S(2)}, u32[]{:S(2)}) collective-permute-start(bf16[256,512]{1,0:T(8,128)(2,1)S(1)} %cut.9), channel_id=1, source_target_pairs={{0,1},{1,0},{2,3},{3,2},{4,5},{5,4},{6,7},{7,6},{8,9},{9,8},{10,11... | collective-permute-start | bytes 786440 | tf_op jit(solution)/shard_map/ppermute | solution.py:295
  42.9 1.2 %collective-permute-start.11 = (bf16[256,512]{1,0:T(8,128)(2,1)S(1)}, bf16[256,512]{1,0:T(8,128)(2,1)S(1)}, u32[]{:S(2)}, u32[]{:S(2)}) collective-permute-start(bf16[256,512]{1,0:T(8,128)(2,1)S(1)} %cut.8), channel_id=1, source_target_pairs={{0,1},{1,0},{2,3},{3,2},{4,5},{5,4},{6,7},{7,6},{8,9},{9,8},{10,11... | collective-permute-start | bytes 786440 | tf_op jit(solution)/shard_map/ppermute | solution.py:295
  44.1 9.3 %all-gather = bf16[1152,128]{1,0:T(8,128)(2,1)S(1)} all-gather(bf16[144,128]{1,0:T(8,128)(2,1)S(1)} %get-tuple-element.13), channel_id=2, replica_groups=mesh['replica'=8,'fsdp'=4] {'replica'}, dimensions={0}, use_global_device_ids=true | all-gather | bytes 331776 | tf_op jit(solution)/shard_map/all_gather | solution.py:300
  53.4 5.2 %update.1 = f32[1024,512]{1,0:T(8,128)} custom-call(bf16[8,144,128]{2,1,0:T(8,128)(2,1)S(1)} %bitcast.8, bf16[128,64]{1,0:T(8,128)(2,1)S(1)} %copy-done.10, bf16[128,64]{1,0:T(8,128)(2,1)S(1)} %copy-done.11, bf16[64,512]{1,0:T(8,128)(2,1)S(1)} %copy-done.4, bf16[64,512]{1,0:T(8,128)(2,1)S(1)} %copy-done.5, ...), custom_call_target="tpu_custom_call" | custom-call | flops 1 | bytes 1 | tf_op jit(solution)/shard_map/update/pallas_call | solution.py:417
  59.0 4.4 %collective-permute-done.11.ao1_ref = bf16[256,512]{1,0:T(8,128)(2,1)S(1)} collective-permute-done((bf16[256,512]{1,0:T(8,128)(2,1)S(1)}, bf16[256,512]{1,0:T(8,128)(2,1)S(1)}, u32[]{:S(2)}, u32[]{:S(2)}) %collective-permute-start.11) | collective-permute-done | bytes 262176 | tf_op jit(solution)/shard_map/ppermute | solution.py:295
  63.4 2.6 %base.1.base_ref = f32[1024,512]{1,0:T(8,128)S(1)} custom-call(s32[1]{0:T(128)} %bitcast.me_ref, bf16[16,128]{1,0:T(8,128)(2,1)S(1)} %pad.4.after_ref.after2_ref.after3_ref.picks_ref, f32[128,128]{1,0:T(8,128)S(1)} %get-tuple-element.12.after_ref.after2_ref.after3_ref.v_ref, bf16[1024,512]{1,0:T(8,128)(2,1)S(1)} %bitcast.7, bf16[256,4096]{1,0:T(8,128)(2,1)S(1)} %copy-done.1, ...), custom_call_target="tpu_custom_call" | custom-call | flops 1 | bytes 1 | tf_op jit(solution)/shard_map/base/pallas_call | solution.py:333
  66.0 0.9 %early.1.early_ref = bf16[1024,512]{1,0:T(8,128)(2,1)} custom-call(f32[1024,512]{1,0:T(8,128)S(1)} %base.1.base_ref, bf16[256,512]{1,0:T(8,128)(2,1)S(1)} %collective-permute-done.9.after_ref.got1_ref, bf16[384,512]{1,0:T(8,128)(2,1)S(1)} %collective-permute-done.14.got2_ref), custom_call_target="tpu_custom_call" | custom-call | flops 1 | bytes 1 | tf_op jit(solution)/shard_map/early/pallas_call | solution.py:428
  66.9 1.0 %collective-permute-done.13.got_ref = bf16[384,512]{1,0:T(8,128)(2,1)S(1)} collective-permute-done((bf16[384,512]{1,0:T(8,128)(2,1)S(1)}, bf16[384,512]{1,0:T(8,128)(2,1)S(1)}, u32[]{:S(2)}, u32[]{:S(2)}) %collective-permute-start.13) | collective-permute-done | bytes 393248 | tf_op jit(solution)/shard_map/ppermute | solution.py:295
  67.9 0.8 %last.1 = bf16[1024,512]{1,0:T(8,128)(2,1)} custom-call(f32[1024,512]{1,0:T(8,128)S(1)} %base.1.base_ref, bf16[384,512]{1,0:T(8,128)(2,1)S(1)} %collective-permute-done.13.got_ref, bf16[1024,512]{1,0:T(8,128)(2,1)} %early.1.early_ref), custom_call_target="tpu_custom_call", output_to_operand_aliasing={{}: (2, {})} | custom-call | flops 1 | bytes 1 | tf_op jit(solution)/shard_map/last/pallas_call | solution.py:438
  (50 shorter events, 2.7 us)
Async XLA Ops:
  0.6 12.6 %collective-permute-start.3 = (bf16[256,512]{1,0:T(8,128)(2,1)}, bf16[256,512]{1,0:T(8,128)(2,1)S(1)}, u32[]{:S(2)}, u32[]{:S(2)}) collective-permute-start(bf16[256,512]{1,0:T(8,128)(2,1)} %g_ref.9), channel_id=1, source_target_pairs={{0,1},{1,0},{2,3},{3,2},{4,5},{5,4},{6,7},{7,6},{8,9},{9,8},{10,11... | collective-permute-start | bytes 786440 | tf_op jit(solution)/shard_map/ppermute | solution.py:295
  6.1 7.1 %copy-start.2 = (bf16[256,512]{1,0:T(8,128)(2,1)S(1)}, bf16[256,512]{1,0:T(8,128)(2,1)}, u32[]{:S(2)}) copy-start(bf16[256,512]{1,0:T(8,128)(2,1)} %g_ref.9) | copy-start | bytes 786436
  6.1 7.0 %collective-permute-start.4 = (bf16[256,256]{1,0:T(8,128)(2,1)S(1)}, bf16[256,256]{1,0:T(8,128)(2,1)S(1)}, u32[]{:S(2)}, u32[]{:S(2)}) collective-permute-start(bf16[256,256]{1,0:T(8,128)(2,1)S(1)} %cut.5), channel_id=1, source_target_pairs={{0,1},{1,0},{2,3},{3,2},{4,5},{5,4},{6,7},{7,6},{8,9},{9,8},{10,11... | collective-permute-start | bytes 393224 | tf_op jit(solution)/shard_map/ppermute | solution.py:295
  6.2 10.2 %collective-permute-start = (bf16[16,128]{1,0:T(8,128)(2,1)S(1)}, bf16[16,128]{1,0:T(8,128)(2,1)S(1)}, u32[]{:S(2)}, u32[]{:S(2)}) collective-permute-start(bf16[16,128]{1,0:T(8,128)(2,1)S(1)} %pad.4.after_ref.after2_ref.after3_ref.picks_ref), channel_id=1, source_target_pairs={{0,1},{1,0},{2,3},{3,2},{4,5},{5,4},{6,7},{7,6},{8,9},{9,8},{10,11... | collective-permute-start | bytes 12296 | tf_op jit(solution)/shard_map/ppermute | solution.py:295
  8.2 8.2 %collective-permute-start.1 = (bf16[16,128]{1,0:T(8,128)(2,1)S(1)}, bf16[16,128]{1,0:T(8,128)(2,1)S(1)}, u32[]{:S(2)}, u32[]{:S(2)}) collective-permute-start(bf16[16,128]{1,0:T(8,128)(2,1)S(1)} %pad.4.after_ref.after2_ref.after3_ref.picks_ref), channel_id=1, source_target_pairs={{0,2},{1,3},{2,0},{3,1},{4,6},{5,7},{6,4},{7,5},{8,10},{9,11},{10,... | collective-permute-start | bytes 12296 | tf_op jit(solution)/shard_map/ppermute | solution.py:295
  10.8 5.6 %collective-permute-start.2 = (bf16[16,128]{1,0:T(8,128)(2,1)S(1)}, bf16[16,128]{1,0:T(8,128)(2,1)S(1)}, u32[]{:S(2)}, u32[]{:S(2)}) collective-permute-start(bf16[16,128]{1,0:T(8,128)(2,1)S(1)} %pad.4.after_ref.after2_ref.after3_ref.picks_ref), channel_id=1, source_target_pairs={{0,3},{1,2},{2,1},{3,0},{4,7},{5,6},{6,5},{7,4},{8,11},{9,10},{10,... | collective-permute-start | bytes 12296 | tf_op jit(solution)/shard_map/ppermute | solution.py:295
  13.6 4.7 %copy-start.3 = (bf16[1,1024,512]{2,1,0:T(8,128)(2,1)S(1)}, bf16[1,1024,512]{2,1,0:T(8,128)(2,1)}, u32[]{:S(2)}) copy-start(bf16[1,1024,512]{2,1,0:T(8,128)(2,1)} %param.14) | copy-start | bytes 3145732
  13.6 4.7 %copy-start.4 = (bf16[64,512]{1,0:T(8,128)(2,1)S(1)}, bf16[64,512]{1,0:T(8,128)(2,1)}, u32[]{:S(2)}) copy-start(bf16[64,512]{1,0:T(8,128)(2,1)} %constant.25.clone.csth_ref) | copy-start | bytes 196612
  13.6 4.7 %copy-start.5 = (bf16[64,512]{1,0:T(8,128)(2,1)S(1)}, bf16[64,512]{1,0:T(8,128)(2,1)}, u32[]{:S(2)}) copy-start(bf16[64,512]{1,0:T(8,128)(2,1)} %constant.26.clone.cstl_ref) | copy-start | bytes 196612
  13.6 16.1 %collective-permute-start.9 = (bf16[256,512]{1,0:T(8,128)(2,1)S(1)}, bf16[256,512]{1,0:T(8,128)(2,1)S(1)}, u32[]{:S(2)}, u32[]{:S(2)}) collective-permute-start(bf16[256,512]{1,0:T(8,128)(2,1)S(1)} %sum_1.1.after_ref), channel_id=1, source_target_pairs={{0,2},{1,3},{2,0},{3,1},{4,6},{5,7},{6,4},{7,5},{8,10},{9,11},{10,... | collective-permute-start | bytes 786440 | tf_op jit(solution)/shard_map/ppermute | solution.py:295
  16.5 10.7 %collective-permute-start.8 = (bf16[256,384]{1,0:T(8,128)(2,1)S(1)}, bf16[256,384]{1,0:T(8,128)(2,1)S(1)}, u32[]{:S(2)}, u32[]{:S(2)}) collective-permute-start(bf16[256,384]{1,0:T(8,128)(2,1)S(1)} %cut.6), channel_id=1, source_target_pairs={{0,1},{1,0},{2,3},{3,2},{4,5},{5,4},{6,7},{7,6},{8,9},{9,8},{10,11... | collective-permute-start | bytes 589832 | tf_op jit(solution)/shard_map/ppermute | solution.py:295
  22.8 7.5 %copy-start.1 = (bf16[256,4096]{1,0:T(8,128)(2,1)S(1)}, bf16[256,4096]{1,0:T(8,128)(2,1)}, u32[]{:S(2)}) copy-start(bf16[256,4096]{1,0:T(8,128)(2,1)} %acts_ref.19) | copy-start | bytes 6291460
  22.8 7.5 %collective-permute-start.5 = (bf16[128,128]{1,0:T(8,128)(2,1)S(1)}, bf16[128,128]{1,0:T(8,128)(2,1)S(1)}, u32[]{:S(2)}, u32[]{:S(2)}) collective-permute-start(bf16[128,128]{1,0:T(8,128)(2,1)S(1)} %get-tuple-element.9), channel_id=1, source_target_pairs={{0,1},{1,0},{2,3},{3,2},{4,5},{5,4},{6,7},{7,6},{8,9},{9,8},{10,11... | collective-permute-start | bytes 98312 | tf_op jit(solution)/shard_map/ppermute | solution.py:295
  23.2 7.0 %collective-permute-start.6 = (bf16[128,128]{1,0:T(8,128)(2,1)S(1)}, bf16[128,128]{1,0:T(8,128)(2,1)S(1)}, u32[]{:S(2)}, u32[]{:S(2)}) collective-permute-start(bf16[128,128]{1,0:T(8,128)(2,1)S(1)} %get-tuple-element.10), channel_id=1, source_target_pairs={{0,2},{1,3},{2,0},{3,1},{4,6},{5,7},{6,4},{7,5},{8,10},{9,11},{10,... | collective-permute-start | bytes 98312 | tf_op jit(solution)/shard_map/ppermute | solution.py:295
  23.8 6.5 %collective-permute-start.7 = (bf16[128,128]{1,0:T(8,128)(2,1)S(1)}, bf16[128,128]{1,0:T(8,128)(2,1)S(1)}, u32[]{:S(2)}, u32[]{:S(2)}) collective-permute-start(bf16[128,128]{1,0:T(8,128)(2,1)S(1)} %get-tuple-element.11), channel_id=1, source_target_pairs={{0,3},{1,2},{2,1},{3,0},{4,7},{5,6},{6,5},{7,4},{8,11},{9,10},{10,... | collective-permute-start | bytes 98312 | tf_op jit(solution)/shard_map/ppermute | solution.py:295
  30.4 10.9 %collective-permute-start.10 = (bf16[256,384]{1,0:T(8,128)(2,1)S(1)}, bf16[256,384]{1,0:T(8,128)(2,1)S(1)}, u32[]{:S(2)}, u32[]{:S(2)}) collective-permute-start(bf16[256,384]{1,0:T(8,128)(2,1)S(1)} %cut.7), channel_id=1, source_target_pairs={{0,1},{1,0},{2,3},{3,2},{4,5},{5,4},{6,7},{7,6},{8,9},{9,8},{10,11... | collective-permute-start | bytes 589832 | tf_op jit(solution)/shard_map/ppermute | solution.py:295
  31.2 34.8 %collective-permute-start.14 = (bf16[384,512]{1,0:T(8,128)(2,1)S(1)}, bf16[384,512]{1,0:T(8,128)(2,1)S(1)}, u32[]{:S(2)}, u32[]{:S(2)}) collective-permute-start(bf16[384,512]{1,0:T(8,128)(2,1)S(1)} %hold.1.after_ref), channel_id=1, source_target_pairs={{0,2},{1,3},{2,0},{3,1},{4,6},{5,7},{6,4},{7,5},{8,10},{9,11},{10,... | collective-permute-start | bytes 1179656 | tf_op jit(solution)/shard_map/ppermute | solution.py:295
  41.7 26.2 %collective-permute-start.13 = (bf16[384,512]{1,0:T(8,128)(2,1)S(1)}, bf16[384,512]{1,0:T(8,128)(2,1)S(1)}, u32[]{:S(2)}, u32[]{:S(2)}) collective-permute-start(bf16[384,512]{1,0:T(8,128)(2,1)S(1)} %sum_3.1.after_ref.after2_ref.after3_ref), channel_id=1, source_target_pairs={{0,2},{1,3},{2,0},{3,1},{4,6},{5,7},{6,4},{7,5},{8,10},{9,11},{10,... | collective-permute-start | bytes 1179656 | tf_op jit(solution)/shard_map/ppermute | solution.py:295
  41.8 11.6 %copy-start.10 = (bf16[128,64]{1,0:T(8,128)(2,1)S(1)}, bf16[128,64]{1,0:T(8,128)(2,1)}, u32[]{:S(2)}) copy-start(bf16[128,64]{1,0:T(8,128)(2,1)} %constant.29.clone.c2th_ref) | copy-start | bytes 49156
  41.8 11.6 %copy-start.11 = (bf16[128,64]{1,0:T(8,128)(2,1)S(1)}, bf16[128,64]{1,0:T(8,128)(2,1)}, u32[]{:S(2)}) copy-start(bf16[128,64]{1,0:T(8,128)(2,1)} %constant.30.clone.c2tl_ref) | copy-start | bytes 49156
  41.9 17.2 %collective-permute-start.12 = (bf16[256,512]{1,0:T(8,128)(2,1)S(1)}, bf16[256,512]{1,0:T(8,128)(2,1)S(1)}, u32[]{:S(2)}, u32[]{:S(2)}) collective-permute-start(bf16[256,512]{1,0:T(8,128)(2,1)S(1)} %cut.9), channel_id=1, source_target_pairs={{0,1},{1,0},{2,3},{3,2},{4,5},{5,4},{6,7},{7,6},{8,9},{9,8},{10,11... | collective-permute-start | bytes 786440 | tf_op jit(solution)/shard_map/ppermute | solution.py:295
  42.9 20.5 %copy-start.6 = (bf16[256,64]{1,0:T(8,128)(2,1)S(1)}, bf16[256,64]{1,0:T(8,128)(2,1)}, u32[]{:S(2)}) copy-start(bf16[256,64]{1,0:T(8,128)(2,1)} %constant.27.clone.c4th_ref) | copy-start | bytes 98308
  42.9 20.5 %copy-start.7 = (bf16[256,64]{1,0:T(8,128)(2,1)S(1)}, bf16[256,64]{1,0:T(8,128)(2,1)}, u32[]{:S(2)}) copy-start(bf16[256,64]{1,0:T(8,128)(2,1)} %constant.28.clone.c4tl_ref) | copy-start | bytes 98308
  42.9 20.5 %collective-permute-start.11 = (bf16[256,512]{1,0:T(8,128)(2,1)S(1)}, bf16[256,512]{1,0:T(8,128)(2,1)S(1)}, u32[]{:S(2)}, u32[]{:S(2)}) collective-permute-start(bf16[256,512]{1,0:T(8,128)(2,1)S(1)} %cut.8), channel_id=1, source_target_pairs={{0,1},{1,0},{2,3},{3,2},{4,5},{5,4},{6,7},{7,6},{8,9},{9,8},{10,11... | collective-permute-start | bytes 786440 | tf_op jit(solution)/shard_map/ppermute | solution.py:295
  (3 other events, 10.9 us)

commit v5 on v4

--- a/solution.py
+++ b/solution.py
@@ -262,11 +262,11 @@
 def last_kernel(base_ref, got_ref, early_ref, out_ref, rows, sems):
     del early_ref
     shard = base_ref.shape[0]
-    size = got_ref.shape[0] // 2
+    size = got_ref.shape[0] // 3
     copies = []
-    for n in range(2):
+    for n in range(3):
         here = slice(n * size, (n + 1) * size)
-        there = slice(shard - (2 - n) * size, shard - (1 - n) * size)
+        there = slice(shard - (3 - n) * size, shard - (2 - n) * size)
         rows[here, :] = (base_ref[there, :] + got_ref[here, :].astype(F32)).astype(BF16)
         copies.append(pltpu.make_async_copy(rows.at[here], out_ref.at[there], sems.at[n]))
         copies[-1].start()
@@ -374,6 +374,18 @@
     picks4 = jnp.concatenate([picks, *got_picks], axis=0)
     cut_2 = cut([(3, lead, second)], picks4, cols_1, got_grads)
     cols_2 = swap_near(cut_2, 1)
+    def hold(x, after, after2):
+        return pl.pallas_call(
+            hold_kernel,
+            out_shape=bf(*x.shape),
+            in_specs=[ANY] * 3,
+            out_specs=ANY,
+            input_output_aliases={0: 0},
+            compiler_params=PARAMS,
+            cost_estimate=COST,
+            name="hold",
+        )(x, after, after2)
+
     own, *parts = call(
         functools.partial(chosen_kernel, top),
         "chosen",
@@ -382,20 +394,12 @@
         "s" + "v" * 8 + "a",
     )
     got = [swap_near(x, s + 1) for s, x in enumerate(parts)]
-    sum_2 = sums(lead, cols_2, got_1, "sum_2")
+    sum_2 = sums(lead, cols_2, parts[0], "sum_2")
+    sum_2 = hold(sum_2, got_1, got_1)
     values, pack = call(
         pack_kernel, "pack", [f32(count, 2 * SIZE), bf(count + crows, 2 * SIZE)], (own, *got, picks, sum_2), "vvvvva"
     )
-    sum_2 = pl.pallas_call(
-        hold_kernel,
-        out_shape=bf(*sum_2.shape),
-        in_specs=[ANY] * 3,
-        out_specs=ANY,
-        input_output_aliases={0: 0},
-        compiler_params=PARAMS,
-        cost_estimate=COST,
-        name="hold",
-    )(sum_2, got_1, values)
+    sum_2 = hold(sum_2, got_1, values)
     got_2 = swap_near(sum_2, 2)
     cols_3 = swap_near(cut([(3, lead + second, shard - lead - second)], values, values, values), 1)
     sum_3 = sums(lead + second, cols_3, sum_2, "sum_3")
@@ -440,7 +444,7 @@
         out_shape=bf(shard, width),
         in_specs=[VMEM(), VMEM(), HBM],
         out_specs=HBM,
-        scratch_shapes=[pltpu.VMEM((shard - lead - second, width), BF16), pltpu.SemaphoreType.DMA((2,))],
+        scratch_shapes=[pltpu.VMEM((shard - lead - second, width), BF16), pltpu.SemaphoreType.DMA((3,))],
         input_output_aliases={2: 0},
         compiler_params=PARAMS,
         cost_estimate=COST,

time: 68.9 us -> 68.9 us (level)
  transfers between devices with their start and end apart: 15 -> 15, of which waited for: 6 -> 7; matrix products, arithmetic and copies ran while one was open for 1% -> 1% of each run, Pallas kernels for 21% -> 21%
where the time goes in v5:
time: 68.9 us; the launch traced here: 68.7 us
  starting transfers between devices  22.6 us (33%)
  waiting for transfers between devices  17.9 us (26%)
  Pallas kernels  15.5 us (22%)
  blocking collectives  9.44 us (14%)
  local copies, waits for them, and re-layouts  1.76 us (3%)
  between operations  0.85 us (1%)
  other arithmetic  0.69 us (1%)
    ppermute x15, starting transfers between devices, swap(): return lax.ppermute(x, axis, [(i, i ^ bit) for i in range(size)])  22.6 us
    ppermute x15, waiting for transfers between devices, swap(): return lax.ppermute(x, axis, [(i, i ^ bit) for i in range(size)])  17.9 us
    all_gather x1, blocking collectives, gather_replicas(): return lax.all_gather(x, 'replica', axis=0, tiled=False)  9.44 us
    pallas_call x6, Pallas kernels, call(): pl.pallas_call(kernel, out_shape=outs, in_specs=[{'s': SMEM, 'a': ANY, 'h...  8.43 us
    pallas_call x1, Pallas kernels, body(): pl.pallas_call(functools.partial(update_kernel, top, crows), grid=(replic...  5.16 us
    unnamed x24, local copies, waits for them, and re-layouts  1.66 us
  transfers between devices with their start and end apart: 15, of which 7 were waited for; matrix products, arithmetic and copies ran while one was open for 1% of the time, Pallas kernels for 21%

profile of v5, /device:TPU:0, one launch (start us, length us, event | category | flops | bytes accessed | tf_op | source)
XLA Modules:
  0.0 68.7 jit_solution(11147162554750218370)
XLA Ops:
  0.6 3.1 %collective-permute-start.3 = (bf16[256,512]{1,0:T(8,128)(2,1)}, bf16[256,512]{1,0:T(8,128)(2,1)S(1)}, u32[]{:S(2)}, u32[]{:S(2)}) collective-permute-start(bf16[256,512]{1,0:T(8,128)(2,1)} %g_ref.9), channel_id=1, source_target_pairs={{0,1},{1,0},{2,3},{3,2},{4,5},{5,4},{6,7},{7,6},{8,9},{9,8},{10,11... | collective-permute-start | bytes 786440 | tf_op jit(solution)/shard_map/ppermute | solution.py:295
  3.7 0.7 %convert_bitcast_fusion = bf16[16,8]{0,1:T(8,128)(2,1)S(1)} fusion(s32[1,16,8]{1,2,0:T(8,128)} %param.15), kind=kLoop, calls=%fused_computation.1 | loop fusion | flops 128 | bytes 768 | tf_op jit(solution)/shard_map/convert_element_type | solution.py:325
  4.5 1.6 %copy-done = bf16[256,4096]{1,0:T(8,128)(2,1)S(1)} copy-done((bf16[256,4096]{1,0:T(8,128)(2,1)S(1)}, bf16[256,4096]{1,0:T(8,128)(2,1)}, u32[]{:S(2)}) %copy-start) | copy-done | bytes 2097176
  6.2 2.0 %collective-permute-start = (bf16[16,128]{1,0:T(8,128)(2,1)S(1)}, bf16[16,128]{1,0:T(8,128)(2,1)S(1)}, u32[]{:S(2)}, u32[]{:S(2)}) collective-permute-start(bf16[16,128]{1,0:T(8,128)(2,1)S(1)} %pad.4.after_ref.after2_ref.after3_ref.picks_ref), channel_id=1, source_target_pairs={{0,1},{1,0},{2,3},{3,2},{4,5},{5,4},{6,7},{7,6},{8,9},{9,8},{10,11... | collective-permute-start | bytes 12296 | tf_op jit(solution)/shard_map/ppermute | solution.py:295
  8.2 2.6 %collective-permute-start.1 = (bf16[16,128]{1,0:T(8,128)(2,1)S(1)}, bf16[16,128]{1,0:T(8,128)(2,1)S(1)}, u32[]{:S(2)}, u32[]{:S(2)}) collective-permute-start(bf16[16,128]{1,0:T(8,128)(2,1)S(1)} %pad.4.after_ref.after2_ref.after3_ref.picks_ref), channel_id=1, source_target_pairs={{0,2},{1,3},{2,0},{3,1},{4,6},{5,7},{6,4},{7,5},{8,10},{9,11},{10,... | collective-permute-start | bytes 12296 | tf_op jit(solution)/shard_map/ppermute | solution.py:295
  10.8 2.4 %collective-permute-done.4.theirs_ref.after_ref.after2_ref = bf16[256,256]{1,0:T(8,128)(2,1)S(1)} collective-permute-done((bf16[256,256]{1,0:T(8,128)(2,1)S(1)}, bf16[256,256]{1,0:T(8,128)(2,1)S(1)}, u32[]{:S(2)}, u32[]{:S(2)}) %collective-permute-start.4) | collective-permute-done | bytes 131104 | tf_op jit(solution)/shard_map/ppermute | solution.py:295
  13.6 2.8 %collective-permute-start.9 = (bf16[256,512]{1,0:T(8,128)(2,1)S(1)}, bf16[256,512]{1,0:T(8,128)(2,1)S(1)}, u32[]{:S(2)}, u32[]{:S(2)}) collective-permute-start(bf16[256,512]{1,0:T(8,128)(2,1)S(1)} %sum_1.1.after_ref), channel_id=1, source_target_pairs={{0,2},{1,3},{2,0},{3,1},{4,6},{5,7},{6,4},{7,5},{8,10},{9,11},{10,... | collective-permute-start | bytes 786440 | tf_op jit(solution)/shard_map/ppermute | solution.py:295
  16.5 1.7 %collective-permute-start.8 = (bf16[256,384]{1,0:T(8,128)(2,1)S(1)}, bf16[256,384]{1,0:T(8,128)(2,1)S(1)}, u32[]{:S(2)}, u32[]{:S(2)}) collective-permute-start(bf16[256,384]{1,0:T(8,128)(2,1)S(1)} %cut.6), channel_id=1, source_target_pairs={{0,1},{1,0},{2,3},{3,2},{4,5},{5,4},{6,7},{7,6},{8,9},{9,8},{10,11... | collective-permute-start | bytes 589832 | tf_op jit(solution)/shard_map/ppermute | solution.py:295
  18.3 4.5 %chosen.1 = (f32[128,128]{1,0:T(8,128)S(1)}, bf16[128,128]{1,0:T(8,128)(2,1)S(1)}, bf16[128,128]{1,0:T(8,128)(2,1)S(1)}, bf16[128,128]{1,0:T(8,128)(2,1)S(1)}) custom-call(s32[1]{0:T(128)} %bitcast.me_ref, bf16[64,128]{1,0:T(8,128)(2,1)S(1)} %pad_maximum_fusion.picks_ref.after_ref, bf16[256,4096]{1,0:T(8,128)(2,1)S(1)} %copy-done, ...), custom_call_target="tpu_custom_call" | custom-call | flops 1 | bytes 1 | tf_op jit(solution)/shard_map/chosen/pallas_call | solution.py:333
  23.2 0.6 collective-permute-start.6
  23.8 3.5 %collective-permute-start.7 = (bf16[128,128]{1,0:T(8,128)(2,1)S(1)}, bf16[128,128]{1,0:T(8,128)(2,1)S(1)}, u32[]{:S(2)}, u32[]{:S(2)}) collective-permute-start(bf16[128,128]{1,0:T(8,128)(2,1)S(1)} %get-tuple-element.11), channel_id=1, source_target_pairs={{0,3},{1,2},{2,1},{3,0},{4,7},{5,6},{6,5},{7,4},{8,11},{9,10},{10,... | collective-permute-start | bytes 98312 | tf_op jit(solution)/shard_map/ppermute | solution.py:295
  27.7 2.1 %collective-permute-done.9.after_ref.after2_ref.got1_ref = bf16[256,512]{1,0:T(8,128)(2,1)S(1)} collective-permute-done((bf16[256,512]{1,0:T(8,128)(2,1)S(1)}, bf16[256,512]{1,0:T(8,128)(2,1)S(1)}, u32[]{:S(2)}, u32[]{:S(2)}) %collective-permute-start.9) | collective-permute-done | bytes 262176 | tf_op jit(solution)/shard_map/ppermute | solution.py:295
  30.2 1.0 %collective-permute-start.10 = (bf16[256,384]{1,0:T(8,128)(2,1)S(1)}, bf16[256,384]{1,0:T(8,128)(2,1)S(1)}, u32[]{:S(2)}, u32[]{:S(2)}) collective-permute-start(bf16[256,384]{1,0:T(8,128)(2,1)S(1)} %cut.7), channel_id=1, source_target_pairs={{0,1},{1,0},{2,3},{3,2},{4,5},{5,4},{6,7},{7,6},{8,9},{9,8},{10,11... | collective-permute-start | bytes 589832 | tf_op jit(solution)/shard_map/ppermute | solution.py:295
  31.2 2.6 %collective-permute-start.14 = (bf16[384,512]{1,0:T(8,128)(2,1)S(1)}, bf16[384,512]{1,0:T(8,128)(2,1)S(1)}, u32[]{:S(2)}, u32[]{:S(2)}) collective-permute-start(bf16[384,512]{1,0:T(8,128)(2,1)S(1)} %hold.3.after_ref), channel_id=1, source_target_pairs={{0,2},{1,3},{2,0},{3,1},{4,6},{5,7},{6,4},{7,5},{8,10},{9,11},{10,... | collective-permute-start | bytes 1179656 | tf_op jit(solution)/shard_map/ppermute | solution.py:295
  33.8 7.3 %collective-permute-done.10.theirs_ref = bf16[256,384]{1,0:T(8,128)(2,1)S(1)} collective-permute-done((bf16[256,384]{1,0:T(8,128)(2,1)S(1)}, bf16[256,384]{1,0:T(8,128)(2,1)S(1)}, u32[]{:S(2)}, u32[]{:S(2)}) %collective-permute-start.10) | collective-permute-done | bytes 196640 | tf_op jit(solution)/shard_map/ppermute | solution.py:295
  41.8 1.1 %collective-permute-start.12 = (bf16[256,512]{1,0:T(8,128)(2,1)S(1)}, bf16[256,512]{1,0:T(8,128)(2,1)S(1)}, u32[]{:S(2)}, u32[]{:S(2)}) collective-permute-start(bf16[256,512]{1,0:T(8,128)(2,1)S(1)} %cut.9), channel_id=1, source_target_pairs={{0,1},{1,0},{2,3},{3,2},{4,5},{5,4},{6,7},{7,6},{8,9},{9,8},{10,11... | collective-permute-start | bytes 786440 | tf_op jit(solution)/shard_map/ppermute | solution.py:295
  42.9 1.1 %collective-permute-start.11 = (bf16[256,512]{1,0:T(8,128)(2,1)S(1)}, bf16[256,512]{1,0:T(8,128)(2,1)S(1)}, u32[]{:S(2)}, u32[]{:S(2)}) collective-permute-start(bf16[256,512]{1,0:T(8,128)(2,1)S(1)} %cut.8), channel_id=1, source_target_pairs={{0,1},{1,0},{2,3},{3,2},{4,5},{5,4},{6,7},{7,6},{8,9},{9,8},{10,11... | collective-permute-start | bytes 786440 | tf_op jit(solution)/shard_map/ppermute | solution.py:295
  44.0 9.4 %all-gather = bf16[1152,128]{1,0:T(8,128)(2,1)S(1)} all-gather(bf16[144,128]{1,0:T(8,128)(2,1)S(1)} %get-tuple-element.13), channel_id=2, replica_groups=mesh['replica'=8,'fsdp'=4] {'replica'}, dimensions={0}, use_global_device_ids=true | all-gather | bytes 331776 | tf_op jit(solution)/shard_map/all_gather | solution.py:300
  53.4 5.2 %update.1 = f32[1024,512]{1,0:T(8,128)} custom-call(bf16[8,144,128]{2,1,0:T(8,128)(2,1)S(1)} %bitcast.8, bf16[128,64]{1,0:T(8,128)(2,1)S(1)} %copy-done.10, bf16[128,64]{1,0:T(8,128)(2,1)S(1)} %copy-done.11, bf16[64,512]{1,0:T(8,128)(2,1)S(1)} %copy-done.4, bf16[64,512]{1,0:T(8,128)(2,1)S(1)} %copy-done.5, ...), custom_call_target="tpu_custom_call" | custom-call | flops 1 | bytes 1 | tf_op jit(solution)/shard_map/update/pallas_call | solution.py:421
  59.0 4.4 %collective-permute-done.11.ao1_ref = bf16[256,512]{1,0:T(8,128)(2,1)S(1)} collective-permute-done((bf16[256,512]{1,0:T(8,128)(2,1)S(1)}, bf16[256,512]{1,0:T(8,128)(2,1)S(1)}, u32[]{:S(2)}, u32[]{:S(2)}) %collective-permute-start.11) | collective-permute-done | bytes 262176 | tf_op jit(solution)/shard_map/ppermute | solution.py:295
  63.4 2.6 %base.1.base_ref = f32[1024,512]{1,0:T(8,128)S(1)} custom-call(s32[1]{0:T(128)} %bitcast.me_ref, bf16[16,128]{1,0:T(8,128)(2,1)S(1)} %pad.4.after_ref.after2_ref.after3_ref.picks_ref, f32[128,128]{1,0:T(8,128)S(1)} %get-tuple-element.12.after_ref.after2_ref.after3_ref.v_ref, bf16[1024,512]{1,0:T(8,128)(2,1)S(1)} %bitcast.7, bf16[256,4096]{1,0:T(8,128)(2,1)S(1)} %copy-done.1, ...), custom_call_target="tpu_custom_call" | custom-call | flops 1 | bytes 1 | tf_op jit(solution)/shard_map/base/pallas_call | solution.py:333
  66.0 0.9 %early.1.early_ref = bf16[1024,512]{1,0:T(8,128)(2,1)} custom-call(f32[1024,512]{1,0:T(8,128)S(1)} %base.1.base_ref, bf16[256,512]{1,0:T(8,128)(2,1)S(1)} %collective-permute-done.9.after_ref.after2_ref.got1_ref, bf16[384,512]{1,0:T(8,128)(2,1)S(1)} %collective-permute-done.14.got2_ref), custom_call_target="tpu_custom_call" | custom-call | flops 1 | bytes 1 | tf_op jit(solution)/shard_map/early/pallas_call | solution.py:432
  66.9 1.0 %collective-permute-done.13.got_ref = bf16[384,512]{1,0:T(8,128)(2,1)S(1)} collective-permute-done((bf16[384,512]{1,0:T(8,128)(2,1)S(1)}, bf16[384,512]{1,0:T(8,128)(2,1)S(1)}, u32[]{:S(2)}, u32[]{:S(2)}) %collective-permute-start.13) | collective-permute-done | bytes 393248 | tf_op jit(solution)/shard_map/ppermute | solution.py:295
  67.9 0.8 %last.1 = bf16[1024,512]{1,0:T(8,128)(2,1)} custom-call(f32[1024,512]{1,0:T(8,128)S(1)} %base.1.base_ref, bf16[384,512]{1,0:T(8,128)(2,1)S(1)} %collective-permute-done.13.got_ref, bf16[1024,512]{1,0:T(8,128)(2,1)} %early.1.early_ref), custom_call_target="tpu_custom_call", output_to_operand_aliasing={{}: (2, {})} | custom-call | flops 1 | bytes 1 | tf_op jit(solution)/shard_map/last/pallas_call | solution.py:442
  (51 shorter events, 3.1 us)
Async XLA Ops:
  0.6 12.6 %collective-permute-start.3 = (bf16[256,512]{1,0:T(8,128)(2,1)}, bf16[256,512]{1,0:T(8,128)(2,1)S(1)}, u32[]{:S(2)}, u32[]{:S(2)}) collective-permute-start(bf16[256,512]{1,0:T(8,128)(2,1)} %g_ref.9), channel_id=1, source_target_pairs={{0,1},{1,0},{2,3},{3,2},{4,5},{5,4},{6,7},{7,6},{8,9},{9,8},{10,11... | collective-permute-start | bytes 786440 | tf_op jit(solution)/shard_map/ppermute | solution.py:295
  6.1 7.1 %copy-start.2 = (bf16[256,512]{1,0:T(8,128)(2,1)S(1)}, bf16[256,512]{1,0:T(8,128)(2,1)}, u32[]{:S(2)}) copy-start(bf16[256,512]{1,0:T(8,128)(2,1)} %g_ref.9) | copy-start | bytes 786436
  6.1 7.0 %collective-permute-start.4 = (bf16[256,256]{1,0:T(8,128)(2,1)S(1)}, bf16[256,256]{1,0:T(8,128)(2,1)S(1)}, u32[]{:S(2)}, u32[]{:S(2)}) collective-permute-start(bf16[256,256]{1,0:T(8,128)(2,1)S(1)} %cut.5), channel_id=1, source_target_pairs={{0,1},{1,0},{2,3},{3,2},{4,5},{5,4},{6,7},{7,6},{8,9},{9,8},{10,11... | collective-permute-start | bytes 393224 | tf_op jit(solution)/shard_map/ppermute | solution.py:295
  6.2 10.2 %collective-permute-start = (bf16[16,128]{1,0:T(8,128)(2,1)S(1)}, bf16[16,128]{1,0:T(8,128)(2,1)S(1)}, u32[]{:S(2)}, u32[]{:S(2)}) collective-permute-start(bf16[16,128]{1,0:T(8,128)(2,1)S(1)} %pad.4.after_ref.after2_ref.after3_ref.picks_ref), channel_id=1, source_target_pairs={{0,1},{1,0},{2,3},{3,2},{4,5},{5,4},{6,7},{7,6},{8,9},{9,8},{10,11... | collective-permute-start | bytes 12296 | tf_op jit(solution)/shard_map/ppermute | solution.py:295
  8.2 8.2 %collective-permute-start.1 = (bf16[16,128]{1,0:T(8,128)(2,1)S(1)}, bf16[16,128]{1,0:T(8,128)(2,1)S(1)}, u32[]{:S(2)}, u32[]{:S(2)}) collective-permute-start(bf16[16,128]{1,0:T(8,128)(2,1)S(1)} %pad.4.after_ref.after2_ref.after3_ref.picks_ref), channel_id=1, source_target_pairs={{0,2},{1,3},{2,0},{3,1},{4,6},{5,7},{6,4},{7,5},{8,10},{9,11},{10,... | collective-permute-start | bytes 12296 | tf_op jit(solution)/shard_map/ppermute | solution.py:295
  10.8 5.6 %collective-permute-start.2 = (bf16[16,128]{1,0:T(8,128)(2,1)S(1)}, bf16[16,128]{1,0:T(8,128)(2,1)S(1)}, u32[]{:S(2)}, u32[]{:S(2)}) collective-permute-start(bf16[16,128]{1,0:T(8,128)(2,1)S(1)} %pad.4.after_ref.after2_ref.after3_ref.picks_ref), channel_id=1, source_target_pairs={{0,3},{1,2},{2,1},{3,0},{4,7},{5,6},{6,5},{7,4},{8,11},{9,10},{10,... | collective-permute-start | bytes 12296 | tf_op jit(solution)/shard_map/ppermute | solution.py:295
  13.6 4.7 %copy-start.3 = (bf16[1,1024,512]{2,1,0:T(8,128)(2,1)S(1)}, bf16[1,1024,512]{2,1,0:T(8,128)(2,1)}, u32[]{:S(2)}) copy-start(bf16[1,1024,512]{2,1,0:T(8,128)(2,1)} %param.14) | copy-start | bytes 3145732
  13.6 4.7 %copy-start.4 = (bf16[64,512]{1,0:T(8,128)(2,1)S(1)}, bf16[64,512]{1,0:T(8,128)(2,1)}, u32[]{:S(2)}) copy-start(bf16[64,512]{1,0:T(8,128)(2,1)} %constant.25.clone.csth_ref) | copy-start | bytes 196612
  13.6 4.7 %copy-start.5 = (bf16[64,512]{1,0:T(8,128)(2,1)S(1)}, bf16[64,512]{1,0:T(8,128)(2,1)}, u32[]{:S(2)}) copy-start(bf16[64,512]{1,0:T(8,128)(2,1)} %constant.26.clone.cstl_ref) | copy-start | bytes 196612
  13.6 16.1 %collective-permute-start.9 = (bf16[256,512]{1,0:T(8,128)(2,1)S(1)}, bf16[256,512]{1,0:T(8,128)(2,1)S(1)}, u32[]{:S(2)}, u32[]{:S(2)}) collective-permute-start(bf16[256,512]{1,0:T(8,128)(2,1)S(1)} %sum_1.1.after_ref), channel_id=1, source_target_pairs={{0,2},{1,3},{2,0},{3,1},{4,6},{5,7},{6,4},{7,5},{8,10},{9,11},{10,... | collective-permute-start | bytes 786440 | tf_op jit(solution)/shard_map/ppermute | solution.py:295
  16.5 10.7 %collective-permute-start.8 = (bf16[256,384]{1,0:T(8,128)(2,1)S(1)}, bf16[256,384]{1,0:T(8,128)(2,1)S(1)}, u32[]{:S(2)}, u32[]{:S(2)}) collective-permute-start(bf16[256,384]{1,0:T(8,128)(2,1)S(1)} %cut.6), channel_id=1, source_target_pairs={{0,1},{1,0},{2,3},{3,2},{4,5},{5,4},{6,7},{7,6},{8,9},{9,8},{10,11... | collective-permute-start | bytes 589832 | tf_op jit(solution)/shard_map/ppermute | solution.py:295
  22.8 7.0 %collective-permute-start.5 = (bf16[128,128]{1,0:T(8,128)(2,1)S(1)}, bf16[128,128]{1,0:T(8,128)(2,1)S(1)}, u32[]{:S(2)}, u32[]{:S(2)}) collective-permute-start(bf16[128,128]{1,0:T(8,128)(2,1)S(1)} %get-tuple-element.9.after_ref), channel_id=1, source_target_pairs={{0,1},{1,0},{2,3},{3,2},{4,5},{5,4},{6,7},{7,6},{8,9},{9,8},{10,11... | collective-permute-start | bytes 98312 | tf_op jit(solution)/shard_map/ppermute | solution.py:295
  23.2 6.9 %collective-permute-start.6 = (bf16[128,128]{1,0:T(8,128)(2,1)S(1)}, bf16[128,128]{1,0:T(8,128)(2,1)S(1)}, u32[]{:S(2)}, u32[]{:S(2)}) collective-permute-start(bf16[128,128]{1,0:T(8,128)(2,1)S(1)} %get-tuple-element.10), channel_id=1, source_target_pairs={{0,2},{1,3},{2,0},{3,1},{4,6},{5,7},{6,4},{7,5},{8,10},{9,11},{10,... | collective-permute-start | bytes 98312 | tf_op jit(solution)/shard_map/ppermute | solution.py:295
  23.8 6.4 %copy-start.1 = (bf16[256,4096]{1,0:T(8,128)(2,1)S(1)}, bf16[256,4096]{1,0:T(8,128)(2,1)}, u32[]{:S(2)}) copy-start(bf16[256,4096]{1,0:T(8,128)(2,1)} %acts_ref.19) | copy-start | bytes 6291460
  23.8 6.3 %collective-permute-start.7 = (bf16[128,128]{1,0:T(8,128)(2,1)S(1)}, bf16[128,128]{1,0:T(8,128)(2,1)S(1)}, u32[]{:S(2)}, u32[]{:S(2)}) collective-permute-start(bf16[128,128]{1,0:T(8,128)(2,1)S(1)} %get-tuple-element.11), channel_id=1, source_target_pairs={{0,3},{1,2},{2,1},{3,0},{4,7},{5,6},{6,5},{7,4},{8,11},{9,10},{10,... | collective-permute-start | bytes 98312 | tf_op jit(solution)/shard_map/ppermute | solution.py:295
  30.2 10.9 %collective-permute-start.10 = (bf16[256,384]{1,0:T(8,128)(2,1)S(1)}, bf16[256,384]{1,0:T(8,128)(2,1)S(1)}, u32[]{:S(2)}, u32[]{:S(2)}) collective-permute-start(bf16[256,384]{1,0:T(8,128)(2,1)S(1)} %cut.7), channel_id=1, source_target_pairs={{0,1},{1,0},{2,3},{3,2},{4,5},{5,4},{6,7},{7,6},{8,9},{9,8},{10,11... | collective-permute-start | bytes 589832 | tf_op jit(solution)/shard_map/ppermute | solution.py:295
  31.2 34.8 %collective-permute-start.14 = (bf16[384,512]{1,0:T(8,128)(2,1)S(1)}, bf16[384,512]{1,0:T(8,128)(2,1)S(1)}, u32[]{:S(2)}, u32[]{:S(2)}) collective-permute-start(bf16[384,512]{1,0:T(8,128)(2,1)S(1)} %hold.3.after_ref), channel_id=1, source_target_pairs={{0,2},{1,3},{2,0},{3,1},{4,6},{5,7},{6,4},{7,5},{8,10},{9,11},{10,... | collective-permute-start | bytes 1179656 | tf_op jit(solution)/shard_map/ppermute | solution.py:295
  41.6 26.3 %collective-permute-start.13 = (bf16[384,512]{1,0:T(8,128)(2,1)S(1)}, bf16[384,512]{1,0:T(8,128)(2,1)S(1)}, u32[]{:S(2)}, u32[]{:S(2)}) collective-permute-start(bf16[384,512]{1,0:T(8,128)(2,1)S(1)} %sum_3.1.after_ref.after2_ref.after3_ref), channel_id=1, source_target_pairs={{0,2},{1,3},{2,0},{3,1},{4,6},{5,7},{6,4},{7,5},{8,10},{9,11},{10,... | collective-permute-start | bytes 1179656 | tf_op jit(solution)/shard_map/ppermute | solution.py:295
  41.7 11.7 %copy-start.10 = (bf16[128,64]{1,0:T(8,128)(2,1)S(1)}, bf16[128,64]{1,0:T(8,128)(2,1)}, u32[]{:S(2)}) copy-start(bf16[128,64]{1,0:T(8,128)(2,1)} %constant.29.clone.c2th_ref) | copy-start | bytes 49156
  41.7 11.7 %copy-start.11 = (bf16[128,64]{1,0:T(8,128)(2,1)S(1)}, bf16[128,64]{1,0:T(8,128)(2,1)}, u32[]{:S(2)}) copy-start(bf16[128,64]{1,0:T(8,128)(2,1)} %constant.30.clone.c2tl_ref) | copy-start | bytes 49156
  41.8 17.3 %collective-permute-start.12 = (bf16[256,512]{1,0:T(8,128)(2,1)S(1)}, bf16[256,512]{1,0:T(8,128)(2,1)S(1)}, u32[]{:S(2)}, u32[]{:S(2)}) collective-permute-start(bf16[256,512]{1,0:T(8,128)(2,1)S(1)} %cut.9), channel_id=1, source_target_pairs={{0,1},{1,0},{2,3},{3,2},{4,5},{5,4},{6,7},{7,6},{8,9},{9,8},{10,11... | collective-permute-start | bytes 786440 | tf_op jit(solution)/shard_map/ppermute | solution.py:295
  42.9 20.5 %copy-start.6 = (bf16[256,64]{1,0:T(8,128)(2,1)S(1)}, bf16[256,64]{1,0:T(8,128)(2,1)}, u32[]{:S(2)}) copy-start(bf16[256,64]{1,0:T(8,128)(2,1)} %constant.27.clone.c4th_ref) | copy-start | bytes 98308
  42.9 20.5 %copy-start.7 = (bf16[256,64]{1,0:T(8,128)(2,1)S(1)}, bf16[256,64]{1,0:T(8,128)(2,1)}, u32[]{:S(2)}) copy-start(bf16[256,64]{1,0:T(8,128)(2,1)} %constant.28.clone.c4tl_ref) | copy-start | bytes 98308
  42.9 20.5 %collective-permute-start.11 = (bf16[256,512]{1,0:T(8,128)(2,1)S(1)}, bf16[256,512]{1,0:T(8,128)(2,1)S(1)}, u32[]{:S(2)}, u32[]{:S(2)}) collective-permute-start(bf16[256,512]{1,0:T(8,128)(2,1)S(1)} %cut.8), channel_id=1, source_target_pairs={{0,1},{1,0},{2,3},{3,2},{4,5},{5,4},{6,7},{7,6},{8,9},{9,8},{10,11... | collective-permute-start | bytes 786440 | tf_op jit(solution)/shard_map/ppermute | solution.py:295
  (3 other events, 10.9 us)

commit v6 on v4

--- a/solution.py
+++ b/solution.py
@@ -401,7 +401,7 @@
     sum_3 = sums(lead + second, cols_3, sum_2, "sum_3")
     got_3 = swap_near(sum_3, 2)
     cols_own = [
-        swap_near(cut([(1, n * (shard // 2), shard // 2)], sum_3, sum_3, sum_3), 1) for n in range(2)
+        swap_near(cut([(1, n * (shard // 2), shard // 2)], (sum_2, sum_3)[n], sum_2, sum_2), 1) for n in range(2)
     ]
     base = call(
         functools.partial(base_kernel, top),

time: 68.9 us -> 68.9 us (level)
  no operation moved by 1% of the time
where the time goes in v6:
time: 68.9 us; the launch traced here: 68.7 us
  starting transfers between devices  22.5 us (33%)
  waiting for transfers between devices  18.1 us (26%)
  Pallas kernels  15.5 us (22%)
  blocking collectives  9.32 us (14%)
  local copies, waits for them, and re-layouts  1.76 us (3%)
  between operations  0.88 us (1%)
  other arithmetic  0.69 us (1%)
    ppermute x15, starting transfers between devices, swap(): return lax.ppermute(x, axis, [(i, i ^ bit) for i in range(size)])  22.5 us
    ppermute x15, waiting for transfers between devices, swap(): return lax.ppermute(x, axis, [(i, i ^ bit) for i in range(size)])  18.1 us
    all_gather x1, blocking collectives, gather_replicas(): return lax.all_gather(x, 'replica', axis=0, tiled=False)  9.32 us
    pallas_call x6, Pallas kernels, call(): pl.pallas_call(kernel, out_shape=outs, in_specs=[{'s': SMEM, 'a': ANY, 'h...  8.41 us
    pallas_call x1, Pallas kernels, body(): pl.pallas_call(functools.partial(update_kernel, top, crows), grid=(replic...  5.16 us
    unnamed x24, local copies, waits for them, and re-layouts  1.66 us
  transfers between devices with their start and end apart: 15, of which 6 were waited for; matrix products, arithmetic and copies ran while one was open for 1% of the time, Pallas kernels for 21%

profile of v6, /device:TPU:0, one launch (start us, length us, event | category | flops | bytes accessed | tf_op | source)
XLA Modules:
  0.0 68.7 jit_solution(11390485391669694806)
XLA Ops:
  0.6 3.1 %collective-permute-start.3 = (bf16[256,512]{1,0:T(8,128)(2,1)}, bf16[256,512]{1,0:T(8,128)(2,1)S(1)}, u32[]{:S(2)}, u32[]{:S(2)}) collective-permute-start(bf16[256,512]{1,0:T(8,128)(2,1)} %g_ref.9), channel_id=1, source_target_pairs={{0,1},{1,0},{2,3},{3,2},{4,5},{5,4},{6,7},{7,6},{8,9},{9,8},{10,11... | collective-permute-start | bytes 786440 | tf_op jit(solution)/shard_map/ppermute | solution.py:295
  3.7 0.7 %convert_bitcast_fusion = bf16[16,8]{0,1:T(8,128)(2,1)S(1)} fusion(s32[1,16,8]{1,2,0:T(8,128)} %param.15), kind=kLoop, calls=%fused_computation.1 | loop fusion | flops 128 | bytes 768 | tf_op jit(solution)/shard_map/convert_element_type | solution.py:325
  4.5 1.6 %copy-done = bf16[256,4096]{1,0:T(8,128)(2,1)S(1)} copy-done((bf16[256,4096]{1,0:T(8,128)(2,1)S(1)}, bf16[256,4096]{1,0:T(8,128)(2,1)}, u32[]{:S(2)}) %copy-start) | copy-done | bytes 2097176
  6.2 2.0 %collective-permute-start = (bf16[16,128]{1,0:T(8,128)(2,1)S(1)}, bf16[16,128]{1,0:T(8,128)(2,1)S(1)}, u32[]{:S(2)}, u32[]{:S(2)}) collective-permute-start(bf16[16,128]{1,0:T(8,128)(2,1)S(1)} %pad.4.after_ref.after2_ref.after3_ref.picks_ref), channel_id=1, source_target_pairs={{0,1},{1,0},{2,3},{3,2},{4,5},{5,4},{6,7},{7,6},{8,9},{9,8},{10,11... | collective-permute-start | bytes 12296 | tf_op jit(solution)/shard_map/ppermute | solution.py:295
  8.2 2.6 %collective-permute-start.1 = (bf16[16,128]{1,0:T(8,128)(2,1)S(1)}, bf16[16,128]{1,0:T(8,128)(2,1)S(1)}, u32[]{:S(2)}, u32[]{:S(2)}) collective-permute-start(bf16[16,128]{1,0:T(8,128)(2,1)S(1)} %pad.4.after_ref.after2_ref.after3_ref.picks_ref), channel_id=1, source_target_pairs={{0,2},{1,3},{2,0},{3,1},{4,6},{5,7},{6,4},{7,5},{8,10},{9,11},{10,... | collective-permute-start | bytes 12296 | tf_op jit(solution)/shard_map/ppermute | solution.py:295
  10.8 2.4 %collective-permute-done.4.theirs_ref.after_ref.after2_ref = bf16[256,256]{1,0:T(8,128)(2,1)S(1)} collective-permute-done((bf16[256,256]{1,0:T(8,128)(2,1)S(1)}, bf16[256,256]{1,0:T(8,128)(2,1)S(1)}, u32[]{:S(2)}, u32[]{:S(2)}) %collective-permute-start.4) | collective-permute-done | bytes 131104 | tf_op jit(solution)/shard_map/ppermute | solution.py:295
  13.6 2.8 %collective-permute-start.9 = (bf16[256,512]{1,0:T(8,128)(2,1)S(1)}, bf16[256,512]{1,0:T(8,128)(2,1)S(1)}, u32[]{:S(2)}, u32[]{:S(2)}) collective-permute-start(bf16[256,512]{1,0:T(8,128)(2,1)S(1)} %sum_1.1.after_ref), channel_id=1, source_target_pairs={{0,2},{1,3},{2,0},{3,1},{4,6},{5,7},{6,4},{7,5},{8,10},{9,11},{10,... | collective-permute-start | bytes 786440 | tf_op jit(solution)/shard_map/ppermute | solution.py:295
  16.5 1.7 %collective-permute-start.8 = (bf16[256,384]{1,0:T(8,128)(2,1)S(1)}, bf16[256,384]{1,0:T(8,128)(2,1)S(1)}, u32[]{:S(2)}, u32[]{:S(2)}) collective-permute-start(bf16[256,384]{1,0:T(8,128)(2,1)S(1)} %cut.6), channel_id=1, source_target_pairs={{0,1},{1,0},{2,3},{3,2},{4,5},{5,4},{6,7},{7,6},{8,9},{9,8},{10,11... | collective-permute-start | bytes 589832 | tf_op jit(solution)/shard_map/ppermute | solution.py:295
  18.3 4.5 %chosen.1 = (f32[128,128]{1,0:T(8,128)S(1)}, bf16[128,128]{1,0:T(8,128)(2,1)S(1)}, bf16[128,128]{1,0:T(8,128)(2,1)S(1)}, bf16[128,128]{1,0:T(8,128)(2,1)S(1)}) custom-call(s32[1]{0:T(128)} %bitcast.me_ref, bf16[64,128]{1,0:T(8,128)(2,1)S(1)} %pad_maximum_fusion.picks_ref.after_ref, bf16[256,4096]{1,0:T(8,128)(2,1)S(1)} %copy-done, ...), custom_call_target="tpu_custom_call" | custom-call | flops 1 | bytes 1 | tf_op jit(solution)/shard_map/chosen/pallas_call | solution.py:333
  23.2 0.6 collective-permute-start.6
  23.8 3.4 %collective-permute-start.7 = (bf16[128,128]{1,0:T(8,128)(2,1)S(1)}, bf16[128,128]{1,0:T(8,128)(2,1)S(1)}, u32[]{:S(2)}, u32[]{:S(2)}) collective-permute-start(bf16[128,128]{1,0:T(8,128)(2,1)S(1)} %get-tuple-element.11), channel_id=1, source_target_pairs={{0,3},{1,2},{2,1},{3,0},{4,7},{5,6},{6,5},{7,4},{8,11},{9,10},{10,... | collective-permute-start | bytes 98312 | tf_op jit(solution)/shard_map/ppermute | solution.py:295
  27.2 2.5 %collective-permute-done.9.after_ref.got1_ref = bf16[256,512]{1,0:T(8,128)(2,1)S(1)} collective-permute-done((bf16[256,512]{1,0:T(8,128)(2,1)S(1)}, bf16[256,512]{1,0:T(8,128)(2,1)S(1)}, u32[]{:S(2)}, u32[]{:S(2)}) %collective-permute-start.9) | collective-permute-done | bytes 262176 | tf_op jit(solution)/shard_map/ppermute | solution.py:295
  30.4 0.8 %collective-permute-start.11 = (bf16[256,384]{1,0:T(8,128)(2,1)S(1)}, bf16[256,384]{1,0:T(8,128)(2,1)S(1)}, u32[]{:S(2)}, u32[]{:S(2)}) collective-permute-start(bf16[256,384]{1,0:T(8,128)(2,1)S(1)} %cut.8), channel_id=1, source_target_pairs={{0,1},{1,0},{2,3},{3,2},{4,5},{5,4},{6,7},{7,6},{8,9},{9,8},{10,11... | collective-permute-start | bytes 589832 | tf_op jit(solution)/shard_map/ppermute | solution.py:295
  31.2 2.6 %collective-permute-start.14 = (bf16[384,512]{1,0:T(8,128)(2,1)S(1)}, bf16[384,512]{1,0:T(8,128)(2,1)S(1)}, u32[]{:S(2)}, u32[]{:S(2)}) collective-permute-start(bf16[384,512]{1,0:T(8,128)(2,1)S(1)} %hold.1.after_ref.after2_ref.after3_ref), channel_id=1, source_target_pairs={{0,2},{1,3},{2,0},{3,1},{4,6},{5,7},{6,4},{7,5},{8,10},{9,11},{10,... | collective-permute-start | bytes 1179656 | tf_op jit(solution)/shard_map/ppermute | solution.py:295
  33.8 7.4 %collective-permute-done.11.theirs_ref = bf16[256,384]{1,0:T(8,128)(2,1)S(1)} collective-permute-done((bf16[256,384]{1,0:T(8,128)(2,1)S(1)}, bf16[256,384]{1,0:T(8,128)(2,1)S(1)}, u32[]{:S(2)}, u32[]{:S(2)}) %collective-permute-start.11) | collective-permute-done | bytes 196640 | tf_op jit(solution)/shard_map/ppermute | solution.py:295
  41.9 1.0 %collective-permute-start.10 = (bf16[256,512]{1,0:T(8,128)(2,1)S(1)}, bf16[256,512]{1,0:T(8,128)(2,1)S(1)}, u32[]{:S(2)}, u32[]{:S(2)}) collective-permute-start(bf16[256,512]{1,0:T(8,128)(2,1)S(1)} %cut.7), channel_id=1, source_target_pairs={{0,1},{1,0},{2,3},{3,2},{4,5},{5,4},{6,7},{7,6},{8,9},{9,8},{10,11... | collective-permute-start | bytes 786440 | tf_op jit(solution)/shard_map/ppermute | solution.py:295
  42.9 1.2 %collective-permute-start.12 = (bf16[256,512]{1,0:T(8,128)(2,1)S(1)}, bf16[256,512]{1,0:T(8,128)(2,1)S(1)}, u32[]{:S(2)}, u32[]{:S(2)}) collective-permute-start(bf16[256,512]{1,0:T(8,128)(2,1)S(1)} %cut.9), channel_id=1, source_target_pairs={{0,1},{1,0},{2,3},{3,2},{4,5},{5,4},{6,7},{7,6},{8,9},{9,8},{10,11... | collective-permute-start | bytes 786440 | tf_op jit(solution)/shard_map/ppermute | solution.py:295
  44.1 9.3 %all-gather = bf16[1152,128]{1,0:T(8,128)(2,1)S(1)} all-gather(bf16[144,128]{1,0:T(8,128)(2,1)S(1)} %get-tuple-element.13), channel_id=2, replica_groups=mesh['replica'=8,'fsdp'=4] {'replica'}, dimensions={0}, use_global_device_ids=true | all-gather | bytes 331776 | tf_op jit(solution)/shard_map/all_gather | solution.py:300
  53.4 5.2 %update.1 = f32[1024,512]{1,0:T(8,128)} custom-call(bf16[8,144,128]{2,1,0:T(8,128)(2,1)S(1)} %bitcast.8, bf16[128,64]{1,0:T(8,128)(2,1)S(1)} %copy-done.10, bf16[128,64]{1,0:T(8,128)(2,1)S(1)} %copy-done.11, bf16[64,512]{1,0:T(8,128)(2,1)S(1)} %copy-done.4, bf16[64,512]{1,0:T(8,128)(2,1)S(1)} %copy-done.5, ...), custom_call_target="tpu_custom_call" | custom-call | flops 1 | bytes 1 | tf_op jit(solution)/shard_map/update/pallas_call | solution.py:417
  59.0 4.4 %collective-permute-done.12.ao2_ref = bf16[256,512]{1,0:T(8,128)(2,1)S(1)} collective-permute-done((bf16[256,512]{1,0:T(8,128)(2,1)S(1)}, bf16[256,512]{1,0:T(8,128)(2,1)S(1)}, u32[]{:S(2)}, u32[]{:S(2)}) %collective-permute-start.12) | collective-permute-done | bytes 262176 | tf_op jit(solution)/shard_map/ppermute | solution.py:295
  63.4 2.6 %base.1.base_ref = f32[1024,512]{1,0:T(8,128)S(1)} custom-call(s32[1]{0:T(128)} %bitcast.me_ref, bf16[16,128]{1,0:T(8,128)(2,1)S(1)} %pad.4.after_ref.after2_ref.after3_ref.picks_ref, f32[128,128]{1,0:T(8,128)S(1)} %get-tuple-element.12.after2_ref.after_ref.after3_ref.v_ref, bf16[1024,512]{1,0:T(8,128)(2,1)S(1)} %bitcast.7, bf16[256,4096]{1,0:T(8,128)(2,1)S(1)} %copy-done.1, ...), custom_call_target="tpu_custom_call" | custom-call | flops 1 | bytes 1 | tf_op jit(solution)/shard_map/base/pallas_call | solution.py:333
  66.0 0.9 %early.1.early_ref = bf16[1024,512]{1,0:T(8,128)(2,1)} custom-call(f32[1024,512]{1,0:T(8,128)S(1)} %base.1.base_ref, bf16[256,512]{1,0:T(8,128)(2,1)S(1)} %collective-permute-done.9.after_ref.got1_ref, bf16[384,512]{1,0:T(8,128)(2,1)S(1)} %collective-permute-done.14.got2_ref), custom_call_target="tpu_custom_call" | custom-call | flops 1 | bytes 1 | tf_op jit(solution)/shard_map/early/pallas_call | solution.py:428
  66.9 1.0 %collective-permute-done.13.got_ref = bf16[384,512]{1,0:T(8,128)(2,1)S(1)} collective-permute-done((bf16[384,512]{1,0:T(8,128)(2,1)S(1)}, bf16[384,512]{1,0:T(8,128)(2,1)S(1)}, u32[]{:S(2)}, u32[]{:S(2)}) %collective-permute-start.13) | collective-permute-done | bytes 393248 | tf_op jit(solution)/shard_map/ppermute | solution.py:295
  67.9 0.8 %last.1 = bf16[1024,512]{1,0:T(8,128)(2,1)} custom-call(f32[1024,512]{1,0:T(8,128)S(1)} %base.1.base_ref, bf16[384,512]{1,0:T(8,128)(2,1)S(1)} %collective-permute-done.13.got_ref, bf16[1024,512]{1,0:T(8,128)(2,1)} %early.1.early_ref), custom_call_target="tpu_custom_call", output_to_operand_aliasing={{}: (2, {})} | custom-call | flops 1 | bytes 1 | tf_op jit(solution)/shard_map/last/pallas_call | solution.py:438
  (50 shorter events, 2.7 us)
Async XLA Ops:
  0.6 12.6 %collective-permute-start.3 = (bf16[256,512]{1,0:T(8,128)(2,1)}, bf16[256,512]{1,0:T(8,128)(2,1)S(1)}, u32[]{:S(2)}, u32[]{:S(2)}) collective-permute-start(bf16[256,512]{1,0:T(8,128)(2,1)} %g_ref.9), channel_id=1, source_target_pairs={{0,1},{1,0},{2,3},{3,2},{4,5},{5,4},{6,7},{7,6},{8,9},{9,8},{10,11... | collective-permute-start | bytes 786440 | tf_op jit(solution)/shard_map/ppermute | solution.py:295
  6.1 7.1 %copy-start.2 = (bf16[256,512]{1,0:T(8,128)(2,1)S(1)}, bf16[256,512]{1,0:T(8,128)(2,1)}, u32[]{:S(2)}) copy-start(bf16[256,512]{1,0:T(8,128)(2,1)} %g_ref.9) | copy-start | bytes 786436
  6.1 7.0 %collective-permute-start.4 = (bf16[256,256]{1,0:T(8,128)(2,1)S(1)}, bf16[256,256]{1,0:T(8,128)(2,1)S(1)}, u32[]{:S(2)}, u32[]{:S(2)}) collective-permute-start(bf16[256,256]{1,0:T(8,128)(2,1)S(1)} %cut.5), channel_id=1, source_target_pairs={{0,1},{1,0},{2,3},{3,2},{4,5},{5,4},{6,7},{7,6},{8,9},{9,8},{10,11... | collective-permute-start | bytes 393224 | tf_op jit(solution)/shard_map/ppermute | solution.py:295
  6.2 10.2 %collective-permute-start = (bf16[16,128]{1,0:T(8,128)(2,1)S(1)}, bf16[16,128]{1,0:T(8,128)(2,1)S(1)}, u32[]{:S(2)}, u32[]{:S(2)}) collective-permute-start(bf16[16,128]{1,0:T(8,128)(2,1)S(1)} %pad.4.after_ref.after2_ref.after3_ref.picks_ref), channel_id=1, source_target_pairs={{0,1},{1,0},{2,3},{3,2},{4,5},{5,4},{6,7},{7,6},{8,9},{9,8},{10,11... | collective-permute-start | bytes 12296 | tf_op jit(solution)/shard_map/ppermute | solution.py:295
  8.2 8.2 %collective-permute-start.1 = (bf16[16,128]{1,0:T(8,128)(2,1)S(1)}, bf16[16,128]{1,0:T(8,128)(2,1)S(1)}, u32[]{:S(2)}, u32[]{:S(2)}) collective-permute-start(bf16[16,128]{1,0:T(8,128)(2,1)S(1)} %pad.4.after_ref.after2_ref.after3_ref.picks_ref), channel_id=1, source_target_pairs={{0,2},{1,3},{2,0},{3,1},{4,6},{5,7},{6,4},{7,5},{8,10},{9,11},{10,... | collective-permute-start | bytes 12296 | tf_op jit(solution)/shard_map/ppermute | solution.py:295
  10.8 5.6 %collective-permute-start.2 = (bf16[16,128]{1,0:T(8,128)(2,1)S(1)}, bf16[16,128]{1,0:T(8,128)(2,1)S(1)}, u32[]{:S(2)}, u32[]{:S(2)}) collective-permute-start(bf16[16,128]{1,0:T(8,128)(2,1)S(1)} %pad.4.after_ref.after2_ref.after3_ref.picks_ref), channel_id=1, source_target_pairs={{0,3},{1,2},{2,1},{3,0},{4,7},{5,6},{6,5},{7,4},{8,11},{9,10},{10,... | collective-permute-start | bytes 12296 | tf_op jit(solution)/shard_map/ppermute | solution.py:295
  13.6 4.7 %copy-start.3 = (bf16[1,1024,512]{2,1,0:T(8,128)(2,1)S(1)}, bf16[1,1024,512]{2,1,0:T(8,128)(2,1)}, u32[]{:S(2)}) copy-start(bf16[1,1024,512]{2,1,0:T(8,128)(2,1)} %param.14) | copy-start | bytes 3145732
  13.6 4.7 %copy-start.4 = (bf16[64,512]{1,0:T(8,128)(2,1)S(1)}, bf16[64,512]{1,0:T(8,128)(2,1)}, u32[]{:S(2)}) copy-start(bf16[64,512]{1,0:T(8,128)(2,1)} %constant.25.clone.csth_ref) | copy-start | bytes 196612
  13.6 4.7 %copy-start.5 = (bf16[64,512]{1,0:T(8,128)(2,1)S(1)}, bf16[64,512]{1,0:T(8,128)(2,1)}, u32[]{:S(2)}) copy-start(bf16[64,512]{1,0:T(8,128)(2,1)} %constant.26.clone.cstl_ref) | copy-start | bytes 196612
  13.6 16.1 %collective-permute-start.9 = (bf16[256,512]{1,0:T(8,128)(2,1)S(1)}, bf16[256,512]{1,0:T(8,128)(2,1)S(1)}, u32[]{:S(2)}, u32[]{:S(2)}) collective-permute-start(bf16[256,512]{1,0:T(8,128)(2,1)S(1)} %sum_1.1.after_ref), channel_id=1, source_target_pairs={{0,2},{1,3},{2,0},{3,1},{4,6},{5,7},{6,4},{7,5},{8,10},{9,11},{10,... | collective-permute-start | bytes 786440 | tf_op jit(solution)/shard_map/ppermute | solution.py:295
  16.5 10.7 %collective-permute-start.8 = (bf16[256,384]{1,0:T(8,128)(2,1)S(1)}, bf16[256,384]{1,0:T(8,128)(2,1)S(1)}, u32[]{:S(2)}, u32[]{:S(2)}) collective-permute-start(bf16[256,384]{1,0:T(8,128)(2,1)S(1)} %cut.6), channel_id=1, source_target_pairs={{0,1},{1,0},{2,3},{3,2},{4,5},{5,4},{6,7},{7,6},{8,9},{9,8},{10,11... | collective-permute-start | bytes 589832 | tf_op jit(solution)/shard_map/ppermute | solution.py:295
  22.8 7.5 %copy-start.1 = (bf16[256,4096]{1,0:T(8,128)(2,1)S(1)}, bf16[256,4096]{1,0:T(8,128)(2,1)}, u32[]{:S(2)}) copy-start(bf16[256,4096]{1,0:T(8,128)(2,1)} %acts_ref.19) | copy-start | bytes 6291460
  22.8 7.5 %collective-permute-start.5 = (bf16[128,128]{1,0:T(8,128)(2,1)S(1)}, bf16[128,128]{1,0:T(8,128)(2,1)S(1)}, u32[]{:S(2)}, u32[]{:S(2)}) collective-permute-start(bf16[128,128]{1,0:T(8,128)(2,1)S(1)} %get-tuple-element.9), channel_id=1, source_target_pairs={{0,1},{1,0},{2,3},{3,2},{4,5},{5,4},{6,7},{7,6},{8,9},{9,8},{10,11... | collective-permute-start | bytes 98312 | tf_op jit(solution)/shard_map/ppermute | solution.py:295
  23.2 7.1 %collective-permute-start.6 = (bf16[128,128]{1,0:T(8,128)(2,1)S(1)}, bf16[128,128]{1,0:T(8,128)(2,1)S(1)}, u32[]{:S(2)}, u32[]{:S(2)}) collective-permute-start(bf16[128,128]{1,0:T(8,128)(2,1)S(1)} %get-tuple-element.10), channel_id=1, source_target_pairs={{0,2},{1,3},{2,0},{3,1},{4,6},{5,7},{6,4},{7,5},{8,10},{9,11},{10,... | collective-permute-start | bytes 98312 | tf_op jit(solution)/shard_map/ppermute | solution.py:295
  23.8 6.5 %collective-permute-start.7 = (bf16[128,128]{1,0:T(8,128)(2,1)S(1)}, bf16[128,128]{1,0:T(8,128)(2,1)S(1)}, u32[]{:S(2)}, u32[]{:S(2)}) collective-permute-start(bf16[128,128]{1,0:T(8,128)(2,1)S(1)} %get-tuple-element.11), channel_id=1, source_target_pairs={{0,3},{1,2},{2,1},{3,0},{4,7},{5,6},{6,5},{7,4},{8,11},{9,10},{10,... | collective-permute-start | bytes 98312 | tf_op jit(solution)/shard_map/ppermute | solution.py:295
  30.4 10.9 %collective-permute-start.11 = (bf16[256,384]{1,0:T(8,128)(2,1)S(1)}, bf16[256,384]{1,0:T(8,128)(2,1)S(1)}, u32[]{:S(2)}, u32[]{:S(2)}) collective-permute-start(bf16[256,384]{1,0:T(8,128)(2,1)S(1)} %cut.8), channel_id=1, source_target_pairs={{0,1},{1,0},{2,3},{3,2},{4,5},{5,4},{6,7},{7,6},{8,9},{9,8},{10,11... | collective-permute-start | bytes 589832 | tf_op jit(solution)/shard_map/ppermute | solution.py:295
  31.2 34.8 %collective-permute-start.14 = (bf16[384,512]{1,0:T(8,128)(2,1)S(1)}, bf16[384,512]{1,0:T(8,128)(2,1)S(1)}, u32[]{:S(2)}, u32[]{:S(2)}) collective-permute-start(bf16[384,512]{1,0:T(8,128)(2,1)S(1)} %hold.1.after_ref.after2_ref.after3_ref), channel_id=1, source_target_pairs={{0,2},{1,3},{2,0},{3,1},{4,6},{5,7},{6,4},{7,5},{8,10},{9,11},{10,... | collective-permute-start | bytes 1179656 | tf_op jit(solution)/shard_map/ppermute | solution.py:295
  41.7 26.2 %collective-permute-start.13 = (bf16[384,512]{1,0:T(8,128)(2,1)S(1)}, bf16[384,512]{1,0:T(8,128)(2,1)S(1)}, u32[]{:S(2)}, u32[]{:S(2)}) collective-permute-start(bf16[384,512]{1,0:T(8,128)(2,1)S(1)} %sum_3.1.after_ref), channel_id=1, source_target_pairs={{0,2},{1,3},{2,0},{3,1},{4,6},{5,7},{6,4},{7,5},{8,10},{9,11},{10,... | collective-permute-start | bytes 1179656 | tf_op jit(solution)/shard_map/ppermute | solution.py:295
  41.8 11.6 %copy-start.10 = (bf16[128,64]{1,0:T(8,128)(2,1)S(1)}, bf16[128,64]{1,0:T(8,128)(2,1)}, u32[]{:S(2)}) copy-start(bf16[128,64]{1,0:T(8,128)(2,1)} %constant.29.clone.c2th_ref) | copy-start | bytes 49156
  41.9 11.6 %copy-start.11 = (bf16[128,64]{1,0:T(8,128)(2,1)S(1)}, bf16[128,64]{1,0:T(8,128)(2,1)}, u32[]{:S(2)}) copy-start(bf16[128,64]{1,0:T(8,128)(2,1)} %constant.30.clone.c2tl_ref) | copy-start | bytes 49156
  41.9 17.2 %collective-permute-start.10 = (bf16[256,512]{1,0:T(8,128)(2,1)S(1)}, bf16[256,512]{1,0:T(8,128)(2,1)S(1)}, u32[]{:S(2)}, u32[]{:S(2)}) collective-permute-start(bf16[256,512]{1,0:T(8,128)(2,1)S(1)} %cut.7), channel_id=1, source_target_pairs={{0,1},{1,0},{2,3},{3,2},{4,5},{5,4},{6,7},{7,6},{8,9},{9,8},{10,11... | collective-permute-start | bytes 786440 | tf_op jit(solution)/shard_map/ppermute | solution.py:295
  42.9 20.5 %copy-start.6 = (bf16[256,64]{1,0:T(8,128)(2,1)S(1)}, bf16[256,64]{1,0:T(8,128)(2,1)}, u32[]{:S(2)}) copy-start(bf16[256,64]{1,0:T(8,128)(2,1)} %constant.27.clone.c4th_ref) | copy-start | bytes 98308
  42.9 20.5 %copy-start.7 = (bf16[256,64]{1,0:T(8,128)(2,1)S(1)}, bf16[256,64]{1,0:T(8,128)(2,1)}, u32[]{:S(2)}) copy-start(bf16[256,64]{1,0:T(8,128)(2,1)} %constant.28.clone.c4tl_ref) | copy-start | bytes 98308
  42.9 20.5 %collective-permute-start.12 = (bf16[256,512]{1,0:T(8,128)(2,1)S(1)}, bf16[256,512]{1,0:T(8,128)(2,1)S(1)}, u32[]{:S(2)}, u32[]{:S(2)}) collective-permute-start(bf16[256,512]{1,0:T(8,128)(2,1)S(1)} %cut.9), channel_id=1, source_target_pairs={{0,1},{1,0},{2,3},{3,2},{4,5},{5,4},{6,7},{7,6},{8,9},{9,8},{10,11... | collective-permute-start | bytes 786440 | tf_op jit(solution)/shard_map/ppermute | solution.py:295
  (3 other events, 10.9 us)
